TPU v7x, 128 devices: a whole 4x4x4 slice. The times are simulated.
128 devices in a mesh: lon: 16 (over y_hi, z, core), lat: 8 (over x, y_lo).
Axes of the slice: x: 4, y: 4 (y_hi: 2, y_lo: 2; y = y_hi * 2 + y_lo), z: 4, core: 2. Of those that a mesh axis runs over, the one named last changes fastest.
Arguments:
- state: bfloat16 [192, 768, 512], P('lat', 'lon'), may hold values from -6 to 6
- attention_in: bfloat16 [2, 512, 1536], replicated, may hold values from -10 to 10
- attention_out: bfloat16 [2, 512, 512], replicated, may hold values from -0.25 to 0.25
- expand_weight: bfloat16 [2, 512, 2048], replicated, may hold values from -0.25 to 0.25
- depth_kernel: bfloat16 [2, 7, 7, 2048], replicated, may hold values from -0.875 to 0.875
- shrink_weight: bfloat16 [2, 2048, 512], replicated, may hold values from -0.125 to 0.125
- norm_attention: float32 [2, 512], replicated, may hold values from 0.1 to 1.9
- norm_feedforward: float32 [2, 512], replicated, may hold values from 0.1 to 1.9
Outputs:
- advanced_state: bfloat16 [192, 768, 512], P('lat', 'lon')
All inputs are finite; a program needn't handle non-finite values.
Results may differ from a plain program's by a relative error of at most 0.009.
Values may be sent and summed in bfloat16 or wider, within the bound.
No kernel may reach another device: no remote copies, remote signals or barrier semaphores. Data moves between devices by JAX's collectives and lax.ppermute only.
A program may use at most 128 MiB of HBM per device.

v0:
```python
import math

import jax
import jax.numpy as jnp
from jax import lax
from jax.sharding import PartitionSpec as P

HEADS = 8
HEAD_DIM = 64
RADIUS = 6
CONV_RADIUS = 3
LAYERS = 2


def with_halo(shard, sides, width, wrap):
    for axis, dim in sides:
        peers, length = (lax.axis_size(axis), shard.shape[dim])
        up = [(i, (i + 1) % peers) for i in range(peers if wrap else peers - 1)]
        down = [(j, i) for i, j in up]
        last = lax.slice_in_dim(shard, length - width, length, axis=dim)
        leading = lax.slice_in_dim(shard, 0, width, axis=dim)
        before = lax.ppermute(last, axis, up)
        after = lax.ppermute(leading, axis, down)
        shard = jnp.concatenate([before, shard, after], axis=dim)
    return shard


def normalize(stream, gain):
    average = jnp.mean(stream, axis=-1, keepdims=True)
    centred = stream - average
    spread = jnp.mean(centred * centred, axis=-1, keepdims=True)
    return (centred * lax.rsqrt(spread + 1e-05) * gain).astype(jnp.bfloat16)


def attend_tile(queries, pairs, band_index, grid_height):
    tile_height, tile_width, channels = queries.shape
    side = 8
    span = side + 2 * RADIUS
    blocks_lat = tile_height // side
    blocks_lon = tile_width // side
    scale = 1.0 / math.sqrt(HEAD_DIM)
    query_rows = jnp.arange(side, dtype=jnp.int32)
    key_rows = jnp.arange(span, dtype=jnp.int32)
    near_local = jnp.abs(key_rows[None, :] - RADIUS - query_rows[:, None]) <= RADIUS
    anchor = jnp.zeros((), jnp.int32)

    def one_block(index):
        block_lat = index // blocks_lon
        block_lon = index % blocks_lon
        row_start = block_lat * side
        col_start = block_lon * side
        query_block = lax.dynamic_slice(
            queries, (row_start, col_start, anchor), (side, side, channels)
        )
        query_block = query_block.reshape(side * side, HEADS, HEAD_DIM)
        window = lax.dynamic_slice(
            pairs, (row_start, col_start, anchor), (span, span, 2 * channels)
        )
        window = window.reshape(span * span, 2 * channels)
        key_block = window[:, :channels].reshape(span * span, HEADS, HEAD_DIM)
        value_block = window[:, channels:].reshape(span * span, HEADS, HEAD_DIM)
        global_rows = band_index * tile_height + row_start + key_rows - RADIUS
        inside = (global_rows >= 0) & (global_rows < grid_height)
        near_rows = near_local & inside[None, :]
        allowed = near_rows[:, None, :, None] & near_local[None, :, None, :]
        allowed = allowed.reshape(side * side, span * span)
        scores = (
            jnp.einsum("qhd,khd->hqk", query_block, key_block, preferred_element_type=jnp.float32)
            * scale
        )
        scores = jnp.where(allowed[None], scores, -jnp.inf)
        peak = jnp.max(scores, axis=-1, keepdims=True)
        expos = jnp.exp(scores - peak)
        weights = (expos / jnp.sum(expos, axis=-1, keepdims=True)).astype(jnp.bfloat16)
        mixed = jnp.einsum("hqk,khd->qhd", weights, value_block, preferred_element_type=jnp.float32)
        return mixed.astype(jnp.bfloat16).reshape(side * side, channels)

    outputs = lax.map(one_block, jnp.arange(blocks_lat * blocks_lon, dtype=jnp.int32))
    outputs = outputs.reshape(blocks_lat, blocks_lon, side, side, channels)
    outputs = jnp.transpose(outputs, (0, 2, 1, 3, 4))
    return outputs.reshape(tile_height * tile_width, channels)


def convolve_tile(wide, kernel, tile_height, tile_width):
    total = jnp.zeros((tile_height, tile_width, wide.shape[2]), jnp.float32)
    for down_shift in range(2 * CONV_RADIUS + 1):
        for east_shift in range(2 * CONV_RADIUS + 1):
            piece = wide[
                down_shift : down_shift + tile_height, east_shift : east_shift + tile_width
            ]
            total = total + piece.astype(jnp.float32) * kernel[down_shift, east_shift].astype(
                jnp.float32
            )
    return total


def per_device(
    state,
    attention_in,
    attention_out,
    expand_weight,
    depth_kernel,
    shrink_weight,
    norm_attention,
    norm_feedforward,
):
    tile_height, tile_width, channels = state.shape
    band_index = lax.axis_index("lat")
    grid_height = tile_height * lax.axis_size("lat")
    stream = state.astype(jnp.float32).reshape(tile_height * tile_width, channels)
    for layer in range(LAYERS):
        normed = normalize(stream, norm_attention[layer])
        weight_in = attention_in[layer]
        queries = jnp.dot(
            normed, weight_in[:, :channels], preferred_element_type=jnp.float32
        ).astype(jnp.bfloat16)
        pairs = jnp.dot(normed, weight_in[:, channels:], preferred_element_type=jnp.float32).astype(
            jnp.bfloat16
        )
        pairs = pairs.reshape(tile_height, tile_width, 2 * channels)
        pairs = with_halo(pairs, (("lat", 0),), RADIUS, False)
        pairs = with_halo(pairs, (("lon", 1),), RADIUS, True)
        mixed = attend_tile(
            queries.reshape(tile_height, tile_width, channels), pairs, band_index, grid_height
        )
        stream = stream + jnp.dot(mixed, attention_out[layer], preferred_element_type=jnp.float32)
        normed_ff = normalize(stream, norm_feedforward[layer])
        hidden = jnp.dot(
            normed_ff, expand_weight[layer], preferred_element_type=jnp.float32
        ).astype(jnp.bfloat16)
        hidden = hidden.reshape(tile_height, tile_width, -1)
        hidden = with_halo(hidden, (("lat", 0),), CONV_RADIUS, False)
        hidden = with_halo(hidden, (("lon", 1),), CONV_RADIUS, True)
        convolved = convolve_tile(hidden, depth_kernel[layer], tile_height, tile_width)
        activated = (
            jax.nn.gelu(convolved, approximate=False)
            .astype(jnp.bfloat16)
            .reshape(tile_height * tile_width, -1)
        )
        stream = stream + jnp.dot(
            activated, shrink_weight[layer], preferred_element_type=jnp.float32
        )
    return stream.astype(jnp.bfloat16).reshape(tile_height, tile_width, channels)


def solution(mesh):
    in_specs = (P("lat", "lon", None), P(), P(), P(), P(), P(), P(), P())
    out_specs = P("lat", "lon", None)
    return jax.shard_map(
        per_device, mesh=mesh, in_specs=in_specs, out_specs=out_specs, check_vma=False
    )
```

profile of v0, /device:TPU:0, one launch (start us, length us, event | category | flops | bytes accessed | tf_op | source)
XLA Modules:
  0.0 856.7 jit_solution(9118999632580343159)
XLA Ops:
  21.8 17.7 %collective-permute-done = bf16[6,48,1024]{2,1,0:T(8,128)(2,1)} collective-permute-done((bf16[6,48,1024]{2,1,0:T(8,128)(2,1)}, bf16[6,48,1024]{2,1,0:T(8,128)(2,1)}, u32[]{:S(2)}, u32[]{:S(2)}) %collective-permute-start) | collective-permute-done | bytes 589856 | tf_op jit(solution)/shard_map/ppermute | solution.py:22
  42.9 5.5 collective-permute-start.3
  49.5 5.3 collective-permute-done.2
  54.7 6.9 pad_maximum_fusion.2
  62.7 169.7 %while.28 = (s32[]{:T(128)}, bf16[18,64,512]{2,1,0:T(8,128)(2,1)}, s32[18]{0:T(128)S(1)}, bf16[36,60,1024]{2,0,1:T(8,128)(2,1)}, s32[]{:T(128)}, /*index=5*/bf16...) while((s32[]{:T(128)}, bf16[18,64,512]{2,1,0:T(8,128)(2,1)}, ...), condition=%wide.region_5.6_spmd.clone.clone, body=%wide.region_2.5_spmd.clone.clone.sunk | while | flops 80546848 | bytes 11913930 | solution.py:78
  239.8 4.4 collective-permute-start.4
  247.0 21.3 %collective-permute-done.4 = bf16[3,48,2048]{2,1,0:T(8,128)(2,1)S(1)} collective-permute-done((bf16[3,48,2048]{2,1,0:T(8,128)(2,1)S(1)}, bf16[3,48,2048]{2,1,0:T(8,128)(2,1)S(1)}, u32[]{:S(2)}, u32[]{:S(2)}) %collective-permute-start.4) | collective-permute-done | bytes 589856 | tf_op jit(solution)/shard_map/ppermute | solution.py:22
  268.9 5.5 collective-permute-start.7
  275.2 5.6 collective-permute-done.6
  280.8 6.7 maximum_maximum_fusion
  287.5 147.2 %fusion.32 = bf16[24,48,2048]{2,1,0:T(8,128)(2,1)} fusion(bf16[24,48,2048]{2,1,0:T(8,128)(2,1)} %bitcast.247, bf16[3,48,2048]{2,1,0:T(8,128)(2,1)S(1)} %collective-permute-done.5, bf16[3,48,2048]{2,1,0:T(8,128)(2,1)S(1)} %collective-permute-done.4, bf16[30,51,2048]{2,1,0:T(8,128)(2,1)} %get-tuple-element.372, bf16[30,51,2048]{2,1,0:T(8,128)(2,1)} %get-tuple-element.371, ...), kind=kLoop, calls=%fused_computation.48 | loop fusion | flops 511967232 | bytes 209199104 | tf_op jit(solution)/shard_map/convert_element_type | solution.py:137
  434.7 5.9 fusion.100
  442.7 4.4 collective-permute-start.8
  450.2 18.7 %collective-permute-done.8 = bf16[6,48,1024]{2,1,0:T(8,128)(2,1)S(1)} collective-permute-done((bf16[6,48,1024]{2,1,0:T(8,128)(2,1)S(1)}, bf16[6,48,1024]{2,1,0:T(8,128)(2,1)S(1)}, u32[]{:S(2)}, u32[]{:S(2)}) %collective-permute-start.8) | collective-permute-done | bytes 589856 | tf_op jit(solution)/shard_map/ppermute | solution.py:22
  471.8 5.4 collective-permute-start.11
  483.9 7.8 pad_maximum_fusion.3
  491.9 158.9 %while.29 = (s32[]{:T(128)}, bf16[18,64,512]{2,1,0:T(8,128)(2,1)S(1)}, s32[18]{0:T(128)S(1)}, bf16[36,60,1024]{2,0,1:T(8,128)(2,1)}, s32[]{:T(128)}, /*index=5*/...) while((s32[]{:T(128)}, ...), condition=%wide.region_13.14_spmd.clone.clone, body=%wide.region_10.13_spmd.clone.clone.sunk | while | flops 80546848 | bytes 11913422 | solution.py:78
  657.6 4.6 collective-permute-start.12
  665.1 18.3 %collective-permute-done.12 = bf16[3,48,2048]{2,1,0:T(8,128)(2,1)S(1)} collective-permute-done((bf16[3,48,2048]{2,1,0:T(8,128)(2,1)S(1)}, bf16[3,48,2048]{2,1,0:T(8,128)(2,1)S(1)}, u32[]{:S(2)}, u32[]{:S(2)}) %collective-permute-start.12) | collective-permute-done | bytes 589856 | tf_op jit(solution)/shard_map/ppermute | solution.py:22
  684.0 5.3 collective-permute-start.15
  690.1 5.8 collective-permute-done.14
  695.9 6.7 maximum_maximum_fusion.1
  702.6 147.3 %fusion.35 = bf16[24,48,2048]{2,1,0:T(8,128)(2,1)} fusion(bf16[24,48,2048]{2,1,0:T(8,128)(2,1)} %bitcast.244, bf16[3,48,2048]{2,1,0:T(8,128)(2,1)S(1)} %collective-permute-done.13, bf16[3,48,2048]{2,1,0:T(8,128)(2,1)S(1)} %collective-permute-done.12, bf16[30,51,2048]{2,1,0:T(8,128)(2,1)} %get-tuple-element.368, bf16[30,51,2048]{2,1,0:T(8,128)(2,1)} %get-tuple-element.367, ...), kind=kLoop, calls=%fused_computation.51 | loop fusion | flops 511967232 | bytes 209199104 | tf_op jit(solution)/shard_map/convert_element_type | solution.py:137
  849.9 6.7 fusion.58
  (746 shorter events, 319.7 us)
Async XLA Ops:
  0.0 7.5 copy-start.2
  9.4 9.9 %copy-start.8 = (f32[2,512]{1,0:T(2,128)S(1)}, f32[2,512]{1,0:T(2,128)}, u32[]{:S(2)}) copy-start(f32[2,512]{1,0:T(2,128)} %param.19) | copy-start | bytes 12292
  10.5 29.1 %collective-permute-start = (bf16[6,48,1024]{2,1,0:T(8,128)(2,1)}, bf16[6,48,1024]{2,1,0:T(8,128)(2,1)}, u32[]{:S(2)}, u32[]{:S(2)}) collective-permute-start(bf16[6,48,1024]{2,1,0:T(8,128)(2,1)} %bitcast.3), channel_id=1, source_target_pairs={{0,1},{1,2},{2,3},{3,4},{4,5},{5,6},{6,7},{8,9},{9,10},{10,11},{11... | collective-permute-start | bytes 1769480 | tf_op jit(solution)/shard_map/ppermute | solution.py:22
  14.9 26.1 %collective-permute-start.1 = (bf16[6,48,1024]{2,1,0:T(8,128)(2,1)}, bf16[6,48,1024]{2,1,0:T(8,128)(2,1)}, u32[]{:S(2)}, u32[]{:S(2)}) collective-permute-start(bf16[6,48,1024]{2,1,0:T(8,128)(2,1)} %bitcast.5), channel_id=1, source_target_pairs={{1,0},{2,1},{3,2},{4,3},{5,4},{6,5},{7,6},{9,8},{10,9},{11,10},{12... | collective-permute-start | bytes 1769480 | tf_op jit(solution)/shard_map/ppermute | solution.py:23
  42.8 11.9 %collective-permute-start.2 = (bf16[36,6,1024]{2,0,1:T(8,128)(2,1)S(1)}, bf16[36,6,1024]{2,0,1:T(8,128)(2,1)S(1)}, u32[]{:S(2)}, u32[]{:S(2)}) collective-permute-start(bf16[36,6,1024]{2,0,1:T(8,128)(2,1)S(1)} %get-tuple-element.381), channel_id=1, source_target_pairs={{0,8},{8,16},{16,24},{24,32},{32,40},{40,48},{48,56},{56,64},{64,7... | collective-permute-start | bytes 1327112 | tf_op jit(solution)/shard_map/ppermute | solution.py:22
  42.9 11.9 %collective-permute-start.3 = (bf16[36,6,1024]{2,0,1:T(8,128)(2,1)S(1)}, bf16[36,6,1024]{2,0,1:T(8,128)(2,1)S(1)}, u32[]{:S(2)}, u32[]{:S(2)}) collective-permute-start(bf16[36,6,1024]{2,0,1:T(8,128)(2,1)S(1)} %get-tuple-element.382), channel_id=1, source_target_pairs={{8,0},{16,8},{24,16},{32,24},{40,32},{48,40},{56,48},{64,56},{72,6... | collective-permute-start | bytes 1327112 | tf_op jit(solution)/shard_map/ppermute | solution.py:23
  236.5 9.0 %copy-start.6 = (bf16[7,7,2048]{2,1,0:T(8,128)(2,1)S(1)}, bf16[7,7,2048]{2,1,0:T(8,128)(2,1)}, u32[]{:S(2)}) copy-start(bf16[7,7,2048]{2,1,0:T(8,128)(2,1)} %get-tuple-element.500) | copy-start | bytes 602116
  239.7 47.8 %copy-start.1 = (bf16[1152,2048]{1,0:T(8,128)(2,1)}, bf16[1152,2048]{1,0:T(8,128)(2,1)S(1)}, u32[]{:S(2)}) copy-start(bf16[1152,2048]{1,0:T(8,128)(2,1)S(1)} %convolution_convert_fusion.3) | copy-start | bytes 14155780
  239.8 28.5 %collective-permute-start.4 = (bf16[3,48,2048]{2,1,0:T(8,128)(2,1)S(1)}, bf16[3,48,2048]{2,1,0:T(8,128)(2,1)S(1)}, u32[]{:S(2)}, u32[]{:S(2)}) collective-permute-start(bf16[3,48,2048]{2,1,0:T(8,128)(2,1)S(1)} %bitcast.264), channel_id=1, source_target_pairs={{0,1},{1,2},{2,3},{3,4},{4,5},{5,6},{6,7},{8,9},{9,10},{10,11},{11... | collective-permute-start | bytes 1769480 | tf_op jit(solution)/shard_map/ppermute | solution.py:22
  244.2 24.1 %collective-permute-start.5 = (bf16[3,48,2048]{2,1,0:T(8,128)(2,1)S(1)}, bf16[3,48,2048]{2,1,0:T(8,128)(2,1)S(1)}, u32[]{:S(2)}, u32[]{:S(2)}) collective-permute-start(bf16[3,48,2048]{2,1,0:T(8,128)(2,1)S(1)} %bitcast.262), channel_id=1, source_target_pairs={{1,0},{2,1},{3,2},{4,3},{5,4},{6,5},{7,6},{9,8},{10,9},{11,10},{12... | collective-permute-start | bytes 1769480 | tf_op jit(solution)/shard_map/ppermute | solution.py:23
  268.9 11.9 %collective-permute-start.6 = (bf16[30,3,2048]{2,1,0:T(4,128)(2,1)S(1)}, bf16[30,3,2048]{2,1,0:T(4,128)(2,1)S(1)}, u32[]{:S(2)}, u32[]{:S(2)}) collective-permute-start(bf16[30,3,2048]{2,1,0:T(4,128)(2,1)S(1)} %get-tuple-element.373), channel_id=1, source_target_pairs={{0,8},{8,16},{16,24},{24,32},{32,40},{40,48},{48,56},{56,64},{64,7... | collective-permute-start | bytes 1105928 | tf_op jit(solution)/shard_map/ppermute | solution.py:22
  268.9 11.9 %collective-permute-start.7 = (bf16[30,3,2048]{2,1,0:T(4,128)(2,1)S(1)}, bf16[30,3,2048]{2,1,0:T(4,128)(2,1)S(1)}, u32[]{:S(2)}, u32[]{:S(2)}) collective-permute-start(bf16[30,3,2048]{2,1,0:T(4,128)(2,1)S(1)} %get-tuple-element.374), channel_id=1, source_target_pairs={{8,0},{16,8},{24,16},{32,24},{40,32},{48,40},{56,48},{64,56},{72,6... | collective-permute-start | bytes 1105928 | tf_op jit(solution)/shard_map/ppermute | solution.py:23
  434.7 6.4 copy-start.7
  440.6 9.5 %copy-start.3 = (f32[1152,512]{1,0:T(8,128)}, f32[1152,512]{1,0:T(8,128)S(1)}, u32[]{:S(2)}) copy-start(f32[1152,512]{1,0:T(8,128)S(1)} %get-tuple-element.496) | copy-start | bytes 7077892
  442.7 26.1 %collective-permute-start.8 = (bf16[6,48,1024]{2,1,0:T(8,128)(2,1)S(1)}, bf16[6,48,1024]{2,1,0:T(8,128)(2,1)S(1)}, u32[]{:S(2)}, u32[]{:S(2)}) collective-permute-start(bf16[6,48,1024]{2,1,0:T(8,128)(2,1)S(1)} %bitcast.266), channel_id=1, source_target_pairs={{0,1},{1,2},{2,3},{3,4},{4,5},{5,6},{6,7},{8,9},{9,10},{10,11},{11... | collective-permute-start | bytes 1769480 | tf_op jit(solution)/shard_map/ppermute | solution.py:22
  447.2 22.0 %collective-permute-start.9 = (bf16[6,48,1024]{2,1,0:T(8,128)(2,1)S(1)}, bf16[6,48,1024]{2,1,0:T(8,128)(2,1)S(1)}, u32[]{:S(2)}, u32[]{:S(2)}) collective-permute-start(bf16[6,48,1024]{2,1,0:T(8,128)(2,1)S(1)} %bitcast.265), channel_id=1, source_target_pairs={{1,0},{2,1},{3,2},{4,3},{5,4},{6,5},{7,6},{9,8},{10,9},{11,10},{12... | collective-permute-start | bytes 1769480 | tf_op jit(solution)/shard_map/ppermute | solution.py:23
  471.8 12.2 %collective-permute-start.10 = (bf16[36,6,1024]{2,0,1:T(8,128)(2,1)}, bf16[36,6,1024]{2,0,1:T(8,128)(2,1)}, u32[]{:S(2)}, u32[]{:S(2)}) collective-permute-start(bf16[36,6,1024]{2,0,1:T(8,128)(2,1)} %get-tuple-element.379), channel_id=1, source_target_pairs={{0,8},{8,16},{16,24},{24,32},{32,40},{40,48},{48,56},{56,64},{64,7... | collective-permute-start | bytes 1327112 | tf_op jit(solution)/shard_map/ppermute | solution.py:22
  471.8 12.2 %collective-permute-start.11 = (bf16[36,6,1024]{2,0,1:T(8,128)(2,1)}, bf16[36,6,1024]{2,0,1:T(8,128)(2,1)}, u32[]{:S(2)}, u32[]{:S(2)}) collective-permute-start(bf16[36,6,1024]{2,0,1:T(8,128)(2,1)} %get-tuple-element.380), channel_id=1, source_target_pairs={{8,0},{16,8},{24,16},{32,24},{40,32},{48,40},{56,48},{64,56},{72,6... | collective-permute-start | bytes 1327112 | tf_op jit(solution)/shard_map/ppermute | solution.py:23
  654.3 9.2 %copy-start.5 = (bf16[7,7,2048]{2,1,0:T(8,128)(2,1)S(1)}, bf16[7,7,2048]{2,1,0:T(8,128)(2,1)}, u32[]{:S(2)}) copy-start(bf16[7,7,2048]{2,1,0:T(8,128)(2,1)} %get-tuple-element.499) | copy-start | bytes 602116
  657.5 45.1 %copy-start = (bf16[1152,2048]{1,0:T(8,128)(2,1)}, bf16[1152,2048]{1,0:T(8,128)(2,1)S(1)}, u32[]{:S(2)}) copy-start(bf16[1152,2048]{1,0:T(8,128)(2,1)S(1)} %convolution_convert_fusion.2) | copy-start | bytes 14155780
  657.6 25.8 %collective-permute-start.12 = (bf16[3,48,2048]{2,1,0:T(8,128)(2,1)S(1)}, bf16[3,48,2048]{2,1,0:T(8,128)(2,1)S(1)}, u32[]{:S(2)}, u32[]{:S(2)}) collective-permute-start(bf16[3,48,2048]{2,1,0:T(8,128)(2,1)S(1)} %bitcast.263), channel_id=1, source_target_pairs={{0,1},{1,2},{2,3},{3,4},{4,5},{5,6},{6,7},{8,9},{9,10},{10,11},{11... | collective-permute-start | bytes 1769480 | tf_op jit(solution)/shard_map/ppermute | solution.py:22
  662.2 21.2 %collective-permute-start.13 = (bf16[3,48,2048]{2,1,0:T(8,128)(2,1)S(1)}, bf16[3,48,2048]{2,1,0:T(8,128)(2,1)S(1)}, u32[]{:S(2)}, u32[]{:S(2)}) collective-permute-start(bf16[3,48,2048]{2,1,0:T(8,128)(2,1)S(1)} %bitcast.261), channel_id=1, source_target_pairs={{1,0},{2,1},{3,2},{4,3},{5,4},{6,5},{7,6},{9,8},{10,9},{11,10},{12... | collective-permute-start | bytes 1769480 | tf_op jit(solution)/shard_map/ppermute | solution.py:23
  684.0 11.9 %collective-permute-start.14 = (bf16[30,3,2048]{2,1,0:T(4,128)(2,1)S(1)}, bf16[30,3,2048]{2,1,0:T(4,128)(2,1)S(1)}, u32[]{:S(2)}, u32[]{:S(2)}) collective-permute-start(bf16[30,3,2048]{2,1,0:T(4,128)(2,1)S(1)} %get-tuple-element.369), channel_id=1, source_target_pairs={{0,8},{8,16},{16,24},{24,32},{32,40},{40,48},{48,56},{56,64},{64,7... | collective-permute-start | bytes 1105928 | tf_op jit(solution)/shard_map/ppermute | solution.py:22
  684.0 11.9 %collective-permute-start.15 = (bf16[30,3,2048]{2,1,0:T(4,128)(2,1)S(1)}, bf16[30,3,2048]{2,1,0:T(4,128)(2,1)S(1)}, u32[]{:S(2)}, u32[]{:S(2)}) collective-permute-start(bf16[30,3,2048]{2,1,0:T(4,128)(2,1)S(1)} %get-tuple-element.370), channel_id=1, source_target_pairs={{8,0},{16,8},{24,16},{32,24},{40,32},{48,40},{56,48},{64,56},{72,6... | collective-permute-start | bytes 1105928 | tf_op jit(solution)/shard_map/ppermute | solution.py:23
  (4 other events, 11.9 us)
where the time goes:
time: 873 us; the launch traced here: 857 us
  other arithmetic  341 us (39%)
  local copies, waits for them, and re-layouts  205 us (23%)
  waiting for transfers between devices  96 us (11%)
  matrix products  95.3 us (11%)
  loops' own time  73.4 us (8%)
  starting transfers between devices  45.3 us (5%)
    convert_element_type x2, other arithmetic, per_device(): activated = jax.nn.gelu(convolved, approximate=False).astype(jnp.bfloat16...  294 us
    ppermute x8, waiting for transfers between devices, with_halo(): before = lax.ppermute(last, axis, up)  95.9 us
    dynamic_slice x72, local copies, waits for them, and re-layouts, one_block(): lax.dynamic_slice(pairs, (row_start, col_start, anchor), (span, span, 2 *...  78.4 us
    another operation x2, loops' own time, attend_tile(): lax.map(one_block, jnp.arange(blocks_lat * blocks_lon, dtype=jnp.int32))  73.4 us
    dot_general x36, matrix products, one_block(): jnp.einsum('hqk,khd->qhd', weights, value_block, preferred_element_type=j...  35.4 us
    dynamic_slice x36, local copies, waits for them, and re-layouts, one_block(): lax.dynamic_slice(queries, (row_start, col_start, anchor), (side, side, c...  30.6 us
    concatenate x4, other arithmetic, with_halo(): shard = jnp.concatenate([before, shard, after], axis=dim)  28.1 us
    ppermute x8, starting transfers between devices, with_halo(): after = lax.ppermute(leading, axis, down)  27.3 us
  transfers between devices with their start and end apart: 16, of which 8 were waited for; matrix products, arithmetic and copies ran while one was open for 2% of the time, Pallas kernels for 0%

commit v1 on v0

v1 whole, which is shorter than its diff:
```python
import functools
import math

import jax
import jax.numpy as jnp
import numpy as np
from jax import lax
from jax.experimental import pallas as pl
from jax.experimental.pallas import tpu as pltpu
from jax.sharding import PartitionSpec as P

BF, F32 = jnp.bfloat16, jnp.float32
D, FF = 512, 2048
RADIUS = 6
REACH = 3
LAYERS = 2
H, W = 24, 48
PH, PW = 12, 8
LH, LW = PH + 2 * REACH, PW + 2 * REACH
SLAB = 24
HALF = LH * LW // 2 + 2
CHUNK = 1024
VMEM = 56 * 2**20


def transforms():
    seen, reps = set(), []
    for a in range(LH):
        for b in range(LW):
            mirror = ((-a) % LH, (-b) % LW)
            if mirror not in seen:
                seen.add((a, b))
                reps.append((a / LH, b / LW, (1.0 if mirror == (a, b) else 2.0) / (LH * LW)))
    fa, fb, weight = np.array(reps).T[:, :, None, None]
    angle = 2 * np.pi * (fa * np.arange(LH)[:, None] + fb * np.arange(LW))
    cos, sin = np.cos(angle), np.sin(angle)
    sin[np.abs(sin) < 1e-9] = 0
    forward = np.zeros((2 * HALF, LH, SLAB))
    first = 8 - REACH
    forward[:HALF, :, first : first + LW] = cos
    forward[HALF:, :, first : first + LW] = -sin
    inverse = np.concatenate(
        [cos[:, :PH, :PW].reshape(HALF, -1).T, -sin[:, :PH, :PW].reshape(HALF, -1).T], 1
    )
    taps = np.concatenate([(cos * weight)[:, :7, :7], (sin * weight)[:, :7, :7]], 0)
    return forward.reshape(2 * HALF, -1), inverse, taps.reshape(2 * HALF, -1)


def norm(x, gain):
    c = x - jnp.mean(x, axis=-1, keepdims=True)
    return c * lax.rsqrt(jnp.mean(c * c, axis=-1, keepdims=True) + 1e-5) * gain


def gelu(x):
    return 0.5 * x * (1.0 + lax.erf(x * np.float32(1 / math.sqrt(2))))


def place_halo(wide, pieces, r):
    n, s, w, e, nw, ne, sw, se = pieces
    wide[:, 0:8, :] = jnp.zeros((H + 2 * r, 8, D), F32)
    wide[:, 8 + W :, :] = jnp.zeros((H + 2 * r, 8, D), F32)
    for rows, left, middle, right in (
        (slice(0, r), nw, n, ne),
        (slice(r, r + H), w, None, e),
        (slice(r + H, r + H + r), sw, s, se),
    ):
        wide[rows, 8 - r : 8, :] = left[...].astype(F32)
        wide[rows, 8 + W : 8 + W + r, :] = right[...].astype(F32)
        if middle is not None:
            wide[rows, 8 : 8 + W, :] = middle[...].astype(F32)


def attend_kernel(grid_height, band_ref, stream_ref, *refs):
    pieces, refs = refs[:8], refs[8:]
    (win_ref, wout_ref, ga_ref, gf_ref, out_ref, nff_ref, on_ref, os_ref, ow_ref, oe_ref) = refs[:10]
    wide, kv, q, mixed, mask = refs[10:]
    step = pl.program_id(0)
    i, j = step // 3, step % 3

    @pl.when(step == 0)
    def _():
        place_halo(wide, pieces, RADIUS)

        def own(r, c):
            y = norm(stream_ref[pl.ds(r * 6, 6)].reshape(6 * W, D), ga_ref[...])
            wide[pl.ds(r * 6 + RADIUS, 6), 8 : 8 + W, :] = y.reshape(6, W, D)
            got = jnp.dot(y.astype(BF), win_ref[:, :D], preferred_element_type=F32)
            q[pl.ds(r * 6, 6)] = (got * 0.125).astype(BF).reshape(6, W, D)
            return c

        lax.fori_loop(0, 4, own, 0)

        def pairs(r, c):
            x = wide[pl.ds(r * 6, 6)].reshape(6 * 64, D).astype(BF)
            got = jnp.dot(x, win_ref[:, D:], preferred_element_type=F32)
            kv[pl.ds(r * 6, 6)] = got.astype(BF).reshape(6, 64, 2 * D)
            return c

        lax.fori_loop(0, 6, pairs, 0)

    @pl.when(j == 0)
    def _():
        row = lax.broadcasted_iota(jnp.int32, (64, 512), 0)
        col = lax.broadcasted_iota(jnp.int32, (64, 512), 1)
        a, b, u, v = row >> 4, row & 15, col >> 5, col & 31
        lat = band_ref[0] * H + i * 4 - RADIUS + u
        ok = (u >= a) & (u <= a + 12) & (v >= b + 2) & (v <= b + 14) & (lat >= 0) & (lat < grid_height)
        mask[...] = jnp.where(ok, 0.0, -jnp.inf)

    j16 = pl.multiple_of(j * 16, 16)
    keys = kv[pl.ds(i * 4, 16), pl.ds(j16, 32), :].reshape(512, 2 * D)
    qb = q[pl.ds(i * 4, 4), pl.ds(j16, 16), :].reshape(64, D)
    head = lax.broadcasted_iota(jnp.int32, (64, 256), 1) >> 6
    outs = []
    for g in range(2):
        k, v = keys[:, g * 256 : (g + 1) * 256], keys[:, D + g * 256 : D + (g + 1) * 256]
        qg = qb[:, g * 256 : (g + 1) * 256]
        qbd = jnp.concatenate([jnp.where(head == h, qg, jnp.zeros_like(qg)) for h in range(4)], 0)
        s = lax.dot_general(qbd, k, (((1,), (1,)), ((), ())), preferred_element_type=F32)
        s = (s.reshape(4, 64, 512) + mask[...][None]).reshape(256, 512)
        p = jnp.exp(s - jnp.max(s, axis=1, keepdims=True))
        total = jnp.sum(p, axis=1, keepdims=True)
        o = jnp.dot(p.astype(BF), v, preferred_element_type=F32) * (1.0 / total)
        r = o[192:]
        for h in range(3):
            r = jnp.where(head == h, o[h * 64 : (h + 1) * 64], r)
        outs.append(r.astype(BF))
    mixed[pl.ds(i * 4, 4), pl.ds(j16, 16), :] = jnp.concatenate(outs, 1).reshape(4, 16, D)

    @pl.when(step == 17)
    def _():
        def finish(r, c):
            x = mixed[pl.ds(r * 6, 6)].reshape(6 * W, D)
            x = jnp.dot(x, wout_ref[...], preferred_element_type=F32)
            x = x + stream_ref[pl.ds(r * 6, 6)].reshape(6 * W, D)
            out_ref[pl.ds(r * 6, 6)] = x.reshape(6, W, D)
            y = norm(x, gf_ref[...]).reshape(6, W, D).astype(BF)
            nff_ref[pl.ds(r * 6, 6)] = y
            ow_ref[pl.ds(r * 6, 6)] = y[:, :REACH]
            oe_ref[pl.ds(r * 6, 6)] = y[:, W - REACH :]

            @pl.when(r == 0)
            def _():
                on_ref[...] = y[:REACH]

            @pl.when(r == 3)
            def _():
                os_ref[...] = y[6 - REACH :]

            return c

        lax.fori_loop(0, 4, finish, 0)


def whole(a):
    return pl.BlockSpec(a.shape, lambda p: (0,) * len(a.shape))


def edge_shapes(r):
    rows, cols = jax.ShapeDtypeStruct((r, W, D), BF), jax.ShapeDtypeStruct((H, r, D), BF)
    return (rows, rows, cols, cols)


def attend(grid_height, band, stream, pieces, *rest):
    outs = (jax.ShapeDtypeStruct((H, W, D), F32), jax.ShapeDtypeStruct((H, W, D), BF)) + edge_shapes(REACH)
    args = (stream, *pieces, *rest)
    return pl.pallas_call(
        functools.partial(attend_kernel, grid_height),
        grid=(18,),
        in_specs=[pl.BlockSpec(memory_space=pltpu.SMEM)] + [whole(x) for x in args],
        out_specs=[whole(o) for o in outs],
        out_shape=outs,
        scratch_shapes=[
            pltpu.VMEM((H + 2 * RADIUS, 64, D), F32),
            pltpu.VMEM((H + 2 * RADIUS, 64, 2 * D), BF),
            pltpu.VMEM((H, W, D), BF),
            pltpu.VMEM((H, W, D), BF),
            pltpu.VMEM((64, 512), F32),
        ],
        compiler_params=pltpu.CompilerParams(vmem_limit_bytes=VMEM),
        name="attend",
    )(band, *args)


def feed_kernel(last, own_ref, stream_ref, *refs):
    pieces, refs = refs[:8], refs[8:]
    forward_ref, inverse_ref, kernel_ref, expand_ref, shrink_ref, gain_ref = refs[:6]
    outs, (wide, result) = refs[6:-2], refs[-2:]
    step = pl.program_id(0)

    @pl.when(step == 0)
    def _():
        place_halo(wide, pieces, REACH)
        wide[REACH : REACH + H, 8 : 8 + W, :] = own_ref[...].astype(F32)

    j8 = pl.multiple_of(step * PW, 8)
    ts = []
    for i in range(H // PH):
        x = wide[i * PH : i * PH + LH, pl.ds(j8, SLAB), :].reshape(LH * SLAB, D).astype(BF)
        ts.append(jnp.dot(forward_ref[...], x, preferred_element_type=F32).astype(BF))
    t = jnp.concatenate(ts, 0)
    acc = stream_ref[:, pl.ds(j8, PW), :].reshape(H * PW, D)
    for n in range(FF // CHUNK):
        c = slice(n * CHUNK, (n + 1) * CHUNK)
        z = jnp.dot(t, expand_ref[:, c], preferred_element_type=F32)
        kr, ki = kernel_ref[:HALF, c], kernel_ref[HALF:, c]
        acts = []
        for i in range(H // PH):
            re, im = z[2 * i * HALF : (2 * i + 1) * HALF], z[(2 * i + 1) * HALF : 2 * (i + 1) * HALF]
            y = jnp.concatenate([(re * kr - im * ki).astype(BF), (re * ki + im * kr).astype(BF)], 0)
            conv = jnp.dot(inverse_ref[...], y, preferred_element_type=F32)
            acts.append(gelu(conv).astype(BF))
        acc = acc + jnp.dot(jnp.concatenate(acts, 0), shrink_ref[c, :], preferred_element_type=F32)
    result[:, pl.ds(j8, PW), :] = acc.reshape(H, PW, D)

    @pl.when(step == W // PW - 1)
    def _():
        if last:
            outs[0][...] = result[...].astype(BF)
            return
        out_ref, on_ref, os_ref, ow_ref, oe_ref = outs
        out_ref[...] = result[...]
        for r in range(H // 6):
            y = norm(result[r * 6 : r * 6 + 6].reshape(6 * W, D), gain_ref[...]).astype(BF).reshape(6, W, D)
            if r == 0:
                on_ref[...] = y
            if r == H // 6 - 1:
                os_ref[...] = y
            ow_ref[r * 6 : r * 6 + 6] = y[:, :RADIUS]
            oe_ref[r * 6 : r * 6 + 6] = y[:, W - RADIUS :]


def feed(last, own, stream, pieces, *rest):
    if last:
        outs = (jax.ShapeDtypeStruct((H, W, D), BF),)
    else:
        outs = (jax.ShapeDtypeStruct((H, W, D), F32),) + edge_shapes(RADIUS)
    args = (own, stream, *pieces, *rest)
    return pl.pallas_call(
        functools.partial(feed_kernel, last),
        grid=(W // PW,),
        in_specs=[whole(x) for x in args],
        out_specs=[whole(o) for o in outs],
        out_shape=outs,
        scratch_shapes=[pltpu.VMEM((H + 2 * REACH, 64, D), F32), pltpu.VMEM((H, W, D), F32)],
        compiler_params=pltpu.CompilerParams(vmem_limit_bytes=VMEM),
        name="feed",
    )(*args)


def per_device(
    sizes,
    state,
    attention_in,
    attention_out,
    expand_weight,
    depth_kernel,
    shrink_weight,
    norm_attention,
    norm_feedforward,
):
    axes, nlat, nlon = sizes

    def pairs(dlat, dlon):
        def index(a, b):
            return a * nlon + b if axes[0] == "lat" else b * nlat + a

        return [
            (index(a, b), index(a + dlat, (b + dlon) % nlon))
            for a in range(nlat)
            for b in range(nlon)
            if 0 <= a + dlat < nlat
        ]

    def exchange(edges, r):
        n, s, w, e = edges

        def move(x, dlat, dlon):
            return lax.ppermute(x, axes, pairs(dlat, dlon))

        return (
            move(s, 1, 0),
            move(n, -1, 0),
            move(e, 0, 1),
            move(w, 0, -1),
            move(s[:, W - r :], 1, 1),
            move(s[:, :r], 1, -1),
            move(n[:, W - r :], -1, 1),
            move(n[:, :r], -1, -1),
        )

    forward, inverse, taps = transforms()
    forward, inverse = jnp.asarray(forward, BF), jnp.asarray(inverse, BF)
    kernels = jnp.einsum(
        "ft,ltc->lfc",
        jnp.asarray(taps, F32),
        depth_kernel.reshape(LAYERS, -1, FF).astype(F32),
        precision=lax.Precision.HIGHEST,
    )
    band = lax.axis_index("lat").astype(jnp.int32).reshape(1)
    stream = state.astype(F32)

    def normed(x):
        return norm(x.astype(F32), norm_attention[0]).astype(BF)

    edges = (
        normed(state[:RADIUS]),
        normed(state[H - RADIUS :]),
        normed(state[:, :RADIUS]),
        normed(state[:, W - RADIUS :]),
    )
    for layer in range(LAYERS):
        last = layer == LAYERS - 1
        ga, gf = norm_attention[layer][None], norm_feedforward[layer][None]
        stream, own, *edges = attend(
            nlat * H, band, stream, exchange(edges, RADIUS), attention_in[layer], attention_out[layer], ga, gf
        )
        stream, *edges = feed(
            last,
            own,
            stream,
            exchange(edges, REACH),
            forward,
            inverse,
            kernels[layer],
            expand_weight[layer],
            shrink_weight[layer],
            norm_attention[min(layer + 1, LAYERS - 1)][None],
        )
    return stream


def solution(mesh):
    in_specs = (P("lat", "lon", None), P(), P(), P(), P(), P(), P(), P())
    sizes = (tuple(mesh.axis_names), mesh.shape["lat"], mesh.shape["lon"])
    return jax.shard_map(
        functools.partial(per_device, sizes),
        mesh=mesh,
        in_specs=in_specs,
        out_specs=P("lat", "lon", None),
        check_vma=False,
    )
```

time: 873 us -> 258 us (0.30); the launches traced: 857 us -> 256 us
  other arithmetic: 341 us -> 6.48 us
  local copies, waits for them, and re-layouts: 205 us -> 20.4 us
  Pallas kernels: 0 us -> 103 us
  matrix products: 95.3 us -> 1.84 us
  loops' own time: 73.4 us -> 0 us
  waiting for transfers between devices: 96 us -> 27.4 us
  starting transfers between devices: 45.3 us -> 96.5 us
    convert_element_type x3, other arithmetic: 295 us -> 3.43 us  [the longest x1 1.75 us: per_device(): stream = state.astype(F32)]
    dynamic_slice x144 -> x0, local copies, waits for them, and re-layouts: 132 us -> none  [the longest x72 78.4 us: one_block(): lax.dynamic_slice(pairs, (row_start, col_start, anchor), (span, span, 2 *...]
    pallas_call x0 -> x4, Pallas kernels: none -> 103 us  [the longest x2 54.7 us: attend(): pl.pallas_call(functools.partial(attend_kernel, grid_height), grid=(18,),...]
    dot_general x82 -> x1, matrix products: 77.7 us -> 1.84 us  [per_device(): jnp.einsum('ft,ltc->lfc', jnp.asarray(taps, F32), depth_kernel.reshape(LA...]
    another operation x2 -> x0, loops' own time: 73.4 us -> none  [attend_tile(): lax.map(one_block, jnp.arange(blocks_lat * blocks_lon, dtype=jnp.int32))]
    ppermute x16 -> x32, waiting for transfers between devices: 96 us -> 27.4 us  [move(): return lax.ppermute(x, axes, pairs(dlat, dlon))]
    ppermute x16 -> x32, starting transfers between devices: 45.3 us -> 96.5 us  [move(): return lax.ppermute(x, axes, pairs(dlat, dlon))]
    concatenate x4 -> x0, other arithmetic: 28.1 us -> none  [with_halo(): shard = jnp.concatenate([before, shard, after], axis=dim)]
  transfers between devices with their start and end apart: 16 -> 32, of which waited for: 8 -> 5; matrix products, arithmetic and copies ran while one was open for 2% -> 7% of each run, Pallas kernels for 0% -> 0%
where the time goes in v1:
time: 258 us; the launch traced here: 256 us
  Pallas kernels  103 us (40%)
  starting transfers between devices  96.5 us (37%)
  waiting for transfers between devices  27.4 us (11%)
  local copies, waits for them, and re-layouts  20.4 us (8%)
  other arithmetic  6.48 us (3%)
    ppermute x32, starting transfers between devices, move(): return lax.ppermute(x, axes, pairs(dlat, dlon))  96.5 us
    pallas_call x2, Pallas kernels, attend(): pl.pallas_call(functools.partial(attend_kernel, grid_height), grid=(18,),...  54.7 us
    pallas_call x2, Pallas kernels, feed(): pl.pallas_call(functools.partial(feed_kernel, last), grid=(W // PW,), in_...  48 us
    ppermute x32, waiting for transfers between devices, move(): return lax.ppermute(x, axes, pairs(dlat, dlon))  27.4 us
  transfers between devices with their start and end apart: 32, of which 5 were waited for; matrix products, arithmetic and copies ran while one was open for 7% of the time, Pallas kernels for 0%

profile of v1, /device:TPU:0, one launch (start us, length us, event | category | flops | bytes accessed | tf_op | source)
XLA Modules:
  0.0 256.0 jit_solution(14902521592461821143)
XLA Ops:
  9.4 9.3 %collective-permute-start = (bf16[6,48,512]{2,1,0:T(8,128)(2,1)S(1)}, bf16[6,48,512]{2,1,0:T(8,128)(2,1)S(1)}, u32[]{:S(2)}, u32[]{:S(2)}) collective-permute-start(bf16[6,48,512]{2,1,0:T(8,128)(2,1)S(1)} %get-tuple-element.58), channel_id=1, source_target_pairs={{0,1},{8,9},{16,17},{24,25},{32,33},{40,41},{48,49},{56,57},{64,65... | collective-permute-start | bytes 884744 | tf_op jit(solution)/shard_map/ppermute | solution.py:279
  18.8 7.0 %collective-permute-start.5 = (bf16[6,6,512]{2,1,0:T(8,128)(2,1)S(1)}, bf16[6,6,512]{2,1,0:T(8,128)(2,1)S(1)}, u32[]{:S(2)}, u32[]{:S(2)}) collective-permute-start(bf16[6,6,512]{2,1,0:T(8,128)(2,1)S(1)} %get-tuple-element.67), channel_id=1, source_target_pairs={{0,121},{8,1},{16,9},{24,17},{32,25},{40,33},{48,41},{56,49},{64,5... | collective-permute-start | bytes 110600 | tf_op jit(solution)/shard_map/ppermute | solution.py:279
  31.2 2.3 slice_bitcast_fusion
  34.3 4.5 %collective-permute-start.4 = (bf16[6,6,512]{2,1,0:T(8,128)(2,1)S(1)}, bf16[6,6,512]{2,1,0:T(8,128)(2,1)S(1)}, u32[]{:S(2)}, u32[]{:S(2)}) collective-permute-start(bf16[6,6,512]{2,1,0:T(8,128)(2,1)S(1)} %get-tuple-element.68), channel_id=1, source_target_pairs={{0,9},{8,17},{16,25},{24,33},{32,41},{40,49},{48,57},{56,65},{64,7... | collective-permute-start | bytes 110600 | tf_op jit(solution)/shard_map/ppermute | solution.py:279
  43.5 27.4 %attend.2 = (f32[24,48,512]{2,1,0:T(8,128)}, bf16[24,48,512]{2,1,0:T(8,128)(2,1)}, bf16[3,48,512]{2,1,0:T(8,128)(2,1)}, bf16[3,48,512]{2,1,0:T(8,128)(2,1)}, bf1...) custom-call(s32[1]{0:T(128)} %bitcast.band_ref, f32[24,48,512]{2,1,0:T(8,128)} %convert_element_type.28.stream_ref, ...), custom_call_target="tpu_custom_call" | custom-call | tf_op jit(solution)/shard_map/attend/pallas_call | solution.py:167
  71.7 6.2 %collective-permute-start.13 = (bf16[3,3,512]{2,1,0:T(4,128)(2,1)S(1)}, bf16[3,3,512]{2,1,0:T(4,128)(2,1)S(1)}, u32[]{:S(2)}, u32[]{:S(2)}) collective-permute-start(bf16[3,3,512]{2,1,0:T(4,128)(2,1)S(1)} %get-tuple-element.75), channel_id=1, source_target_pairs={{0,121},{8,1},{16,9},{24,17},{32,25},{40,33},{48,41},{56,49},{64,5... | collective-permute-start | bytes 27656 | tf_op jit(solution)/shard_map/ppermute | solution.py:279
  77.9 3.4 %collective-permute-start.12 = (bf16[3,3,512]{2,1,0:T(4,128)(2,1)S(1)}, bf16[3,3,512]{2,1,0:T(4,128)(2,1)S(1)}, u32[]{:S(2)}, u32[]{:S(2)}) collective-permute-start(bf16[3,3,512]{2,1,0:T(4,128)(2,1)S(1)} %get-tuple-element.76), channel_id=1, source_target_pairs={{0,9},{8,17},{16,25},{24,33},{32,41},{40,49},{48,57},{56,65},{64,7... | collective-permute-start | bytes 27656 | tf_op jit(solution)/shard_map/ppermute | solution.py:279
  83.5 2.7 %slice_bitcast_fusion.3 = (bf16[512,2048]{1,0:T(8,128)(2,1)}, bf16[512,2048]{1,0:T(8,128)(2,1)}) fusion(bf16[2,512,2048]{2,1,0:T(8,128)(2,1)S(1)} %copy-done.2), kind=kLoop, calls=%fused_computation.4 | loop fusion | bytes 8388608 | tf_op jit(solution)/shard_map/squeeze | solution.py:326
  86.2 6.7 %collective-permute-start.8 = (bf16[3,48,512]{2,1,0:T(8,128)(2,1)S(1)}, bf16[3,48,512]{2,1,0:T(8,128)(2,1)S(1)}, u32[]{:S(2)}, u32[]{:S(2)}) collective-permute-start(bf16[3,48,512]{2,1,0:T(8,128)(2,1)S(1)} %copy-done.41), channel_id=1, source_target_pairs={{0,1},{8,9},{16,17},{24,25},{32,33},{40,41},{48,49},{56,57},{64,65... | collective-permute-start | bytes 442376 | tf_op jit(solution)/shard_map/ppermute | solution.py:279
  95.7 5.6 %collective-permute-start.11 = (bf16[24,3,512]{2,1,0:T(4,128)(2,1)S(1)}, bf16[24,3,512]{2,1,0:T(4,128)(2,1)S(1)}, u32[]{:S(2)}, u32[]{:S(2)}) collective-permute-start(bf16[24,3,512]{2,1,0:T(4,128)(2,1)S(1)} %copy-done.43), channel_id=1, source_target_pairs={{0,120},{8,0},{16,8},{24,16},{32,24},{40,32},{48,40},{56,48},{64,5... | collective-permute-start | bytes 221192 | tf_op jit(solution)/shard_map/ppermute | solution.py:279
  101.3 2.3 slice_bitcast_fusion.2
  104.5 24.6 %feed.2 = (f32[24,48,512]{2,1,0:T(8,128)}, bf16[6,48,512]{2,1,0:T(8,128)(2,1)}, bf16[6,48,512]{2,1,0:T(8,128)(2,1)}, bf16[24,6,512]{2,1,0:T(8,128)(2,1)}, bf16[24,6,512]{2,1,0:T(8,128)(2,1)}) custom-call(bf16[24,48,512]{2,1,0:T(8,128)(2,1)} %get-tuple-element.22.own_ref, f32[24,48,512]{2,1,0:T(8,128)} %get-tuple-element.23.stream_ref, ...), custom_call_target="tpu_custom_call" | custom-call | tf_op jit(solution)/shard_map/feed/pallas_call | solution.py:239
  129.9 11.0 %collective-permute-start.21 = (bf16[6,6,512]{2,1,0:T(8,128)(2,1)S(1)}, bf16[6,6,512]{2,1,0:T(8,128)(2,1)S(1)}, u32[]{:S(2)}, u32[]{:S(2)}) collective-permute-start(bf16[6,6,512]{2,1,0:T(8,128)(2,1)S(1)} %get-tuple-element.63), channel_id=1, source_target_pairs={{0,121},{8,1},{16,9},{24,17},{32,25},{40,33},{48,41},{56,49},{64,5... | collective-permute-start | bytes 110600 | tf_op jit(solution)/shard_map/ppermute | solution.py:279
  140.9 3.6 %collective-permute-start.16 = (bf16[6,48,512]{2,1,0:T(8,128)(2,1)}, bf16[6,48,512]{2,1,0:T(8,128)(2,1)S(1)}, u32[]{:S(2)}, u32[]{:S(2)}) collective-permute-start(bf16[6,48,512]{2,1,0:T(8,128)(2,1)} %get-tuple-element.29), channel_id=1, source_target_pairs={{0,1},{8,9},{16,17},{24,25},{32,33},{40,41},{48,49},{56,57},{64,65... | collective-permute-start | bytes 884744 | tf_op jit(solution)/shard_map/ppermute | solution.py:279
  145.9 6.4 %collective-permute-start.19 = (bf16[24,6,512]{2,1,0:T(8,128)(2,1)}, bf16[24,6,512]{2,1,0:T(8,128)(2,1)S(1)}, u32[]{:S(2)}, u32[]{:S(2)}) collective-permute-start(bf16[24,6,512]{2,1,0:T(8,128)(2,1)} %get-tuple-element.32), channel_id=1, source_target_pairs={{0,120},{8,0},{16,8},{24,16},{32,24},{40,32},{48,40},{56,48},{64,5... | collective-permute-start | bytes 442376 | tf_op jit(solution)/shard_map/ppermute | solution.py:279
  155.7 4.7 %collective-permute-done.23.refs_7_ = bf16[6,6,512]{2,1,0:T(8,128)(2,1)S(1)} collective-permute-done((bf16[6,6,512]{2,1,0:T(8,128)(2,1)S(1)}, bf16[6,6,512]{2,1,0:T(8,128)(2,1)S(1)}, u32[]{:S(2)}, u32[]{:S(2)}) %collective-permute-start.23) | collective-permute-done | bytes 36896 | tf_op jit(solution)/shard_map/ppermute | solution.py:279
  161.7 9.1 %collective-permute-done.22.refs_6_ = bf16[6,6,512]{2,1,0:T(8,128)(2,1)S(1)} collective-permute-done((bf16[6,6,512]{2,1,0:T(8,128)(2,1)S(1)}, bf16[6,6,512]{2,1,0:T(8,128)(2,1)S(1)}, u32[]{:S(2)}, u32[]{:S(2)}) %collective-permute-start.22) | collective-permute-done | bytes 36896 | tf_op jit(solution)/shard_map/ppermute | solution.py:279
  171.8 27.2 %attend.3 = (f32[24,48,512]{2,1,0:T(8,128)}, bf16[24,48,512]{2,1,0:T(8,128)(2,1)}, bf16[3,48,512]{2,1,0:T(8,128)(2,1)}, bf16[3,48,512]{2,1,0:T(8,128)(2,1)}, bf1...) custom-call(s32[1]{0:T(128)} %bitcast.band_ref, f32[24,48,512]{2,1,0:T(8,128)} %get-tuple-element.28.stream_ref, ...), custom_call_target="tpu_custom_call" | custom-call | tf_op jit(solution)/shard_map/attend/pallas_call | solution.py:167
  199.8 4.5 %collective-permute-start.29 = (bf16[3,3,512]{2,1,0:T(4,128)(2,1)S(1)}, bf16[3,3,512]{2,1,0:T(4,128)(2,1)S(1)}, u32[]{:S(2)}, u32[]{:S(2)}) collective-permute-start(bf16[3,3,512]{2,1,0:T(4,128)(2,1)S(1)} %get-tuple-element.71), channel_id=1, source_target_pairs={{0,121},{8,1},{16,9},{24,17},{32,25},{40,33},{48,41},{56,49},{64,5... | collective-permute-start | bytes 27656 | tf_op jit(solution)/shard_map/ppermute | solution.py:279
  205.7 3.8 %collective-permute-start.28 = (bf16[3,3,512]{2,1,0:T(4,128)(2,1)S(1)}, bf16[3,3,512]{2,1,0:T(4,128)(2,1)S(1)}, u32[]{:S(2)}, u32[]{:S(2)}) collective-permute-start(bf16[3,3,512]{2,1,0:T(4,128)(2,1)S(1)} %get-tuple-element.72), channel_id=1, source_target_pairs={{0,9},{8,17},{16,25},{24,33},{32,41},{40,49},{48,57},{56,65},{64,7... | collective-permute-start | bytes 27656 | tf_op jit(solution)/shard_map/ppermute | solution.py:279
  209.6 5.6 %collective-permute-start.27 = (bf16[24,3,512]{2,1,0:T(4,128)(2,1)}, bf16[24,3,512]{2,1,0:T(4,128)(2,1)S(1)}, u32[]{:S(2)}, u32[]{:S(2)}) collective-permute-start(bf16[24,3,512]{2,1,0:T(4,128)(2,1)} %get-tuple-element.38), channel_id=1, source_target_pairs={{0,120},{8,0},{16,8},{24,16},{32,24},{40,32},{48,40},{56,48},{64,5... | collective-permute-start | bytes 221192 | tf_op jit(solution)/shard_map/ppermute | solution.py:279
  218.6 3.9 %collective-permute-done.31.refs_7_ = bf16[3,3,512]{2,1,0:T(4,128)(2,1)S(1)} collective-permute-done((bf16[3,3,512]{2,1,0:T(4,128)(2,1)S(1)}, bf16[3,3,512]{2,1,0:T(4,128)(2,1)S(1)}, u32[]{:S(2)}, u32[]{:S(2)}) %collective-permute-start.31) | collective-permute-done | bytes 9248 | tf_op jit(solution)/shard_map/ppermute | solution.py:279
  223.8 8.2 %collective-permute-done.30.refs_6_ = bf16[3,3,512]{2,1,0:T(4,128)(2,1)S(1)} collective-permute-done((bf16[3,3,512]{2,1,0:T(4,128)(2,1)S(1)}, bf16[3,3,512]{2,1,0:T(4,128)(2,1)S(1)}, u32[]{:S(2)}, u32[]{:S(2)}) %collective-permute-start.30) | collective-permute-done | bytes 9248 | tf_op jit(solution)/shard_map/ppermute | solution.py:279
  232.7 23.3 %feed.3 = bf16[24,48,512]{2,1,0:T(8,128)(2,1)} custom-call(bf16[24,48,512]{2,1,0:T(8,128)(2,1)} %get-tuple-element.33.own_ref, f32[24,48,512]{2,1,0:T(8,128)} %get-tuple-element.34.stream_ref, bf16[3,48,512]{2,1,0:T(8,128)(2,1)} %copy-done.14, bf16[3,48,512]{2,1,0:T(8,128)(2,1)} %copy-done.17, bf16[24,3,512]{2,1,0:T(4,128)(2,1)} %copy-done.18, ...), custom_call_target="tpu_custom_call" | custom-call | tf_op jit(solution)/shard_map/feed/pallas_call | solution.py:239
  (163 shorter events, 41.8 us)
Async XLA Ops:
  5.5 37.1 %collective-permute-start.1 = (bf16[6,48,512]{2,1,0:T(8,128)(2,1)S(1)}, bf16[6,48,512]{2,1,0:T(8,128)(2,1)S(1)}, u32[]{:S(2)}, u32[]{:S(2)}) collective-permute-start(bf16[6,48,512]{2,1,0:T(8,128)(2,1)S(1)} %get-tuple-element.57), channel_id=1, source_target_pairs={{1,0},{9,8},{17,16},{25,24},{33,32},{41,40},{49,48},{57,56},{65,64... | collective-permute-start | bytes 884744 | tf_op jit(solution)/shard_map/ppermute | solution.py:279
  6.8 26.9 %collective-permute-start.7 = (bf16[6,6,512]{2,1,0:T(8,128)(2,1)S(1)}, bf16[6,6,512]{2,1,0:T(8,128)(2,1)S(1)}, u32[]{:S(2)}, u32[]{:S(2)}) collective-permute-start(bf16[6,6,512]{2,1,0:T(8,128)(2,1)S(1)} %get-tuple-element.65), channel_id=1, source_target_pairs={{1,120},{9,0},{17,8},{25,16},{33,24},{41,32},{49,40},{57,48},{65,5... | collective-permute-start | bytes 110600 | tf_op jit(solution)/shard_map/ppermute | solution.py:279
  8.2 25.7 %collective-permute-start.6 = (bf16[6,6,512]{2,1,0:T(8,128)(2,1)S(1)}, bf16[6,6,512]{2,1,0:T(8,128)(2,1)S(1)}, u32[]{:S(2)}, u32[]{:S(2)}) collective-permute-start(bf16[6,6,512]{2,1,0:T(8,128)(2,1)S(1)} %get-tuple-element.66), channel_id=1, source_target_pairs={{1,8},{9,16},{17,24},{25,32},{33,40},{41,48},{49,56},{57,64},{65,7... | collective-permute-start | bytes 110600 | tf_op jit(solution)/shard_map/ppermute | solution.py:279
  9.4 33.2 %collective-permute-start = (bf16[6,48,512]{2,1,0:T(8,128)(2,1)S(1)}, bf16[6,48,512]{2,1,0:T(8,128)(2,1)S(1)}, u32[]{:S(2)}, u32[]{:S(2)}) collective-permute-start(bf16[6,48,512]{2,1,0:T(8,128)(2,1)S(1)} %get-tuple-element.58), channel_id=1, source_target_pairs={{0,1},{8,9},{16,17},{24,25},{32,33},{40,41},{48,49},{56,57},{64,65... | collective-permute-start | bytes 884744 | tf_op jit(solution)/shard_map/ppermute | solution.py:279
  18.8 15.5 %collective-permute-start.5 = (bf16[6,6,512]{2,1,0:T(8,128)(2,1)S(1)}, bf16[6,6,512]{2,1,0:T(8,128)(2,1)S(1)}, u32[]{:S(2)}, u32[]{:S(2)}) collective-permute-start(bf16[6,6,512]{2,1,0:T(8,128)(2,1)S(1)} %get-tuple-element.67), channel_id=1, source_target_pairs={{0,121},{8,1},{16,9},{24,17},{32,25},{40,33},{48,41},{56,49},{64,5... | collective-permute-start | bytes 110600 | tf_op jit(solution)/shard_map/ppermute | solution.py:279
  71.7 22.6 %collective-permute-start.13 = (bf16[3,3,512]{2,1,0:T(4,128)(2,1)S(1)}, bf16[3,3,512]{2,1,0:T(4,128)(2,1)S(1)}, u32[]{:S(2)}, u32[]{:S(2)}) collective-permute-start(bf16[3,3,512]{2,1,0:T(4,128)(2,1)S(1)} %get-tuple-element.75), channel_id=1, source_target_pairs={{0,121},{8,1},{16,9},{24,17},{32,25},{40,33},{48,41},{56,49},{64,5... | collective-permute-start | bytes 27656 | tf_op jit(solution)/shard_map/ppermute | solution.py:279
  77.9 17.7 %collective-permute-start.12 = (bf16[3,3,512]{2,1,0:T(4,128)(2,1)S(1)}, bf16[3,3,512]{2,1,0:T(4,128)(2,1)S(1)}, u32[]{:S(2)}, u32[]{:S(2)}) collective-permute-start(bf16[3,3,512]{2,1,0:T(4,128)(2,1)S(1)} %get-tuple-element.76), channel_id=1, source_target_pairs={{0,9},{8,17},{16,25},{24,33},{32,41},{40,49},{48,57},{56,65},{64,7... | collective-permute-start | bytes 27656 | tf_op jit(solution)/shard_map/ppermute | solution.py:279
  82.0 13.7 %collective-permute-start.15 = (bf16[3,3,512]{2,1,0:T(4,128)(2,1)S(1)}, bf16[3,3,512]{2,1,0:T(4,128)(2,1)S(1)}, u32[]{:S(2)}, u32[]{:S(2)}) collective-permute-start(bf16[3,3,512]{2,1,0:T(4,128)(2,1)S(1)} %get-tuple-element.73), channel_id=1, source_target_pairs={{1,120},{9,0},{17,8},{25,16},{33,24},{41,32},{49,40},{57,48},{65,5... | collective-permute-start | bytes 27656 | tf_op jit(solution)/shard_map/ppermute | solution.py:279
  86.2 17.5 %collective-permute-start.8 = (bf16[3,48,512]{2,1,0:T(8,128)(2,1)S(1)}, bf16[3,48,512]{2,1,0:T(8,128)(2,1)S(1)}, u32[]{:S(2)}, u32[]{:S(2)}) collective-permute-start(bf16[3,48,512]{2,1,0:T(8,128)(2,1)S(1)} %copy-done.41), channel_id=1, source_target_pairs={{0,1},{8,9},{16,17},{24,25},{32,33},{40,41},{48,49},{56,57},{64,65... | collective-permute-start | bytes 442376 | tf_op jit(solution)/shard_map/ppermute | solution.py:279
  93.0 10.7 %collective-permute-start.9 = (bf16[3,48,512]{2,1,0:T(8,128)(2,1)S(1)}, bf16[3,48,512]{2,1,0:T(8,128)(2,1)S(1)}, u32[]{:S(2)}, u32[]{:S(2)}) collective-permute-start(bf16[3,48,512]{2,1,0:T(8,128)(2,1)S(1)} %copy-done.40), channel_id=1, source_target_pairs={{1,0},{9,8},{17,16},{25,24},{33,32},{41,40},{49,48},{57,56},{65,64... | collective-permute-start | bytes 442376 | tf_op jit(solution)/shard_map/ppermute | solution.py:279
  129.9 22.3 %collective-permute-start.21 = (bf16[6,6,512]{2,1,0:T(8,128)(2,1)S(1)}, bf16[6,6,512]{2,1,0:T(8,128)(2,1)S(1)}, u32[]{:S(2)}, u32[]{:S(2)}) collective-permute-start(bf16[6,6,512]{2,1,0:T(8,128)(2,1)S(1)} %get-tuple-element.63), channel_id=1, source_target_pairs={{0,121},{8,1},{16,9},{24,17},{32,25},{40,33},{48,41},{56,49},{64,5... | collective-permute-start | bytes 110600 | tf_op jit(solution)/shard_map/ppermute | solution.py:279
  140.9 30.0 %collective-permute-start.16 = (bf16[6,48,512]{2,1,0:T(8,128)(2,1)}, bf16[6,48,512]{2,1,0:T(8,128)(2,1)S(1)}, u32[]{:S(2)}, u32[]{:S(2)}) collective-permute-start(bf16[6,48,512]{2,1,0:T(8,128)(2,1)} %get-tuple-element.29), channel_id=1, source_target_pairs={{0,1},{8,9},{16,17},{24,25},{32,33},{40,41},{48,49},{56,57},{64,65... | collective-permute-start | bytes 884744 | tf_op jit(solution)/shard_map/ppermute | solution.py:279
  144.5 9.9 %collective-permute-start.20 = (bf16[6,6,512]{2,1,0:T(8,128)(2,1)S(1)}, bf16[6,6,512]{2,1,0:T(8,128)(2,1)S(1)}, u32[]{:S(2)}, u32[]{:S(2)}) collective-permute-start(bf16[6,6,512]{2,1,0:T(8,128)(2,1)S(1)} %get-tuple-element.64), channel_id=1, source_target_pairs={{0,9},{8,17},{16,25},{24,33},{32,41},{40,49},{48,57},{56,65},{64,7... | collective-permute-start | bytes 110600 | tf_op jit(solution)/shard_map/ppermute | solution.py:279
  145.8 25.0 %collective-permute-start.18 = (bf16[24,6,512]{2,1,0:T(8,128)(2,1)}, bf16[24,6,512]{2,1,0:T(8,128)(2,1)S(1)}, u32[]{:S(2)}, u32[]{:S(2)}) collective-permute-start(bf16[24,6,512]{2,1,0:T(8,128)(2,1)} %get-tuple-element.31), channel_id=1, source_target_pairs={{0,8},{8,16},{16,24},{24,32},{32,40},{40,48},{48,56},{56,64},{64,7... | collective-permute-start | bytes 442376 | tf_op jit(solution)/shard_map/ppermute | solution.py:279
  145.9 25.0 %collective-permute-start.19 = (bf16[24,6,512]{2,1,0:T(8,128)(2,1)}, bf16[24,6,512]{2,1,0:T(8,128)(2,1)S(1)}, u32[]{:S(2)}, u32[]{:S(2)}) collective-permute-start(bf16[24,6,512]{2,1,0:T(8,128)(2,1)} %get-tuple-element.32), channel_id=1, source_target_pairs={{0,120},{8,0},{16,8},{24,16},{32,24},{40,32},{48,40},{56,48},{64,5... | collective-permute-start | bytes 442376 | tf_op jit(solution)/shard_map/ppermute | solution.py:279
  152.3 18.6 %collective-permute-start.17 = (bf16[6,48,512]{2,1,0:T(8,128)(2,1)}, bf16[6,48,512]{2,1,0:T(8,128)(2,1)S(1)}, u32[]{:S(2)}, u32[]{:S(2)}) collective-permute-start(bf16[6,48,512]{2,1,0:T(8,128)(2,1)} %get-tuple-element.30), channel_id=1, source_target_pairs={{1,0},{9,8},{17,16},{25,24},{33,32},{41,40},{49,48},{57,56},{65,64... | collective-permute-start | bytes 884744 | tf_op jit(solution)/shard_map/ppermute | solution.py:279
  160.4 10.4 %collective-permute-start.22 = (bf16[6,6,512]{2,1,0:T(8,128)(2,1)S(1)}, bf16[6,6,512]{2,1,0:T(8,128)(2,1)S(1)}, u32[]{:S(2)}, u32[]{:S(2)}) collective-permute-start(bf16[6,6,512]{2,1,0:T(8,128)(2,1)S(1)} %get-tuple-element.62), channel_id=1, source_target_pairs={{1,8},{9,16},{17,24},{25,32},{33,40},{41,48},{49,56},{57,64},{65,7... | collective-permute-start | bytes 110600 | tf_op jit(solution)/shard_map/ppermute | solution.py:279
  199.8 15.4 %collective-permute-start.29 = (bf16[3,3,512]{2,1,0:T(4,128)(2,1)S(1)}, bf16[3,3,512]{2,1,0:T(4,128)(2,1)S(1)}, u32[]{:S(2)}, u32[]{:S(2)}) collective-permute-start(bf16[3,3,512]{2,1,0:T(4,128)(2,1)S(1)} %get-tuple-element.71), channel_id=1, source_target_pairs={{0,121},{8,1},{16,9},{24,17},{32,25},{40,33},{48,41},{56,49},{64,5... | collective-permute-start | bytes 27656 | tf_op jit(solution)/shard_map/ppermute | solution.py:279
  204.4 27.6 %collective-permute-start.24 = (bf16[3,48,512]{2,1,0:T(8,128)(2,1)}, bf16[3,48,512]{2,1,0:T(8,128)(2,1)S(1)}, u32[]{:S(2)}, u32[]{:S(2)}) collective-permute-start(bf16[3,48,512]{2,1,0:T(8,128)(2,1)} %get-tuple-element.35), channel_id=1, source_target_pairs={{0,1},{8,9},{16,17},{24,25},{32,33},{40,41},{48,49},{56,57},{64,65... | collective-permute-start | bytes 442376 | tf_op jit(solution)/shard_map/ppermute | solution.py:279
  205.7 11.6 %collective-permute-start.28 = (bf16[3,3,512]{2,1,0:T(4,128)(2,1)S(1)}, bf16[3,3,512]{2,1,0:T(4,128)(2,1)S(1)}, u32[]{:S(2)}, u32[]{:S(2)}) collective-permute-start(bf16[3,3,512]{2,1,0:T(4,128)(2,1)S(1)} %get-tuple-element.72), channel_id=1, source_target_pairs={{0,9},{8,17},{16,25},{24,33},{32,41},{40,49},{48,57},{56,65},{64,7... | collective-permute-start | bytes 27656 | tf_op jit(solution)/shard_map/ppermute | solution.py:279
  209.5 22.4 %collective-permute-start.26 = (bf16[24,3,512]{2,1,0:T(4,128)(2,1)}, bf16[24,3,512]{2,1,0:T(4,128)(2,1)S(1)}, u32[]{:S(2)}, u32[]{:S(2)}) collective-permute-start(bf16[24,3,512]{2,1,0:T(4,128)(2,1)} %get-tuple-element.37), channel_id=1, source_target_pairs={{0,8},{8,16},{16,24},{24,32},{32,40},{40,48},{48,56},{56,64},{64,7... | collective-permute-start | bytes 221192 | tf_op jit(solution)/shard_map/ppermute | solution.py:279
  209.6 22.4 %collective-permute-start.27 = (bf16[24,3,512]{2,1,0:T(4,128)(2,1)}, bf16[24,3,512]{2,1,0:T(4,128)(2,1)S(1)}, u32[]{:S(2)}, u32[]{:S(2)}) collective-permute-start(bf16[24,3,512]{2,1,0:T(4,128)(2,1)} %get-tuple-element.38), channel_id=1, source_target_pairs={{0,120},{8,0},{16,8},{24,16},{32,24},{40,32},{48,40},{56,48},{64,5... | collective-permute-start | bytes 221192 | tf_op jit(solution)/shard_map/ppermute | solution.py:279
  215.2 16.8 %collective-permute-start.25 = (bf16[3,48,512]{2,1,0:T(8,128)(2,1)}, bf16[3,48,512]{2,1,0:T(8,128)(2,1)S(1)}, u32[]{:S(2)}, u32[]{:S(2)}) collective-permute-start(bf16[3,48,512]{2,1,0:T(8,128)(2,1)} %get-tuple-element.36), channel_id=1, source_target_pairs={{1,0},{9,8},{17,16},{25,24},{33,32},{41,40},{49,48},{57,56},{65,64... | collective-permute-start | bytes 442376 | tf_op jit(solution)/shard_map/ppermute | solution.py:279
  222.5 9.5 %collective-permute-start.30 = (bf16[3,3,512]{2,1,0:T(4,128)(2,1)S(1)}, bf16[3,3,512]{2,1,0:T(4,128)(2,1)S(1)}, u32[]{:S(2)}, u32[]{:S(2)}) collective-permute-start(bf16[3,3,512]{2,1,0:T(4,128)(2,1)S(1)} %get-tuple-element.70), channel_id=1, source_target_pairs={{1,8},{9,16},{17,24},{25,32},{33,40},{41,48},{49,56},{57,64},{65,7... | collective-permute-start | bytes 27656 | tf_op jit(solution)/shard_map/ppermute | solution.py:279
  (53 other events, 460.0 us)

commit v2 on v1

v2 whole, which is shorter than its diff:
```python
import functools
import math

import jax
import jax.numpy as jnp
import numpy as np
from jax import lax
from jax.experimental import pallas as pl
from jax.experimental.pallas import tpu as pltpu
from jax.sharding import PartitionSpec as P

BF, F32 = jnp.bfloat16, jnp.float32
D, FF = 512, 2048
RADIUS = 6
REACH = 3
LAYERS = 2
H, W = 24, 48
PH, PW = 12, 8
LH, LW = PH + 2 * REACH, PW + 2 * REACH
SLAB = 24
HALF = LH * LW // 2 + 2
CHUNK = 1024
VMEM = 40 * 2**20


def transforms():
    seen, reps = set(), []
    for a in range(LH):
        for b in range(LW):
            mirror = ((-a) % LH, (-b) % LW)
            if mirror not in seen:
                seen.add((a, b))
                reps.append((a / LH, b / LW, (1.0 if mirror == (a, b) else 2.0) / (LH * LW)))
    fa, fb, weight = np.array(reps).T[:, :, None, None]
    angle = 2 * np.pi * (fa * np.arange(LH)[:, None] + fb * np.arange(LW))
    cos, sin = np.cos(angle), np.sin(angle)
    sin[np.abs(sin) < 1e-9] = 0
    forward = np.zeros((2 * HALF, LH, SLAB))
    first = 8 - REACH
    forward[:HALF, :, first : first + LW] = cos
    forward[HALF:, :, first : first + LW] = -sin
    inverse = np.concatenate(
        [cos[:, :PH, :PW].reshape(HALF, -1).T, -sin[:, :PH, :PW].reshape(HALF, -1).T], 1
    )
    taps = np.concatenate([(cos * weight)[:, :7, :7], (sin * weight)[:, :7, :7]], 0)
    return forward.reshape(2 * HALF, -1), inverse, taps.reshape(2 * HALF, -1)


def norm(x, gain):
    c = x - jnp.mean(x, axis=-1, keepdims=True)
    return c * lax.rsqrt(jnp.mean(c * c, axis=-1, keepdims=True) + 1e-5) * gain


def gelu(x):
    return 0.5 * x * (1.0 + lax.erf(x * np.float32(1 / math.sqrt(2))))


def whole(a):
    return pl.BlockSpec(a.shape, lambda p: (0,) * len(a.shape))


def of_layer(a, layer):
    return pl.BlockSpec((None,) + a.shape[1:], lambda p: (layer,) + (0,) * (len(a.shape) - 1))


def shape(*dims, dtype=BF):
    return jax.ShapeDtypeStruct(dims, dtype)


def call(body, name, grid, args, specs, outs, out_specs, scratch, cost):
    return pl.pallas_call(
        body,
        grid=(grid,),
        in_specs=specs,
        out_specs=out_specs,
        out_shape=outs,
        scratch_shapes=scratch,
        compiler_params=pltpu.CompilerParams(vmem_limit_bytes=VMEM),
        cost_estimate=pl.CostEstimate(flops=int(cost * 6e8), bytes_accessed=10**6, transcendentals=0),
        name=name,
    )(*args)


def project_kernel(x_ref, win_ref, gain_ref, q_ref, kv_ref):
    y = norm(x_ref[...].astype(F32).reshape(6 * W, D), gain_ref[...])
    q = jnp.dot(y.astype(BF), win_ref[:, :D], preferred_element_type=F32)
    q_ref[...] = (q * 0.125).astype(BF).reshape(6, W, D)
    y = y.reshape(6, W, D)[:, 8:40].reshape(6 * 32, D).astype(BF)
    kv_ref[...] = jnp.dot(y, win_ref[:, D:], preferred_element_type=F32).astype(BF).reshape(6, 32, 2 * D)


def project(layer, x, win, gains):
    def rows(width, depth):
        return pl.BlockSpec((6, width, depth), lambda p: (p, 0, 0))

    return call(
        project_kernel,
        "project",
        H // 6,
        (x, win, gains),
        [rows(W, D), of_layer(win, layer), of_layer(gains, layer)],
        (shape(H, W, D), shape(H, 32, 2 * D)),
        (rows(W, D), rows(32, 2 * D)),
        [],
        4,
    )


def fill_mask(mask, t, i, band, grid_height):
    row = lax.broadcasted_iota(jnp.int32, (64, 512), 0)
    col = lax.broadcasted_iota(jnp.int32, (64, 512), 1)
    a, b, u, v = row >> 4, row & 15, col >> 5, col & 31
    lat = band * H + i * 4 - RADIUS + u
    ok = (u >= a) & (u <= a + 12) & (v >= b + 2) & (v <= b + 14) & (lat >= 0) & (lat < grid_height)
    mask[t] = jnp.where(ok, 0.0, -jnp.inf)


def attend_block(qb, keys, mask):
    head = lax.broadcasted_iota(jnp.int32, (64, 256), 1) >> 6
    outs = []
    for g in range(2):
        k, v = keys[:, g * 256 : (g + 1) * 256], keys[:, D + g * 256 : D + (g + 1) * 256]
        qg = qb[:, g * 256 : (g + 1) * 256]
        qbd = jnp.concatenate([jnp.where(head == h, qg, jnp.zeros_like(qg)) for h in range(4)], 0)
        s = lax.dot_general(qbd, k, (((1,), (1,)), ((), ())), preferred_element_type=F32)
        s = (s.reshape(4, 64, 512) + mask[None]).reshape(256, 512)
        p = jnp.exp(s - jnp.max(s, axis=1, keepdims=True))
        total = jnp.sum(p, axis=1, keepdims=True)
        o = jnp.dot(p.astype(BF), v, preferred_element_type=F32) * (1.0 / total)
        r = o[192:]
        for h in range(3):
            r = jnp.where(head == h, o[h * 64 : (h + 1) * 64], r)
        outs.append(r.astype(BF))
    return jnp.concatenate(outs, 1)


def attend_kernel(kind, raw, bands, grid_height, band_ref, *refs):
    (q0, q1, x0, x1, wout_ref, gf_ref), refs = refs[:6], refs[6:]
    j = pl.program_id(0)
    gain = refs[0]

    def incoming(piece):
        piece = piece[...].astype(F32)
        return norm(piece, gain[...]) if raw else piece

    @pl.when(j == 0)
    def _():
        for t in range(2):
            fill_mask(refs[-1], t, bands[t], band_ref[0], grid_height)

    j16 = pl.multiple_of(j * 16, 16)
    columns = pl.ds(j16, 32)
    if kind == "inner":
        ga, win, kvm, x, w, e, xo, yo, wo, eo, kv, wide, mask = refs

        @pl.when(j == 0)
        def _():
            edge = jnp.zeros((H, 2, D), F32)
            wide[0, :, 0:2] = edge
            wide[0, :, 2:8] = incoming(w)
            wide[0, :, 8:16] = norm(x[:, 0:16].astype(F32)[:, :8], ga[...])
            wide[1, :, 0:8] = norm(x[:, 32:48].astype(F32)[:, 8:], ga[...])
            wide[1, :, 8:14] = incoming(e)
            wide[1, :, 14:16] = edge
            for side in range(2):
                y = wide[side].reshape(H * 16, D).astype(BF)
                y = jnp.dot(y, win[:, D:], preferred_element_type=F32)
                kv[:, side * 48 : side * 48 + 16] = y.astype(BF).reshape(H, 16, 2 * D)
            kv[:, 16:48] = kvm[...]

        windows = [kv[i * 4 - RADIUS : i * 4 - RADIUS + 16, columns] for i in bands]
    elif kind == "outer":
        ga, win, kv, n, s, xo, yo, wo, eo, no, so, kvh, wide, halo, mask = refs

        @pl.when(j == 0)
        def _():
            edge = jnp.zeros((12, 2, D), F32)
            wide[:, 0:2] = edge
            wide[:, 62:64] = edge
            wide[:6, 2:62] = incoming(n)
            wide[6:, 2:62] = incoming(s)
            y = wide[...].reshape(12 * 64, D).astype(BF)
            halo[...] = jnp.dot(y, win[:, D:], preferred_element_type=F32).astype(BF).reshape(12, 64, 2 * D)
            kvh[...] = halo[4:8]

        windows = [
            jnp.concatenate([halo[:6, columns], kv[:10, columns]], 0),
            jnp.concatenate([kv[14:, columns], halo[6:, columns]], 0),
        ]
    else:
        ga, kv, kvh, xo, yo, wo, eo, mask = refs
        windows = [
            jnp.concatenate([kvh[:2, columns], kv[:14, columns]], 0),
            jnp.concatenate([kv[10:, columns], kvh[2:, columns]], 0),
        ]
    mixed, old = [], []
    for t in range(2):
        qb = (q0, q1)[t][:, pl.ds(j16, 16)].reshape(64, D)
        mixed.append(attend_block(qb, windows[t].reshape(512, 2 * D), mask[t]))
        old.append((x0, x1)[t][:, pl.ds(j16, 16)].reshape(64, D).astype(F32))
    new = jnp.dot(jnp.concatenate(mixed, 0), wout_ref[...], preferred_element_type=F32)
    new = new + jnp.concatenate(old, 0)
    y = norm(new, gf_ref[...]).astype(BF).reshape(8, 16, D)
    xo[:, pl.ds(j16, 16)] = new.reshape(8, 16, D)
    yo[:, pl.ds(j16, 16)] = y

    @pl.when(j == 0)
    def _():
        wo[...] = y[:, :REACH]

    @pl.when(j == 2)
    def _():
        eo[...] = y[:, 16 - REACH :]

    if kind == "outer":

        @pl.when(j == 2)
        def _():
            no[...] = yo[:REACH]
            so[...] = yo[8 - REACH :]


def attend(kind, raw, layer, grid_height, band, q, x, wout, gf, ga, extra, cost):
    bands = {"inner": (2, 3), "outer": (0, 5), "between": (1, 4)}[kind]

    def rows(i):
        return pl.BlockSpec((4, W, D), lambda p: (i, 0, 0))

    args = (band, q, q, x, x, wout, gf, ga) + extra
    specs = [pl.BlockSpec(memory_space=pltpu.SMEM)] + [rows(bands[0]), rows(bands[1])] * 2
    specs += [of_layer(a, layer) for a in (wout, gf, ga)]
    specs += [of_layer(a, layer) if a.ndim == 3 and a.shape[0] == LAYERS else whole(a) for a in extra]
    outs = (shape(8, W, D, dtype=F32), shape(8, W, D), shape(8, REACH, D), shape(8, REACH, D))
    scratch = []
    if kind == "inner":
        outs += (shape(H, 64, 2 * D),)
        scratch += [pltpu.VMEM((2, H, 16, D), F32)]
    elif kind == "outer":
        outs += (shape(REACH, W, D), shape(REACH, W, D), shape(4, 64, 2 * D))
        scratch += [pltpu.VMEM((12, 64, D), F32), pltpu.VMEM((12, 64, 2 * D), BF)]
    scratch += [pltpu.VMEM((2, 64, 512), F32)]
    body = functools.partial(attend_kernel, kind, raw, bands, grid_height)
    return call(body, kind, 3, args, specs, outs, tuple(whole(o) for o in outs), scratch, cost)


def feed_kernel(last, *refs):
    (x_in, x_out, x_mid, y_in, y_out, y_mid, n_ref, s_ref, w_ref, e_ref), refs = refs[:10], refs[10:]
    forward_ref, inverse_ref, kernel_ref, expand_ref, shrink_ref, gain_ref = refs[:6]
    outs, (wide, result) = refs[6:-2], refs[-2:]
    step = pl.program_id(0)

    @pl.when(step == 0)
    def _():
        wide[:, 0:8] = jnp.zeros((H + 2 * REACH, 8, D), F32)
        wide[:, 8 + W :] = jnp.zeros((H + 2 * REACH, 8, D), F32)
        wide[:, 8 - REACH : 8] = w_ref[...].astype(F32)
        wide[:, 8 + W : 8 + W + REACH] = e_ref[...].astype(F32)
        first = 0
        for piece in (n_ref, y_out[:4], y_mid[:4], y_in, y_mid[4:], y_out[4:], s_ref):
            wide[first : first + piece.shape[0], 8 : 8 + W] = piece[...].astype(F32)
            first += piece.shape[0]

    j8 = pl.multiple_of(step * PW, 8)
    here = pl.ds(j8, PW)
    ts = []
    for i in range(H // PH):
        x = wide[i * PH : i * PH + LH, pl.ds(j8, SLAB), :].reshape(LH * SLAB, D).astype(BF)
        ts.append(jnp.dot(forward_ref[...], x, preferred_element_type=F32).astype(BF))
    t = jnp.concatenate(ts, 0)
    acc = [x_out[:4, here], x_mid[:4, here], x_in[:, here], x_mid[4:, here], x_out[4:, here]]
    acc = jnp.concatenate(acc, 0).reshape(H * PW, D)
    for n in range(FF // CHUNK):
        c = slice(n * CHUNK, (n + 1) * CHUNK)
        z = jnp.dot(t, expand_ref[:, c], preferred_element_type=F32)
        kr, ki = kernel_ref[:HALF, c], kernel_ref[HALF:, c]
        acts = []
        for i in range(H // PH):
            re, im = z[2 * i * HALF : (2 * i + 1) * HALF], z[(2 * i + 1) * HALF : 2 * (i + 1) * HALF]
            y = jnp.concatenate([(re * kr - im * ki).astype(BF), (re * ki + im * kr).astype(BF)], 0)
            conv = jnp.dot(inverse_ref[...], y, preferred_element_type=F32)
            acts.append(gelu(conv).astype(BF))
        acc = acc + jnp.dot(jnp.concatenate(acts, 0), shrink_ref[c, :], preferred_element_type=F32)
    result[:, here, :] = acc.reshape(H, PW, D)

    @pl.when(step == W // PW - 1)
    def _():
        if last:
            outs[0][...] = result[...].astype(BF)
            return
        out_ref, on_ref, os_ref, ow_ref, oe_ref = outs
        out_ref[...] = result[...]
        for r in range(H // 6):
            y = norm(result[r * 6 : r * 6 + 6].reshape(6 * W, D), gain_ref[...]).astype(BF).reshape(6, W, D)
            if r == 0:
                on_ref[...] = y
            if r == H // 6 - 1:
                os_ref[...] = y
            ow_ref[r * 6 : r * 6 + 6] = y[:, :RADIUS]
            oe_ref[r * 6 : r * 6 + 6] = y[:, W - RADIUS :]


def feed(last, layer, pieces, matrices, kernels, expand, shrink, gain):
    if last:
        outs = (shape(H, W, D),)
    else:
        rows, cols = shape(RADIUS, W, D), shape(H, RADIUS, D)
        outs = (shape(H, W, D, dtype=F32), rows, rows, cols, cols)
    args = (*pieces, *matrices, kernels, expand, shrink, gain)
    specs = [whole(a) for a in (*pieces, *matrices)] + [of_layer(a, layer) for a in (kernels, expand, shrink)]
    return call(
        functools.partial(feed_kernel, last),
        "feed",
        W // PW,
        args,
        specs + [whole(gain)],
        outs,
        tuple(whole(o) for o in outs),
        [pltpu.VMEM((H + 2 * REACH, 64, D), F32), pltpu.VMEM((H, W, D), F32)],
        24,
    )


def per_device(
    sizes,
    state,
    attention_in,
    attention_out,
    expand_weight,
    depth_kernel,
    shrink_weight,
    norm_attention,
    norm_feedforward,
):
    nlat, nlon = sizes
    north = [(i, i + 1) for i in range(nlat - 1)]
    south = [(b, a) for a, b in north]
    east = [(i, (i + 1) % nlon) for i in range(nlon)]
    west = [(b, a) for a, b in east]

    def trade_lat(n, s):
        return lax.ppermute(s, "lat", north), lax.ppermute(n, "lat", south)

    def trade_lon(w, e):
        return lax.ppermute(e, "lon", east), lax.ppermute(w, "lon", west)

    forward, inverse, taps = transforms()
    matrices = (jnp.asarray(forward, BF), jnp.asarray(inverse, BF))
    kernels = jnp.einsum(
        "ft,ltc->lfc",
        jnp.asarray(taps, F32),
        depth_kernel.reshape(LAYERS, -1, FF).astype(F32),
        precision=lax.Precision.HIGHEST,
    )
    band = lax.axis_index("lat").astype(jnp.int32).reshape(1)
    gains_a, gains_f = norm_attention[:, None], norm_feedforward[:, None]
    x = state
    n, s, w, e = state[:RADIUS], state[H - RADIUS :], state[:, :RADIUS], state[:, W - RADIUS :]
    for layer in range(LAYERS):
        raw = layer == 0
        last = layer == LAYERS - 1
        run = functools.partial(attend, raw=raw, layer=layer, grid_height=nlat * H, band=band, wout=attention_out)
        run = functools.partial(run, gf=gains_f, ga=gains_a, x=x)
        w, e = trade_lon(w, e)
        q, kvm = project(layer, x, attention_in, gains_a)
        n = jnp.concatenate([w[:RADIUS], n, e[:RADIUS]], 1)
        s = jnp.concatenate([w[H - RADIUS :], s, e[H - RADIUS :]], 1)
        n, s = trade_lat(n, s)
        x_in, y_in, w_in, e_in, kv = run("inner", q=q, extra=(attention_in, kvm, x, w, e), cost=8)
        x_out, y_out, w_out, e_out, no, so, kvh = run("outer", q=q, extra=(attention_in, kv, n, s), cost=8)
        n, s = trade_lat(no, so)
        x_mid, y_mid, w_mid, e_mid = run("between", q=q, extra=(kv, kvh), cost=8)
        w = jnp.concatenate([n[:, :REACH], w_out[:4], w_mid[:4], w_in, w_mid[4:], w_out[4:], s[:, :REACH]], 0)
        e = jnp.concatenate(
            [n[:, W - REACH :], e_out[:4], e_mid[:4], e_in, e_mid[4:], e_out[4:], s[:, W - REACH :]], 0
        )
        w, e = trade_lon(w, e)
        x, *edges = feed(
            last,
            layer,
            (x_in, x_out, x_mid, y_in, y_out, y_mid, n, s, w, e),
            matrices,
            kernels,
            expand_weight,
            shrink_weight,
            norm_attention[min(layer + 1, LAYERS - 1)][None],
        )
        if not last:
            n, s, w, e = edges
    return x


def solution(mesh):
    in_specs = (P("lat", "lon", None), P(), P(), P(), P(), P(), P(), P())
    sizes = (mesh.shape["lat"], mesh.shape["lon"])
    return jax.shard_map(
        functools.partial(per_device, sizes),
        mesh=mesh,
        in_specs=in_specs,
        out_specs=P("lat", "lon", None),
        check_vma=False,
    )
```

time: 258 us -> 186 us (0.72)
  starting transfers between devices: 96.5 us -> 49 us
  Pallas kernels: 103 us -> 79.7 us
  waiting for transfers between devices: 27.4 us -> 35.7 us
  other arithmetic: 6.48 us -> 0.46 us
  local copies, waits for them, and re-layouts: 20.4 us -> 16.5 us
    ppermute x32 -> x16, starting transfers between devices: 96.5 us -> 49 us  [the longest x8 25.7 us: trade_lon(): return (lax.ppermute(e, 'lon', east), lax.ppermute(w, 'lon', west))]
    pallas_call x4 -> x10, Pallas kernels: 103 us -> 79.7 us  [call(): pl.pallas_call(body, grid=(grid,), in_specs=specs, out_specs=out_specs, o...]
    squeeze x5 -> x0, local copies, waits for them, and re-layouts: 10.4 us -> none  [the longest x1 2.72 us: per_device(): expand_weight[layer]]
    unnamed x90 -> x67, local copies, waits for them, and re-layouts: 3.23 us -> 12.9 us
    ppermute x32 -> x16, waiting for transfers between devices: 27.4 us -> 35.7 us  [the longest x8 20.5 us: trade_lat(): return (lax.ppermute(s, 'lat', north), lax.ppermute(n, 'lat', south))]
    convert_element_type x3 -> x0, other arithmetic: 3.43 us -> none  [the longest x1 1.75 us: per_device(): stream = state.astype(F32)]
    slice x9 -> x6, local copies, waits for them, and re-layouts: 5.37 us -> 2.24 us  [the longest x1 1.12 us: per_device(): state[:, :RADIUS]]
    reduce_sum x4 -> x0, other arithmetic: 3.01 us -> none  [the longest x2 1.62 us: norm(): return c * lax.rsqrt(jnp.mean(c * c, axis=-1, keepdims=True) + 1e-05) * gain]
  transfers between devices with their start and end apart: 32 -> 16, of which waited for: 5 -> 12; matrix products, arithmetic and copies ran while one was open for 7% -> 3% of each run, Pallas kernels for 0% -> 14%
where the time goes in v2:
time: 186 us; the launch traced here: 184 us
  Pallas kernels  79.7 us (43%)
  starting transfers between devices  49 us (26%)
  waiting for transfers between devices  35.7 us (19%)
  local copies, waits for them, and re-layouts  16.5 us (9%)
    pallas_call x10, Pallas kernels, call(): pl.pallas_call(body, grid=(grid,), in_specs=specs, out_specs=out_specs, o...  79.7 us
    ppermute x8, starting transfers between devices, trade_lon(): return (lax.ppermute(e, 'lon', east), lax.ppermute(w, 'lon', west))  25.7 us
    ppermute x8, starting transfers between devices, trade_lat(): return (lax.ppermute(s, 'lat', north), lax.ppermute(n, 'lat', south))  23.3 us
    ppermute x8, waiting for transfers between devices, trade_lat(): return (lax.ppermute(s, 'lat', north), lax.ppermute(n, 'lat', south))  20.5 us
    ppermute x8, waiting for transfers between devices, trade_lon(): return (lax.ppermute(e, 'lon', east), lax.ppermute(w, 'lon', west))  15.3 us
    unnamed x67, local copies, waits for them, and re-layouts  12.9 us
  transfers between devices with their start and end apart: 16, of which 12 were waited for; matrix products, arithmetic and copies ran while one was open for 3% of the time, Pallas kernels for 14%

profile of v2, /device:TPU:0, one launch (start us, length us, event | category | flops | bytes accessed | tf_op | source)
XLA Modules:
  0.0 183.7 jit_solution(16325879877714036514)
XLA Ops:
  1.1 6.3 %collective-permute-start.1 = (bf16[24,6,512]{2,1,0:T(8,128)(2,1)S(1)}, bf16[24,6,512]{2,1,0:T(8,128)(2,1)S(1)}, u32[]{:S(2)}, u32[]{:S(2)}) collective-permute-start(bf16[24,6,512]{2,1,0:T(8,128)(2,1)S(1)} %get-tuple-element.89), channel_id=1, source_target_pairs={{8,0},{16,8},{24,16},{32,24},{40,32},{48,40},{56,48},{64,56},{72,6... | collective-permute-start | bytes 442376 | tf_op jit(solution)/shard_map/ppermute | solution.py:344
  13.0 3.0 %project.2 = (bf16[24,48,512]{2,1,0:T(8,128)(2,1)S(1)}, bf16[24,32,1024]{2,1,0:T(8,128)(2,1)S(1)}) custom-call(bf16[24,48,512]{2,1,0:T(8,128)(2,1)S(1)} %copy-done.1, bf16[2,512,1536]{2,1,0:T(8,128)(2,1)S(1)} %copy-done.3, f32[2,1,512]{2,1,0:T(1,128)S(1)} %broadcast_in_dim.6.gain_ref.refs_6_), custom_call_target="tpu_custom_call" | custom-call | flops 2400000000 | bytes 1000000 | tf_op jit(solution)/shard_map/project/pallas_call | solution.py:71
  16.2 2.6 %collective-permute-start.2 = (bf16[6,60,512]{2,1,0:T(8,128)(2,1)S(1)}, bf16[6,60,512]{2,1,0:T(8,128)(2,1)S(1)}, u32[]{:S(2)}, u32[]{:S(2)}) collective-permute-start(bf16[6,60,512]{2,1,0:T(8,128)(2,1)S(1)} %pad_maximum_fusion), channel_id=1, source_target_pairs={{0,1},{1,2},{2,3},{3,4},{4,5},{5,6},{6,7},{8,9},{9,10},{10,11},{11... | collective-permute-start | bytes 1105928 | tf_op jit(solution)/shard_map/ppermute | solution.py:341
  20.3 5.9 %inner.2 = (f32[8,48,512]{2,1,0:T(8,128)S(1)}, bf16[8,48,512]{2,1,0:T(8,128)(2,1)S(1)}, bf16[8,3,512]{2,1,0:T(4,128)(2,1)S(1)}, bf16[8,3,512]{2,1,0:T(4,128)(2,1)S(1)}, bf16[24,64,1024]{2,1,0:T(8,128)(2,1)S(1)}) custom-call(s32[1]{0:T(128)} %bitcast.band_ref, bf16[24,48,512]{2,1,0:T(8,128)(2,1)S(1)} %get-tuple-element.46.refs_0_.refs_1_, ...), custom_call_target="tpu_custom_call" | custom-call | flops 4800000000 | bytes 1000000 | tf_op jit(solution)/shard_map/inner/pallas_call | solution.py:71
  26.2 6.4 %collective-permute-done.2.refs_9_ = bf16[6,60,512]{2,1,0:T(8,128)(2,1)S(1)} collective-permute-done((bf16[6,60,512]{2,1,0:T(8,128)(2,1)S(1)}, bf16[6,60,512]{2,1,0:T(8,128)(2,1)S(1)}, u32[]{:S(2)}, u32[]{:S(2)}) %collective-permute-start.2) | collective-permute-done | bytes 368672 | tf_op jit(solution)/shard_map/ppermute | solution.py:341
  32.6 6.0 %outer.2 = (f32[8,48,512]{2,1,0:T(8,128)S(1)}, bf16[8,48,512]{2,1,0:T(8,128)(2,1)S(1)}, bf16[8,3,512]{2,1,0:T(4,128)(2,1)S(1)}, bf16[8,3,512]{2,1,0:T(4,128)(2,1...) custom-call(s32[1]{0:T(128)} %bitcast.band_ref, ...), custom_call_target="tpu_custom_call" | custom-call | flops 4800000000 | bytes 1000000 | tf_op jit(solution)/shard_map/outer/pallas_call | solution.py:71
  38.6 4.4 %collective-permute-start.4 = (bf16[3,48,512]{2,1,0:T(8,128)(2,1)S(1)}, bf16[3,48,512]{2,1,0:T(8,128)(2,1)S(1)}, u32[]{:S(2)}, u32[]{:S(2)}) collective-permute-start(bf16[3,48,512]{2,1,0:T(8,128)(2,1)S(1)} %get-tuple-element.56), channel_id=1, source_target_pairs={{0,1},{1,2},{2,3},{3,4},{4,5},{5,6},{6,7},{8,9},{9,10},{10,11},{11... | collective-permute-start | bytes 442376 | tf_op jit(solution)/shard_map/ppermute | solution.py:341
  43.0 4.5 %between.2 = (f32[8,48,512]{2,1,0:T(8,128)S(1)}, bf16[8,48,512]{2,1,0:T(8,128)(2,1)S(1)}, bf16[8,3,512]{2,1,0:T(4,128)(2,1)S(1)}, bf16[8,3,512]{2,1,0:T(4,128)(2,1)S(1)}) custom-call(s32[1]{0:T(128)} %bitcast.band_ref, bf16[24,48,512]{2,1,0:T(8,128)(2,1)S(1)} %get-tuple-element.46.refs_0_.refs_1_, ...), custom_call_target="tpu_custom_call" | custom-call | flops 4800000000 | bytes 1000000 | tf_op jit(solution)/shard_map/between/pallas_call | solution.py:71
  49.1 5.8 %collective-permute-done.5.refs_7_ = bf16[3,48,512]{2,1,0:T(8,128)(2,1)S(1)} collective-permute-done((bf16[3,48,512]{2,1,0:T(8,128)(2,1)S(1)}, bf16[3,48,512]{2,1,0:T(8,128)(2,1)S(1)}, u32[]{:S(2)}, u32[]{:S(2)}) %collective-permute-start.5) | collective-permute-done | bytes 147488 | tf_op jit(solution)/shard_map/ppermute | solution.py:341
  54.9 5.6 %collective-permute-start.7 = (bf16[30,3,512]{2,1,0:T(4,128)(2,1)S(1)}, bf16[30,3,512]{2,1,0:T(4,128)(2,1)S(1)}, u32[]{:S(2)}, u32[]{:S(2)}) collective-permute-start(bf16[30,3,512]{2,1,0:T(4,128)(2,1)S(1)} %get-tuple-element.103), channel_id=1, source_target_pairs={{8,0},{16,8},{24,16},{32,24},{40,32},{48,40},{56,48},{64,56},{72,6... | collective-permute-start | bytes 276488 | tf_op jit(solution)/shard_map/ppermute | solution.py:344
  63.0 5.5 %collective-permute-done.6.refs_8_ = bf16[30,3,512]{2,1,0:T(4,128)(2,1)S(1)} collective-permute-done((bf16[30,3,512]{2,1,0:T(4,128)(2,1)S(1)}, bf16[30,3,512]{2,1,0:T(4,128)(2,1)S(1)}, u32[]{:S(2)}, u32[]{:S(2)}) %collective-permute-start.6) | collective-permute-done | bytes 92192 | tf_op jit(solution)/shard_map/ppermute | solution.py:344
  68.5 21.0 %feed.2 = (f32[24,48,512]{2,1,0:T(8,128)S(1)}, bf16[6,48,512]{2,1,0:T(8,128)(2,1)S(1)}, bf16[6,48,512]{2,1,0:T(8,128)(2,1)S(1)}, bf16[24,6,512]{2,1,0:T(8,128)(2,1)S(1)}, bf16[24,6,512]{2,1,0:T(8,128)(2,1)S(1)}) custom-call(f32[8,48,512]{2,1,0:T(8,128)S(1)} %get-tuple-element.48.refs_0_, f32[8,48,512]{2,1,0:T(8,128)S(1)} %get-tuple-element.50.refs_1_, ...), custom_call_target="tpu_custom_call" | custom-call | flops 14400000000 | bytes 1000000 | tf_op jit(solution)/shard_map/feed/pallas_call | solution.py:71
  89.5 5.3 %collective-permute-start.9 = (bf16[24,6,512]{2,1,0:T(8,128)(2,1)S(1)}, bf16[24,6,512]{2,1,0:T(8,128)(2,1)S(1)}, u32[]{:S(2)}, u32[]{:S(2)}) collective-permute-start(bf16[24,6,512]{2,1,0:T(8,128)(2,1)S(1)} %get-tuple-element.68), channel_id=1, source_target_pairs={{8,0},{16,8},{24,16},{32,24},{40,32},{48,40},{56,48},{64,56},{72,6... | collective-permute-start | bytes 442376 | tf_op jit(solution)/shard_map/ppermute | solution.py:344
  94.9 3.0 %project.3 = (bf16[24,48,512]{2,1,0:T(8,128)(2,1)S(1)}, bf16[24,32,1024]{2,1,0:T(8,128)(2,1)S(1)}) custom-call(f32[24,48,512]{2,1,0:T(8,128)S(1)} %get-tuple-element.64.x_ref.refs_2_.refs_3_.refs_9_, bf16[2,512,1536]{2,1,0:T(8,128)(2,1)S(1)} %copy-done.4, f32[2,1,512]{2,1,0:T(1,128)S(1)} %broadcast_in_dim.6.gain_ref.refs_6_), custom_call_target="tpu_custom_call" | custom-call | flops 2400000000 | bytes 1000000 | tf_op jit(solution)/shard_map/project/pallas_call | solution.py:71
  99.3 2.8 %collective-permute-start.10 = (bf16[6,60,512]{2,1,0:T(8,128)(2,1)S(1)}, bf16[6,60,512]{2,1,0:T(8,128)(2,1)S(1)}, u32[]{:S(2)}, u32[]{:S(2)}) collective-permute-start(bf16[6,60,512]{2,1,0:T(8,128)(2,1)S(1)} %pad_maximum_fusion.2), channel_id=1, source_target_pairs={{0,1},{1,2},{2,3},{3,4},{4,5},{5,6},{6,7},{8,9},{9,10},{10,11},{11... | collective-permute-start | bytes 1105928 | tf_op jit(solution)/shard_map/ppermute | solution.py:341
  103.5 5.6 %inner.3 = (f32[8,48,512]{2,1,0:T(8,128)S(1)}, bf16[8,48,512]{2,1,0:T(8,128)(2,1)S(1)}, bf16[8,3,512]{2,1,0:T(4,128)(2,1)S(1)}, bf16[8,3,512]{2,1,0:T(4,128)(2,1)S(1)}, bf16[24,64,1024]{2,1,0:T(8,128)(2,1)S(1)}) custom-call(s32[1]{0:T(128)} %bitcast.band_ref, bf16[24,48,512]{2,1,0:T(8,128)(2,1)S(1)} %get-tuple-element.65.refs_0_.refs_1_, ...), custom_call_target="tpu_custom_call" | custom-call | flops 4800000000 | bytes 1000000 | tf_op jit(solution)/shard_map/inner/pallas_call | solution.py:71
  113.6 5.4 %outer.3 = (f32[8,48,512]{2,1,0:T(8,128)S(1)}, bf16[8,48,512]{2,1,0:T(8,128)(2,1)S(1)}, bf16[8,3,512]{2,1,0:T(4,128)(2,1)S(1)}, bf16[8,3,512]{2,1,0:T(4,128)(2,1...) custom-call(s32[1]{0:T(128)} %bitcast.band_ref, ...), custom_call_target="tpu_custom_call" | custom-call | flops 4800000000 | bytes 1000000 | tf_op jit(solution)/shard_map/outer/pallas_call | solution.py:71
  119.9 8.4 %collective-permute-start.12 = (bf16[3,48,512]{2,1,0:T(8,128)(2,1)S(1)}, bf16[3,48,512]{2,1,0:T(8,128)(2,1)S(1)}, u32[]{:S(2)}, u32[]{:S(2)}) collective-permute-start(bf16[3,48,512]{2,1,0:T(8,128)(2,1)S(1)} %get-tuple-element.79), channel_id=1, source_target_pairs={{0,1},{1,2},{2,3},{3,4},{4,5},{5,6},{6,7},{8,9},{9,10},{10,11},{11... | collective-permute-start | bytes 442376 | tf_op jit(solution)/shard_map/ppermute | solution.py:341
  131.9 4.5 %between.3 = (f32[8,48,512]{2,1,0:T(8,128)S(1)}, bf16[8,48,512]{2,1,0:T(8,128)(2,1)S(1)}, bf16[8,3,512]{2,1,0:T(4,128)(2,1)S(1)}, bf16[8,3,512]{2,1,0:T(4,128)(2,1)S(1)}) custom-call(s32[1]{0:T(128)} %bitcast.band_ref, bf16[24,48,512]{2,1,0:T(8,128)(2,1)S(1)} %get-tuple-element.65.refs_0_.refs_1_, ...), custom_call_target="tpu_custom_call" | custom-call | flops 4800000000 | bytes 1000000 | tf_op jit(solution)/shard_map/between/pallas_call | solution.py:71
  137.9 5.5 %collective-permute-done.13.refs_7_ = bf16[3,48,512]{2,1,0:T(8,128)(2,1)S(1)} collective-permute-done((bf16[3,48,512]{2,1,0:T(8,128)(2,1)S(1)}, bf16[3,48,512]{2,1,0:T(8,128)(2,1)S(1)}, u32[]{:S(2)}, u32[]{:S(2)}) %collective-permute-start.13) | collective-permute-done | bytes 147488 | tf_op jit(solution)/shard_map/ppermute | solution.py:341
  143.4 8.4 %collective-permute-start.15 = (bf16[30,3,512]{2,1,0:T(4,128)(2,1)S(1)}, bf16[30,3,512]{2,1,0:T(4,128)(2,1)S(1)}, u32[]{:S(2)}, u32[]{:S(2)}) collective-permute-start(bf16[30,3,512]{2,1,0:T(4,128)(2,1)S(1)} %get-tuple-element.99), channel_id=1, source_target_pairs={{8,0},{16,8},{24,16},{32,24},{40,32},{48,40},{56,48},{64,56},{72,6... | collective-permute-start | bytes 276488 | tf_op jit(solution)/shard_map/ppermute | solution.py:344
  151.9 2.4 %collective-permute-done.15.refs_9_ = bf16[30,3,512]{2,1,0:T(4,128)(2,1)S(1)} collective-permute-done((bf16[30,3,512]{2,1,0:T(4,128)(2,1)S(1)}, bf16[30,3,512]{2,1,0:T(4,128)(2,1)S(1)}, u32[]{:S(2)}, u32[]{:S(2)}) %collective-permute-start.15) | collective-permute-done | bytes 92192 | tf_op jit(solution)/shard_map/ppermute | solution.py:344
  154.3 5.5 %collective-permute-done.14.refs_8_ = bf16[30,3,512]{2,1,0:T(4,128)(2,1)S(1)} collective-permute-done((bf16[30,3,512]{2,1,0:T(4,128)(2,1)S(1)}, bf16[30,3,512]{2,1,0:T(4,128)(2,1)S(1)}, u32[]{:S(2)}, u32[]{:S(2)}) %collective-permute-start.14) | collective-permute-done | bytes 92192 | tf_op jit(solution)/shard_map/ppermute | solution.py:344
  163.0 20.8 %feed.3 = bf16[24,48,512]{2,1,0:T(8,128)(2,1)} custom-call(f32[8,48,512]{2,1,0:T(8,128)S(1)} %copy-done.14, f32[8,48,512]{2,1,0:T(8,128)S(1)} %copy-done.16, f32[8,48,512]{2,1,0:T(8,128)S(1)} %get-tuple-element.75.refs_2_, bf16[8,48,512]{2,1,0:T(8,128)(2,1)S(1)} %copy-done.18, bf16[8,48,512]{2,1,0:T(8,128)(2,1)S(1)} %copy-done.20, ...), custom_call_target="tpu_custom_call" | custom-call | flops 14400000000 | bytes 1000000 | tf_op jit(solution)/shard_map/feed/pallas_call | solution.py:71
  (101 shorter events, 28.8 us)
Async XLA Ops:
  0.0 60.5 %copy-start = (bf16[2,7,7,2048]{3,0,2,1:T(2,128)(2,1)S(1)}, bf16[2,7,7,2048]{3,0,2,1:T(2,128)(2,1)}, u32[]{:S(2)}) copy-start(bf16[2,7,7,2048]{3,0,2,1:T(2,128)(2,1)} %param.15) | copy-start | bytes 1204228
  1.1 14.9 %collective-permute-start.1 = (bf16[24,6,512]{2,1,0:T(8,128)(2,1)S(1)}, bf16[24,6,512]{2,1,0:T(8,128)(2,1)S(1)}, u32[]{:S(2)}, u32[]{:S(2)}) collective-permute-start(bf16[24,6,512]{2,1,0:T(8,128)(2,1)S(1)} %get-tuple-element.89), channel_id=1, source_target_pairs={{8,0},{16,8},{24,16},{32,24},{40,32},{48,40},{56,48},{64,56},{72,6... | collective-permute-start | bytes 442376 | tf_op jit(solution)/shard_map/ppermute | solution.py:344
  7.4 8.7 %collective-permute-start = (bf16[24,6,512]{2,1,0:T(8,128)(2,1)S(1)}, bf16[24,6,512]{2,1,0:T(8,128)(2,1)S(1)}, u32[]{:S(2)}, u32[]{:S(2)}) collective-permute-start(bf16[24,6,512]{2,1,0:T(8,128)(2,1)S(1)} %get-tuple-element.90), channel_id=1, source_target_pairs={{0,8},{8,16},{16,24},{24,32},{32,40},{40,48},{48,56},{56,64},{64,7... | collective-permute-start | bytes 442376 | tf_op jit(solution)/shard_map/ppermute | solution.py:344
  16.2 16.4 %collective-permute-start.2 = (bf16[6,60,512]{2,1,0:T(8,128)(2,1)S(1)}, bf16[6,60,512]{2,1,0:T(8,128)(2,1)S(1)}, u32[]{:S(2)}, u32[]{:S(2)}) collective-permute-start(bf16[6,60,512]{2,1,0:T(8,128)(2,1)S(1)} %pad_maximum_fusion), channel_id=1, source_target_pairs={{0,1},{1,2},{2,3},{3,4},{4,5},{5,6},{6,7},{8,9},{9,10},{10,11},{11... | collective-permute-start | bytes 1105928 | tf_op jit(solution)/shard_map/ppermute | solution.py:341
  19.0 13.7 %collective-permute-start.3 = (bf16[6,60,512]{2,1,0:T(8,128)(2,1)S(1)}, bf16[6,60,512]{2,1,0:T(8,128)(2,1)S(1)}, u32[]{:S(2)}, u32[]{:S(2)}) collective-permute-start(bf16[6,60,512]{2,1,0:T(8,128)(2,1)S(1)} %pad_maximum_fusion.1), channel_id=1, source_target_pairs={{1,0},{2,1},{3,2},{4,3},{5,4},{6,5},{7,6},{9,8},{10,9},{11,10},{12... | collective-permute-start | bytes 1105928 | tf_op jit(solution)/shard_map/ppermute | solution.py:341
  38.6 10.3 %collective-permute-start.4 = (bf16[3,48,512]{2,1,0:T(8,128)(2,1)S(1)}, bf16[3,48,512]{2,1,0:T(8,128)(2,1)S(1)}, u32[]{:S(2)}, u32[]{:S(2)}) collective-permute-start(bf16[3,48,512]{2,1,0:T(8,128)(2,1)S(1)} %get-tuple-element.56), channel_id=1, source_target_pairs={{0,1},{1,2},{2,3},{3,4},{4,5},{5,6},{6,7},{8,9},{9,10},{10,11},{11... | collective-permute-start | bytes 442376 | tf_op jit(solution)/shard_map/ppermute | solution.py:341
  43.0 17.5 %copy-start.21 = (f32[256,49,1]{0,1,2:T(8,128)S(1)}, f32[256,49,1]{0,1,2:T(8,128)}, u32[]{:S(2)}) copy-start(f32[256,49,1]{0,1,2:T(8,128)} %constant.13) | copy-start | bytes 150532
  47.6 7.3 %collective-permute-start.5 = (bf16[3,48,512]{2,1,0:T(8,128)(2,1)S(1)}, bf16[3,48,512]{2,1,0:T(8,128)(2,1)S(1)}, u32[]{:S(2)}, u32[]{:S(2)}) collective-permute-start(bf16[3,48,512]{2,1,0:T(8,128)(2,1)S(1)} %get-tuple-element.57), channel_id=1, source_target_pairs={{1,0},{2,1},{3,2},{4,3},{5,4},{6,5},{7,6},{9,8},{10,9},{11,10},{12... | collective-permute-start | bytes 442376 | tf_op jit(solution)/shard_map/ppermute | solution.py:341
  54.9 8.1 %collective-permute-start.7 = (bf16[30,3,512]{2,1,0:T(4,128)(2,1)S(1)}, bf16[30,3,512]{2,1,0:T(4,128)(2,1)S(1)}, u32[]{:S(2)}, u32[]{:S(2)}) collective-permute-start(bf16[30,3,512]{2,1,0:T(4,128)(2,1)S(1)} %get-tuple-element.103), channel_id=1, source_target_pairs={{8,0},{16,8},{24,16},{32,24},{40,32},{48,40},{56,48},{64,56},{72,6... | collective-permute-start | bytes 276488 | tf_op jit(solution)/shard_map/ppermute | solution.py:344
  60.5 7.9 %collective-permute-start.6 = (bf16[30,3,512]{2,1,0:T(4,128)(2,1)S(1)}, bf16[30,3,512]{2,1,0:T(4,128)(2,1)S(1)}, u32[]{:S(2)}, u32[]{:S(2)}) collective-permute-start(bf16[30,3,512]{2,1,0:T(4,128)(2,1)S(1)} %get-tuple-element.104), channel_id=1, source_target_pairs={{0,8},{8,16},{16,24},{24,32},{32,40},{40,48},{48,56},{56,64},{64,7... | collective-permute-start | bytes 276488 | tf_op jit(solution)/shard_map/ppermute | solution.py:344
  68.4 26.4 %copy-start.4 = (bf16[2,512,1536]{2,1,0:T(8,128)(2,1)S(1)}, bf16[2,512,1536]{2,1,0:T(8,128)(2,1)}, u32[]{:S(2)}) copy-start(bf16[2,512,1536]{2,1,0:T(8,128)(2,1)} %refs_7_.7) | copy-start | bytes 9437188
  89.4 14.0 %copy-start.10 = (f32[24,48,512]{2,1,0:T(8,128)}, f32[24,48,512]{2,1,0:T(8,128)S(1)}, u32[]{:S(2)}) copy-start(f32[24,48,512]{2,1,0:T(8,128)S(1)} %get-tuple-element.64.x_ref.refs_2_.refs_3_.refs_9_) | copy-start | bytes 7077892
  89.5 8.8 %collective-permute-start.8 = (bf16[24,6,512]{2,1,0:T(8,128)(2,1)S(1)}, bf16[24,6,512]{2,1,0:T(8,128)(2,1)S(1)}, u32[]{:S(2)}, u32[]{:S(2)}) collective-permute-start(bf16[24,6,512]{2,1,0:T(8,128)(2,1)S(1)} %get-tuple-element.67), channel_id=1, source_target_pairs={{0,8},{8,16},{16,24},{24,32},{32,40},{40,48},{48,56},{56,64},{64,7... | collective-permute-start | bytes 442376 | tf_op jit(solution)/shard_map/ppermute | solution.py:344
  89.5 9.6 %collective-permute-start.9 = (bf16[24,6,512]{2,1,0:T(8,128)(2,1)S(1)}, bf16[24,6,512]{2,1,0:T(8,128)(2,1)S(1)}, u32[]{:S(2)}, u32[]{:S(2)}) collective-permute-start(bf16[24,6,512]{2,1,0:T(8,128)(2,1)S(1)} %get-tuple-element.68), channel_id=1, source_target_pairs={{8,0},{16,8},{24,16},{32,24},{40,32},{48,40},{56,48},{64,56},{72,6... | collective-permute-start | bytes 442376 | tf_op jit(solution)/shard_map/ppermute | solution.py:344
  99.3 11.4 %collective-permute-start.10 = (bf16[6,60,512]{2,1,0:T(8,128)(2,1)S(1)}, bf16[6,60,512]{2,1,0:T(8,128)(2,1)S(1)}, u32[]{:S(2)}, u32[]{:S(2)}) collective-permute-start(bf16[6,60,512]{2,1,0:T(8,128)(2,1)S(1)} %pad_maximum_fusion.2), channel_id=1, source_target_pairs={{0,1},{1,2},{2,3},{3,4},{4,5},{5,6},{6,7},{8,9},{9,10},{10,11},{11... | collective-permute-start | bytes 1105928 | tf_op jit(solution)/shard_map/ppermute | solution.py:341
  102.2 9.8 %collective-permute-start.11 = (bf16[6,60,512]{2,1,0:T(8,128)(2,1)S(1)}, bf16[6,60,512]{2,1,0:T(8,128)(2,1)S(1)}, u32[]{:S(2)}, u32[]{:S(2)}) collective-permute-start(bf16[6,60,512]{2,1,0:T(8,128)(2,1)S(1)} %pad_maximum_fusion.3), channel_id=1, source_target_pairs={{1,0},{2,1},{3,2},{4,3},{5,4},{6,5},{7,6},{9,8},{10,9},{11,10},{12... | collective-permute-start | bytes 1105928 | tf_op jit(solution)/shard_map/ppermute | solution.py:341
  119.9 16.4 %copy-start.19 = (bf16[8,48,512]{2,1,0:T(8,128)(2,1)}, bf16[8,48,512]{2,1,0:T(8,128)(2,1)S(1)}, u32[]{:S(2)}) copy-start(bf16[8,48,512]{2,1,0:T(8,128)(2,1)S(1)} %get-tuple-element.77.refs_4_) | copy-start | bytes 1179652
  119.9 17.8 %collective-permute-start.12 = (bf16[3,48,512]{2,1,0:T(8,128)(2,1)S(1)}, bf16[3,48,512]{2,1,0:T(8,128)(2,1)S(1)}, u32[]{:S(2)}, u32[]{:S(2)}) collective-permute-start(bf16[3,48,512]{2,1,0:T(8,128)(2,1)S(1)} %get-tuple-element.79), channel_id=1, source_target_pairs={{0,1},{1,2},{2,3},{3,4},{4,5},{5,6},{6,7},{8,9},{9,10},{10,11},{11... | collective-permute-start | bytes 442376 | tf_op jit(solution)/shard_map/ppermute | solution.py:341
  131.9 27.9 %copy-start.14 = (f32[8,48,512]{2,1,0:T(8,128)S(1)}, f32[8,48,512]{2,1,0:T(8,128)}, u32[]{:S(2)}) copy-start(f32[8,48,512]{2,1,0:T(8,128)} %copy-done.13) | copy-start | bytes 2359300
  131.9 27.9 %copy-start.16 = (f32[8,48,512]{2,1,0:T(8,128)S(1)}, f32[8,48,512]{2,1,0:T(8,128)}, u32[]{:S(2)}) copy-start(f32[8,48,512]{2,1,0:T(8,128)} %copy-done.15) | copy-start | bytes 2359300
  131.9 27.9 %copy-start.18 = (bf16[8,48,512]{2,1,0:T(8,128)(2,1)S(1)}, bf16[8,48,512]{2,1,0:T(8,128)(2,1)}, u32[]{:S(2)}) copy-start(bf16[8,48,512]{2,1,0:T(8,128)(2,1)} %copy-done.17) | copy-start | bytes 1179652
  136.4 7.0 %collective-permute-start.13 = (bf16[3,48,512]{2,1,0:T(8,128)(2,1)S(1)}, bf16[3,48,512]{2,1,0:T(8,128)(2,1)S(1)}, u32[]{:S(2)}, u32[]{:S(2)}) collective-permute-start(bf16[3,48,512]{2,1,0:T(8,128)(2,1)S(1)} %get-tuple-element.80), channel_id=1, source_target_pairs={{1,0},{2,1},{3,2},{4,3},{5,4},{6,5},{7,6},{9,8},{10,9},{11,10},{12... | collective-permute-start | bytes 442376 | tf_op jit(solution)/shard_map/ppermute | solution.py:341
  143.4 10.8 %collective-permute-start.15 = (bf16[30,3,512]{2,1,0:T(4,128)(2,1)S(1)}, bf16[30,3,512]{2,1,0:T(4,128)(2,1)S(1)}, u32[]{:S(2)}, u32[]{:S(2)}) collective-permute-start(bf16[30,3,512]{2,1,0:T(4,128)(2,1)S(1)} %get-tuple-element.99), channel_id=1, source_target_pairs={{8,0},{16,8},{24,16},{32,24},{40,32},{48,40},{56,48},{64,56},{72,6... | collective-permute-start | bytes 276488 | tf_op jit(solution)/shard_map/ppermute | solution.py:344
  151.8 7.9 %collective-permute-start.14 = (bf16[30,3,512]{2,1,0:T(4,128)(2,1)S(1)}, bf16[30,3,512]{2,1,0:T(4,128)(2,1)S(1)}, u32[]{:S(2)}, u32[]{:S(2)}) collective-permute-start(bf16[30,3,512]{2,1,0:T(4,128)(2,1)S(1)} %get-tuple-element.100), channel_id=1, source_target_pairs={{0,8},{8,16},{16,24},{24,32},{32,40},{40,48},{48,56},{56,64},{64,7... | collective-permute-start | bytes 276488 | tf_op jit(solution)/shard_map/ppermute | solution.py:344
  (15 other events, 72.8 us)

commit v3 on v2

--- a/solution.py
+++ b/solution.py
@@ -19,8 +19,9 @@
 LH, LW = PH + 2 * REACH, PW + 2 * REACH
 SLAB = 24
 HALF = LH * LW // 2 + 2
-CHUNK = 1024
-VMEM = 40 * 2**20
+CHUNK = 256
+PAIR = 2
+PROJECT_VMEM, ATTEND_VMEM, FEED_VMEM = 12, 16, 20
 
 
 def transforms():
@@ -67,7 +68,7 @@
     return jax.ShapeDtypeStruct(dims, dtype)
 
 
-def call(body, name, grid, args, specs, outs, out_specs, scratch, cost):
+def call(body, name, limit, grid, args, specs, outs, out_specs, scratch, cost):
     return pl.pallas_call(
         body,
         grid=(grid,),
@@ -75,16 +76,16 @@
         out_specs=out_specs,
         out_shape=outs,
         scratch_shapes=scratch,
-        compiler_params=pltpu.CompilerParams(vmem_limit_bytes=VMEM),
+        compiler_params=pltpu.CompilerParams(vmem_limit_bytes=limit * 2**20),
         cost_estimate=pl.CostEstimate(flops=int(cost * 6e8), bytes_accessed=10**6, transcendentals=0),
         name=name,
     )(*args)
 
 
-def project_kernel(x_ref, win_ref, gain_ref, q_ref, kv_ref):
-    y = norm(x_ref[...].astype(F32).reshape(6 * W, D), gain_ref[...])
+def project_kernel(layer, x_ref, win_ref, gain_ref, q_ref, kv_ref):
+    y = norm(x_ref[...].astype(F32).reshape(6 * W, D), gain_ref[layer : layer + 1])
     q = jnp.dot(y.astype(BF), win_ref[:, :D], preferred_element_type=F32)
-    q_ref[...] = (q * 0.125).astype(BF).reshape(6, W, D)
+    q_ref[...] = (q * np.float32(0.125 / math.log(2))).astype(BF).reshape(6, W, D)
     y = y.reshape(6, W, D)[:, 8:40].reshape(6 * 32, D).astype(BF)
     kv_ref[...] = jnp.dot(y, win_ref[:, D:], preferred_element_type=F32).astype(BF).reshape(6, 32, 2 * D)
 
@@ -94,11 +95,12 @@
         return pl.BlockSpec((6, width, depth), lambda p: (p, 0, 0))
 
     return call(
-        project_kernel,
+        functools.partial(project_kernel, layer),
         "project",
+        PROJECT_VMEM,
         H // 6,
         (x, win, gains),
-        [rows(W, D), of_layer(win, layer), of_layer(gains, layer)],
+        [rows(W, D), of_layer(win, layer), whole(gains)],
         (shape(H, W, D), shape(H, 32, 2 * D)),
         (rows(W, D), rows(32, 2 * D)),
         [],
@@ -124,7 +126,7 @@
         qbd = jnp.concatenate([jnp.where(head == h, qg, jnp.zeros_like(qg)) for h in range(4)], 0)
         s = lax.dot_general(qbd, k, (((1,), (1,)), ((), ())), preferred_element_type=F32)
         s = (s.reshape(4, 64, 512) + mask[None]).reshape(256, 512)
-        p = jnp.exp(s - jnp.max(s, axis=1, keepdims=True))
+        p = jnp.exp2(s - jnp.max(s, axis=1, keepdims=True))
         total = jnp.sum(p, axis=1, keepdims=True)
         o = jnp.dot(p.astype(BF), v, preferred_element_type=F32) * (1.0 / total)
         r = o[192:]
@@ -134,14 +136,14 @@
     return jnp.concatenate(outs, 1)
 
 
-def attend_kernel(kind, raw, bands, grid_height, band_ref, *refs):
+def attend_kernel(kind, layer, raw, bands, grid_height, band_ref, *refs):
     (q0, q1, x0, x1, wout_ref, gf_ref), refs = refs[:6], refs[6:]
     j = pl.program_id(0)
-    gain = refs[0]
+    gain_a, gain_f = refs[0][layer : layer + 1], gf_ref[layer : layer + 1]
 
     def incoming(piece):
         piece = piece[...].astype(F32)
-        return norm(piece, gain[...]) if raw else piece
+        return norm(piece, gain_a) if raw else piece
 
     @pl.when(j == 0)
     def _():
@@ -158,8 +160,8 @@
             edge = jnp.zeros((H, 2, D), F32)
             wide[0, :, 0:2] = edge
             wide[0, :, 2:8] = incoming(w)
-            wide[0, :, 8:16] = norm(x[:, 0:16].astype(F32)[:, :8], ga[...])
-            wide[1, :, 0:8] = norm(x[:, 32:48].astype(F32)[:, 8:], ga[...])
+            wide[0, :, 8:16] = norm(x[:, 0:16].astype(F32)[:, :8], gain_a)
+            wide[1, :, 0:8] = norm(x[:, 32:48].astype(F32)[:, 8:], gain_a)
             wide[1, :, 8:14] = incoming(e)
             wide[1, :, 14:16] = edge
             for side in range(2):
@@ -200,7 +202,7 @@
         old.append((x0, x1)[t][:, pl.ds(j16, 16)].reshape(64, D).astype(F32))
     new = jnp.dot(jnp.concatenate(mixed, 0), wout_ref[...], preferred_element_type=F32)
     new = new + jnp.concatenate(old, 0)
-    y = norm(new, gf_ref[...]).astype(BF).reshape(8, 16, D)
+    y = norm(new, gain_f).astype(BF).reshape(8, 16, D)
     xo[:, pl.ds(j16, 16)] = new.reshape(8, 16, D)
     yo[:, pl.ds(j16, 16)] = y
 
@@ -228,7 +230,7 @@
 
     args = (band, q, q, x, x, wout, gf, ga) + extra
     specs = [pl.BlockSpec(memory_space=pltpu.SMEM)] + [rows(bands[0]), rows(bands[1])] * 2
-    specs += [of_layer(a, layer) for a in (wout, gf, ga)]
+    specs += [of_layer(wout, layer), whole(gf), whole(ga)]
     specs += [of_layer(a, layer) if a.ndim == 3 and a.shape[0] == LAYERS else whole(a) for a in extra]
     outs = (shape(8, W, D, dtype=F32), shape(8, W, D), shape(8, REACH, D), shape(8, REACH, D))
     scratch = []
@@ -239,14 +241,14 @@
         outs += (shape(REACH, W, D), shape(REACH, W, D), shape(4, 64, 2 * D))
         scratch += [pltpu.VMEM((12, 64, D), F32), pltpu.VMEM((12, 64, 2 * D), BF)]
     scratch += [pltpu.VMEM((2, 64, 512), F32)]
-    body = functools.partial(attend_kernel, kind, raw, bands, grid_height)
-    return call(body, kind, 3, args, specs, outs, tuple(whole(o) for o in outs), scratch, cost)
-
-
-def feed_kernel(last, *refs):
+    body = functools.partial(attend_kernel, kind, layer, raw, bands, grid_height)
+    return call(body, kind, ATTEND_VMEM, 3, args, specs, outs, tuple(whole(o) for o in outs), scratch, cost)
+
+
+def feed_kernel(layer, last, *refs):
     (x_in, x_out, x_mid, y_in, y_out, y_mid, n_ref, s_ref, w_ref, e_ref), refs = refs[:10], refs[10:]
     forward_ref, inverse_ref, kernel_ref, expand_ref, shrink_ref, gain_ref = refs[:6]
-    outs, (wide, result) = refs[6:-2], refs[-2:]
+    outs, (wide, result, spectra) = refs[6:-3], refs[-3:]
     step = pl.program_id(0)
 
     @pl.when(step == 0)
@@ -260,29 +262,49 @@
             wide[first : first + piece.shape[0], 8 : 8 + W] = piece[...].astype(F32)
             first += piece.shape[0]
 
-    j8 = pl.multiple_of(step * PW, 8)
-    here = pl.ds(j8, PW)
-    ts = []
-    for i in range(H // PH):
-        x = wide[i * PH : i * PH + LH, pl.ds(j8, SLAB), :].reshape(LH * SLAB, D).astype(BF)
-        ts.append(jnp.dot(forward_ref[...], x, preferred_element_type=F32).astype(BF))
-    t = jnp.concatenate(ts, 0)
-    acc = [x_out[:4, here], x_mid[:4, here], x_in[:, here], x_mid[4:, here], x_out[4:, here]]
-    acc = jnp.concatenate(acc, 0).reshape(H * PW, D)
-    for n in range(FF // CHUNK):
+    here = pl.ds(pl.multiple_of(step * PAIR * PW, PAIR * PW), PAIR * PW)
+    count = PAIR * H // PH
+    for c in range(PAIR):
+        slab = pl.ds(pl.multiple_of((step * PAIR + c) * PW, PW), SLAB)
+        for i in range(H // PH):
+            x = wide[i * PH : i * PH + LH, slab, :].reshape(LH * SLAB, D).astype(BF)
+            first = (c * (H // PH) + i) * 2 * HALF
+            t = jnp.dot(forward_ref[...], x, preferred_element_type=F32).astype(BF)
+            spectra[first : first + 2 * HALF] = t
+    t = spectra[...]
+
+    def expanded(n):
+        return jnp.dot(t, expand_ref[:, n * CHUNK : (n + 1) * CHUNK], preferred_element_type=F32)
+
+    def activated(n, z):
         c = slice(n * CHUNK, (n + 1) * CHUNK)
-        z = jnp.dot(t, expand_ref[:, c], preferred_element_type=F32)
         kr, ki = kernel_ref[:HALF, c], kernel_ref[HALF:, c]
         acts = []
-        for i in range(H // PH):
+        for i in range(count):
             re, im = z[2 * i * HALF : (2 * i + 1) * HALF], z[(2 * i + 1) * HALF : 2 * (i + 1) * HALF]
             y = jnp.concatenate([(re * kr - im * ki).astype(BF), (re * ki + im * kr).astype(BF)], 0)
-            conv = jnp.dot(inverse_ref[...], y, preferred_element_type=F32)
-            acts.append(gelu(conv).astype(BF))
-        acc = acc + jnp.dot(jnp.concatenate(acts, 0), shrink_ref[c, :], preferred_element_type=F32)
-    result[:, here, :] = acc.reshape(H, PW, D)
-
-    @pl.when(step == W // PW - 1)
+            acts.append(gelu(jnp.dot(inverse_ref[...], y, preferred_element_type=F32)).astype(BF))
+        return jnp.concatenate(acts, 0)
+
+    def shrunk(n, act):
+        return jnp.dot(act, shrink_ref[n * CHUNK : (n + 1) * CHUNK], preferred_element_type=F32)
+
+    acc = jnp.zeros((PAIR * H * PW, D), F32)
+    z, act = expanded(0), None
+    for n in range(FF // CHUNK):
+        ahead = expanded(n + 1) if n + 1 < FF // CHUNK else None
+        if act is not None:
+            acc = acc + shrunk(n - 1, act)
+        act, z = activated(n, z), ahead
+    acc = acc + shrunk(FF // CHUNK - 1, act)
+    old = [x_out[:4, here], x_mid[:4, here], x_in[:, here], x_mid[4:, here], x_out[4:, here]]
+    old = jnp.concatenate(old, 0)
+    size = H * PW
+    for c in range(PAIR):
+        new = acc[c * size : (c + 1) * size].reshape(H, PW, D) + old[:, c * PW : (c + 1) * PW]
+        result[:, pl.ds(pl.multiple_of((step * PAIR + c) * PW, PW), PW), :] = new
+
+    @pl.when(step == W // PW // PAIR - 1)
     def _():
         if last:
             outs[0][...] = result[...].astype(BF)
@@ -290,7 +312,7 @@
         out_ref, on_ref, os_ref, ow_ref, oe_ref = outs
         out_ref[...] = result[...]
         for r in range(H // 6):
-            y = norm(result[r * 6 : r * 6 + 6].reshape(6 * W, D), gain_ref[...]).astype(BF).reshape(6, W, D)
+            y = norm(result[r * 6 : r * 6 + 6].reshape(6 * W, D), gain_ref[layer + 1 : layer + 2]).astype(BF).reshape(6, W, D)
             if r == 0:
                 on_ref[...] = y
             if r == H // 6 - 1:
@@ -308,14 +330,19 @@
     args = (*pieces, *matrices, kernels, expand, shrink, gain)
     specs = [whole(a) for a in (*pieces, *matrices)] + [of_layer(a, layer) for a in (kernels, expand, shrink)]
     return call(
-        functools.partial(feed_kernel, last),
+        functools.partial(feed_kernel, layer, last),
         "feed",
-        W // PW,
+        FEED_VMEM,
+        W // PW // PAIR,
         args,
         specs + [whole(gain)],
         outs,
         tuple(whole(o) for o in outs),
-        [pltpu.VMEM((H + 2 * REACH, 64, D), F32), pltpu.VMEM((H, W, D), F32)],
+        [
+            pltpu.VMEM((H + 2 * REACH, 64, D), F32),
+            pltpu.VMEM((H, W, D), F32),
+            pltpu.VMEM((PAIR * H // PH * 2 * HALF, D), BF),
+        ],
         24,
     )
 
@@ -352,7 +379,7 @@
         precision=lax.Precision.HIGHEST,
     )
     band = lax.axis_index("lat").astype(jnp.int32).reshape(1)
-    gains_a, gains_f = norm_attention[:, None], norm_feedforward[:, None]
+    gains_a, gains_f = norm_attention, norm_feedforward
     x = state
     n, s, w, e = state[:RADIUS], state[H - RADIUS :], state[:, :RADIUS], state[:, W - RADIUS :]
     for layer in range(LAYERS):
@@ -369,6 +396,7 @@
         x_out, y_out, w_out, e_out, no, so, kvh = run("outer", q=q, extra=(attention_in, kv, n, s), cost=8)
         n, s = trade_lat(no, so)
         x_mid, y_mid, w_mid, e_mid = run("between", q=q, extra=(kv, kvh), cost=8)
+        n, s, w_out, e_out, w_mid, e_mid = lax.optimization_barrier((n, s, w_out, e_out, w_mid, e_mid))
         w = jnp.concatenate([n[:, :REACH], w_out[:4], w_mid[:4], w_in, w_mid[4:], w_out[4:], s[:, :REACH]], 0)
         e = jnp.concatenate(
             [n[:, W - REACH :], e_out[:4], e_mid[:4], e_in, e_mid[4:], e_out[4:], s[:, W - REACH :]], 0
@@ -382,7 +410,7 @@
             kernels,
             expand_weight,
             shrink_weight,
-            norm_attention[min(layer + 1, LAYERS - 1)][None],
+            gains_a,
         )
         if not last:
             n, s, w, e = edges

time: 186 us -> 152 us (0.82)
  local copies, waits for them, and re-layouts: 16.5 us -> 6.52 us
  Pallas kernels: 79.7 us -> 70.2 us
  starting transfers between devices: 49 us -> 40.6 us
  waiting for transfers between devices: 35.7 us -> 30.3 us
    pallas_call x10, Pallas kernels: 79.7 us -> 70.2 us  [call(): pl.pallas_call(body, grid=(grid,), in_specs=specs, out_specs=out_specs, o...]
    unnamed x67 -> x49, local copies, waits for them, and re-layouts: 12.9 us -> 4.24 us
    ppermute x8, waiting for transfers between devices: 20.5 us -> 14.4 us  [trade_lat(): return (lax.ppermute(s, 'lat', north), lax.ppermute(n, 'lat', south))]
    ppermute x8, starting transfers between devices: 25.7 us -> 20.3 us  [trade_lon(): return (lax.ppermute(e, 'lon', east), lax.ppermute(w, 'lon', west))]
    ppermute x8, starting transfers between devices: 23.3 us -> 20.2 us  [trade_lat(): return (lax.ppermute(s, 'lat', north), lax.ppermute(n, 'lat', south))]
  transfers between devices with their start and end apart: 16 -> 16, of which waited for: 12 -> 12; matrix products, arithmetic and copies ran while one was open for 3% -> 2% of each run, Pallas kernels for 14% -> 18%
where the time goes in v3:
time: 152 us; the launch traced here: 150 us
  Pallas kernels  70.2 us (46%)
  starting transfers between devices  40.6 us (27%)
  waiting for transfers between devices  30.3 us (20%)
  local copies, waits for them, and re-layouts  6.52 us (4%)
  matrix products  1.85 us (1%)
    pallas_call x10, Pallas kernels, call(): pl.pallas_call(body, grid=(grid,), in_specs=specs, out_specs=out_specs, o...  70.2 us
    ppermute x8, starting transfers between devices, trade_lon(): return (lax.ppermute(e, 'lon', east), lax.ppermute(w, 'lon', west))  20.3 us
    ppermute x8, starting transfers between devices, trade_lat(): return (lax.ppermute(s, 'lat', north), lax.ppermute(n, 'lat', south))  20.2 us
    ppermute x8, waiting for transfers between devices, trade_lon(): return (lax.ppermute(e, 'lon', east), lax.ppermute(w, 'lon', west))  15.9 us
    ppermute x8, waiting for transfers between devices, trade_lat(): return (lax.ppermute(s, 'lat', north), lax.ppermute(n, 'lat', south))  14.4 us
    unnamed x49, local copies, waits for them, and re-layouts  4.24 us
  transfers between devices with their start and end apart: 16, of which 12 were waited for; matrix products, arithmetic and copies ran while one was open for 2% of the time, Pallas kernels for 18%

profile of v3, /device:TPU:0, one launch (start us, length us, event | category | flops | bytes accessed | tf_op | source)
XLA Modules:
  0.0 150.3 jit_solution(8809901636169342833)
XLA Ops:
  1.1 6.3 %collective-permute-start.1 = (bf16[24,6,512]{2,1,0:T(8,128)(2,1)S(1)}, bf16[24,6,512]{2,1,0:T(8,128)(2,1)S(1)}, u32[]{:S(2)}, u32[]{:S(2)}) collective-permute-start(bf16[24,6,512]{2,1,0:T(8,128)(2,1)S(1)} %get-tuple-element.113), channel_id=1, source_target_pairs={{8,0},{16,8},{24,16},{32,24},{40,32},{48,40},{56,48},{64,56},{72,6... | collective-permute-start | bytes 442376 | tf_op jit(solution)/shard_map/ppermute | solution.py:371
  12.4 3.0 %project.2 = (bf16[24,48,512]{2,1,0:T(8,128)(2,1)S(1)}, bf16[24,32,1024]{2,1,0:T(8,128)(2,1)S(1)}) custom-call(bf16[24,48,512]{2,1,0:T(8,128)(2,1)S(1)} %copy-done.1, bf16[2,512,1536]{2,1,0:T(8,128)(2,1)S(1)} %copy-done.5, f32[2,512]{1,0:T(2,128)S(1)} %copy-done.9), custom_call_target="tpu_custom_call" | custom-call | flops 2400000000 | bytes 1000000 | tf_op jit(solution)/shard_map/project/pallas_call | solution.py:72
  16.2 2.6 %collective-permute-start.2 = (bf16[6,60,512]{2,1,0:T(8,128)(2,1)S(1)}, bf16[6,60,512]{2,1,0:T(8,128)(2,1)S(1)}, u32[]{:S(2)}, u32[]{:S(2)}) collective-permute-start(bf16[6,60,512]{2,1,0:T(8,128)(2,1)S(1)} %pad_maximum_fusion), channel_id=1, source_target_pairs={{0,1},{1,2},{2,3},{3,4},{4,5},{5,6},{6,7},{8,9},{9,10},{10,11},{11... | collective-permute-start | bytes 1105928 | tf_op jit(solution)/shard_map/ppermute | solution.py:368
  20.3 5.9 %inner.2 = (f32[8,48,512]{2,1,0:T(8,128)S(1)}, bf16[8,48,512]{2,1,0:T(8,128)(2,1)S(1)}, bf16[8,3,512]{2,1,0:T(4,128)(2,1)S(1)}, bf16[8,3,512]{2,1,0:T(4,128)(2,1)S(1)}, bf16[24,64,1024]{2,1,0:T(8,128)(2,1)S(1)}) custom-call(s32[1]{0:T(128)} %bitcast.band_ref, bf16[24,48,512]{2,1,0:T(8,128)(2,1)S(1)} %get-tuple-element.58.refs_0_.refs_1_, ...), custom_call_target="tpu_custom_call" | custom-call | flops 4800000000 | bytes 1000000 | tf_op jit(solution)/shard_map/inner/pallas_call | solution.py:72
  26.2 5.7 %collective-permute-done.2.refs_9_ = bf16[6,60,512]{2,1,0:T(8,128)(2,1)S(1)} collective-permute-done((bf16[6,60,512]{2,1,0:T(8,128)(2,1)S(1)}, bf16[6,60,512]{2,1,0:T(8,128)(2,1)S(1)}, u32[]{:S(2)}, u32[]{:S(2)}) %collective-permute-start.2) | collective-permute-done | bytes 368672 | tf_op jit(solution)/shard_map/ppermute | solution.py:368
  32.0 5.9 %outer.2 = (f32[8,48,512]{2,1,0:T(8,128)S(1)}, bf16[8,48,512]{2,1,0:T(8,128)(2,1)S(1)}, bf16[8,3,512]{2,1,0:T(4,128)(2,1)S(1)}, bf16[8,3,512]{2,1,0:T(4,128)(2,1...) custom-call(s32[1]{0:T(128)} %bitcast.band_ref, ...), custom_call_target="tpu_custom_call" | custom-call | flops 4800000000 | bytes 1000000 | tf_op jit(solution)/shard_map/outer/pallas_call | solution.py:72
  37.8 4.4 %collective-permute-start.4 = (bf16[3,48,512]{2,1,0:T(8,128)(2,1)S(1)}, bf16[3,48,512]{2,1,0:T(8,128)(2,1)S(1)}, u32[]{:S(2)}, u32[]{:S(2)}) collective-permute-start(bf16[3,48,512]{2,1,0:T(8,128)(2,1)S(1)} %get-tuple-element.68), channel_id=1, source_target_pairs={{0,1},{1,2},{2,3},{3,4},{4,5},{5,6},{6,7},{8,9},{9,10},{10,11},{11... | collective-permute-start | bytes 442376 | tf_op jit(solution)/shard_map/ppermute | solution.py:368
  43.6 4.4 %between.2 = (f32[8,48,512]{2,1,0:T(8,128)S(1)}, bf16[8,48,512]{2,1,0:T(8,128)(2,1)S(1)}, bf16[8,3,512]{2,1,0:T(4,128)(2,1)S(1)}, bf16[8,3,512]{2,1,0:T(4,128)(2,1)S(1)}) custom-call(s32[1]{0:T(128)} %bitcast.band_ref, bf16[24,48,512]{2,1,0:T(8,128)(2,1)S(1)} %get-tuple-element.58.refs_0_.refs_1_, ...), custom_call_target="tpu_custom_call" | custom-call | flops 4800000000 | bytes 1000000 | tf_op jit(solution)/shard_map/between/pallas_call | solution.py:72
  49.8 5.6 %collective-permute-start.7 = (bf16[30,3,512]{2,1,0:T(4,128)(2,1)S(1)}, bf16[30,3,512]{2,1,0:T(4,128)(2,1)S(1)}, u32[]{:S(2)}, u32[]{:S(2)}) collective-permute-start(bf16[30,3,512]{2,1,0:T(4,128)(2,1)S(1)} %get-tuple-element.127), channel_id=1, source_target_pairs={{8,0},{16,8},{24,16},{32,24},{40,32},{48,40},{56,48},{64,56},{72,6... | collective-permute-start | bytes 276488 | tf_op jit(solution)/shard_map/ppermute | solution.py:371
  57.8 5.5 %collective-permute-done.6.refs_8_ = bf16[30,3,512]{2,1,0:T(4,128)(2,1)S(1)} collective-permute-done((bf16[30,3,512]{2,1,0:T(4,128)(2,1)S(1)}, bf16[30,3,512]{2,1,0:T(4,128)(2,1)S(1)}, u32[]{:S(2)}, u32[]{:S(2)}) %collective-permute-start.6) | collective-permute-done | bytes 92192 | tf_op jit(solution)/shard_map/ppermute | solution.py:371
  63.3 16.0 %feed.2 = (f32[24,48,512]{2,1,0:T(8,128)S(1)}, bf16[6,48,512]{2,1,0:T(8,128)(2,1)S(1)}, bf16[6,48,512]{2,1,0:T(8,128)(2,1)S(1)}, bf16[24,6,512]{2,1,0:T(8,128)(2,1)S(1)}, bf16[24,6,512]{2,1,0:T(8,128)(2,1)S(1)}) custom-call(f32[8,48,512]{2,1,0:T(8,128)S(1)} %get-tuple-element.60.refs_0_, f32[8,48,512]{2,1,0:T(8,128)S(1)} %get-tuple-element.62.refs_1_, ...), custom_call_target="tpu_custom_call" | custom-call | flops 14400000000 | bytes 1000000 | tf_op jit(solution)/shard_map/feed/pallas_call | solution.py:72
  79.4 5.3 %collective-permute-start.9 = (bf16[24,6,512]{2,1,0:T(8,128)(2,1)S(1)}, bf16[24,6,512]{2,1,0:T(8,128)(2,1)S(1)}, u32[]{:S(2)}, u32[]{:S(2)}) collective-permute-start(bf16[24,6,512]{2,1,0:T(8,128)(2,1)S(1)} %get-tuple-element.86), channel_id=1, source_target_pairs={{8,0},{16,8},{24,16},{32,24},{40,32},{48,40},{56,48},{64,56},{72,6... | collective-permute-start | bytes 442376 | tf_op jit(solution)/shard_map/ppermute | solution.py:371
  84.7 3.0 %project.3 = (bf16[24,48,512]{2,1,0:T(8,128)(2,1)S(1)}, bf16[24,32,1024]{2,1,0:T(8,128)(2,1)S(1)}) custom-call(f32[24,48,512]{2,1,0:T(8,128)S(1)} %get-tuple-element.82.x_ref.refs_2_.refs_3_.refs_9_, bf16[2,512,1536]{2,1,0:T(8,128)(2,1)S(1)} %copy-done.6, f32[2,512]{1,0:T(2,128)S(1)} %copy-done.10), custom_call_target="tpu_custom_call" | custom-call | flops 2400000000 | bytes 1000000 | tf_op jit(solution)/shard_map/project/pallas_call | solution.py:72
  89.1 2.8 %collective-permute-start.10 = (bf16[6,60,512]{2,1,0:T(8,128)(2,1)S(1)}, bf16[6,60,512]{2,1,0:T(8,128)(2,1)S(1)}, u32[]{:S(2)}, u32[]{:S(2)}) collective-permute-start(bf16[6,60,512]{2,1,0:T(8,128)(2,1)S(1)} %pad_maximum_fusion.2), channel_id=1, source_target_pairs={{0,1},{1,2},{2,3},{3,4},{4,5},{5,6},{6,7},{8,9},{9,10},{10,11},{11... | collective-permute-start | bytes 1105928 | tf_op jit(solution)/shard_map/ppermute | solution.py:368
  93.5 5.7 %inner.3 = (f32[8,48,512]{2,1,0:T(8,128)S(1)}, bf16[8,48,512]{2,1,0:T(8,128)(2,1)S(1)}, bf16[8,3,512]{2,1,0:T(4,128)(2,1)S(1)}, bf16[8,3,512]{2,1,0:T(4,128)(2,1)S(1)}, bf16[24,64,1024]{2,1,0:T(8,128)(2,1)S(1)}) custom-call(s32[1]{0:T(128)} %bitcast.band_ref, bf16[24,48,512]{2,1,0:T(8,128)(2,1)S(1)} %get-tuple-element.83.refs_0_.refs_1_, ...), custom_call_target="tpu_custom_call" | custom-call | flops 4800000000 | bytes 1000000 | tf_op jit(solution)/shard_map/inner/pallas_call | solution.py:72
  99.3 1.9 %collective-permute-done.10.refs_9_ = bf16[6,60,512]{2,1,0:T(8,128)(2,1)S(1)} collective-permute-done((bf16[6,60,512]{2,1,0:T(8,128)(2,1)S(1)}, bf16[6,60,512]{2,1,0:T(8,128)(2,1)S(1)}, u32[]{:S(2)}, u32[]{:S(2)}) %collective-permute-start.10) | collective-permute-done | bytes 368672 | tf_op jit(solution)/shard_map/ppermute | solution.py:368
  101.2 3.5 %collective-permute-done.11.refs_10_ = bf16[6,60,512]{2,1,0:T(8,128)(2,1)S(1)} collective-permute-done((bf16[6,60,512]{2,1,0:T(8,128)(2,1)S(1)}, bf16[6,60,512]{2,1,0:T(8,128)(2,1)S(1)}, u32[]{:S(2)}, u32[]{:S(2)}) %collective-permute-start.11) | collective-permute-done | bytes 368672 | tf_op jit(solution)/shard_map/ppermute | solution.py:368
  104.7 5.4 %outer.3 = (f32[8,48,512]{2,1,0:T(8,128)S(1)}, bf16[8,48,512]{2,1,0:T(8,128)(2,1)S(1)}, bf16[8,3,512]{2,1,0:T(4,128)(2,1)S(1)}, bf16[8,3,512]{2,1,0:T(4,128)(2,1...) custom-call(s32[1]{0:T(128)} %bitcast.band_ref, ...), custom_call_target="tpu_custom_call" | custom-call | flops 4800000000 | bytes 1000000 | tf_op jit(solution)/shard_map/outer/pallas_call | solution.py:72
  110.1 5.1 %collective-permute-start.12 = (bf16[3,48,512]{2,1,0:T(8,128)(2,1)S(1)}, bf16[3,48,512]{2,1,0:T(8,128)(2,1)S(1)}, u32[]{:S(2)}, u32[]{:S(2)}) collective-permute-start(bf16[3,48,512]{2,1,0:T(8,128)(2,1)S(1)} %get-tuple-element.97), channel_id=1, source_target_pairs={{0,1},{1,2},{2,3},{3,4},{4,5},{5,6},{6,7},{8,9},{9,10},{10,11},{11... | collective-permute-start | bytes 442376 | tf_op jit(solution)/shard_map/ppermute | solution.py:368
  116.5 4.4 %between.3 = (f32[8,48,512]{2,1,0:T(8,128)S(1)}, bf16[8,48,512]{2,1,0:T(8,128)(2,1)S(1)}, bf16[8,3,512]{2,1,0:T(4,128)(2,1)S(1)}, bf16[8,3,512]{2,1,0:T(4,128)(2,1)S(1)}) custom-call(s32[1]{0:T(128)} %bitcast.band_ref, bf16[24,48,512]{2,1,0:T(8,128)(2,1)S(1)} %get-tuple-element.83.refs_0_.refs_1_, ...), custom_call_target="tpu_custom_call" | custom-call | flops 4800000000 | bytes 1000000 | tf_op jit(solution)/shard_map/between/pallas_call | solution.py:72
  122.9 3.1 %collective-permute-start.15 = (bf16[30,3,512]{2,1,0:T(4,128)(2,1)S(1)}, bf16[30,3,512]{2,1,0:T(4,128)(2,1)S(1)}, u32[]{:S(2)}, u32[]{:S(2)}) collective-permute-start(bf16[30,3,512]{2,1,0:T(4,128)(2,1)S(1)} %get-tuple-element.123), channel_id=1, source_target_pairs={{8,0},{16,8},{24,16},{32,24},{40,32},{48,40},{56,48},{64,56},{72,6... | collective-permute-start | bytes 276488 | tf_op jit(solution)/shard_map/ppermute | solution.py:371
  126.0 2.4 %collective-permute-done.15.refs_9_ = bf16[30,3,512]{2,1,0:T(4,128)(2,1)S(1)} collective-permute-done((bf16[30,3,512]{2,1,0:T(4,128)(2,1)S(1)}, bf16[30,3,512]{2,1,0:T(4,128)(2,1)S(1)}, u32[]{:S(2)}, u32[]{:S(2)}) %collective-permute-start.15) | collective-permute-done | bytes 92192 | tf_op jit(solution)/shard_map/ppermute | solution.py:371
  128.4 5.5 %collective-permute-done.14.refs_8_ = bf16[30,3,512]{2,1,0:T(4,128)(2,1)S(1)} collective-permute-done((bf16[30,3,512]{2,1,0:T(4,128)(2,1)S(1)}, bf16[30,3,512]{2,1,0:T(4,128)(2,1)S(1)}, u32[]{:S(2)}, u32[]{:S(2)}) %collective-permute-start.14) | collective-permute-done | bytes 92192 | tf_op jit(solution)/shard_map/ppermute | solution.py:371
  133.9 16.5 %feed.3 = bf16[24,48,512]{2,1,0:T(8,128)(2,1)} custom-call(f32[8,48,512]{2,1,0:T(8,128)S(1)} %get-tuple-element.87.refs_0_, f32[8,48,512]{2,1,0:T(8,128)S(1)} %get-tuple-element.91.refs_1_, f32[8,48,512]{2,1,0:T(8,128)S(1)} %get-tuple-element.93.refs_2_, bf16[8,48,512]{2,1,0:T(8,128)(2,1)S(1)} %get-tuple-element.94.refs_3_, ...), custom_call_target="tpu_custom_call" | custom-call | flops 14400000000 | bytes 1000000 | tf_op jit(solution)/shard_map/feed/pallas_call | solution.py:72
  (80 shorter events, 20.1 us)
Async XLA Ops:
  0.0 55.4 %copy-start = (bf16[2,7,7,2048]{3,0,2,1:T(2,128)(2,1)S(1)}, bf16[2,7,7,2048]{3,0,2,1:T(2,128)(2,1)}, u32[]{:S(2)}) copy-start(bf16[2,7,7,2048]{3,0,2,1:T(2,128)(2,1)} %param.15) | copy-start | bytes 1204228
  1.1 14.2 %collective-permute-start.1 = (bf16[24,6,512]{2,1,0:T(8,128)(2,1)S(1)}, bf16[24,6,512]{2,1,0:T(8,128)(2,1)S(1)}, u32[]{:S(2)}, u32[]{:S(2)}) collective-permute-start(bf16[24,6,512]{2,1,0:T(8,128)(2,1)S(1)} %get-tuple-element.113), channel_id=1, source_target_pairs={{8,0},{16,8},{24,16},{32,24},{40,32},{48,40},{56,48},{64,56},{72,6... | collective-permute-start | bytes 442376 | tf_op jit(solution)/shard_map/ppermute | solution.py:371
  7.4 8.7 %collective-permute-start = (bf16[24,6,512]{2,1,0:T(8,128)(2,1)S(1)}, bf16[24,6,512]{2,1,0:T(8,128)(2,1)S(1)}, u32[]{:S(2)}, u32[]{:S(2)}) collective-permute-start(bf16[24,6,512]{2,1,0:T(8,128)(2,1)S(1)} %get-tuple-element.114), channel_id=1, source_target_pairs={{0,8},{8,16},{16,24},{24,32},{32,40},{40,48},{48,56},{56,64},{64,7... | collective-permute-start | bytes 442376 | tf_op jit(solution)/shard_map/ppermute | solution.py:371
  12.3 7.9 %copy-start.2 = (bf16[24,48,512]{2,1,0:T(8,128)(2,1)S(1)}, bf16[24,48,512]{2,1,0:T(8,128)(2,1)}, u32[]{:S(2)}) copy-start(bf16[24,48,512]{2,1,0:T(8,128)(2,1)} %refs_3_.5) | copy-start | bytes 3538948
  12.3 7.9 %copy-start.6 = (bf16[2,512,1536]{2,1,0:T(8,128)(2,1)S(1)}, bf16[2,512,1536]{2,1,0:T(8,128)(2,1)}, u32[]{:S(2)}) copy-start(bf16[2,512,1536]{2,1,0:T(8,128)(2,1)} %refs_7_.7) | copy-start | bytes 9437188
  12.3 7.9 %copy-start.7 = (bf16[2,512,512]{2,1,0:T(8,128)(2,1)S(1)}, bf16[2,512,512]{2,1,0:T(8,128)(2,1)}, u32[]{:S(2)}) copy-start(bf16[2,512,512]{2,1,0:T(8,128)(2,1)} %refs_4_.11) | copy-start | bytes 3145732
  12.3 7.9 %copy-start.8 = (f32[2,512]{1,0:T(2,128)S(1)}, f32[2,512]{1,0:T(2,128)}, u32[]{:S(2)}) copy-start(f32[2,512]{1,0:T(2,128)} %refs_5_.11) | copy-start | bytes 12292
  12.4 8.0 %copy-start.10 = (f32[2,512]{1,0:T(2,128)S(1)}, f32[2,512]{1,0:T(2,128)}, u32[]{:S(2)}) copy-start(f32[2,512]{1,0:T(2,128)} %refs_15_.3) | copy-start | bytes 12292
  16.2 15.7 %collective-permute-start.2 = (bf16[6,60,512]{2,1,0:T(8,128)(2,1)S(1)}, bf16[6,60,512]{2,1,0:T(8,128)(2,1)S(1)}, u32[]{:S(2)}, u32[]{:S(2)}) collective-permute-start(bf16[6,60,512]{2,1,0:T(8,128)(2,1)S(1)} %pad_maximum_fusion), channel_id=1, source_target_pairs={{0,1},{1,2},{2,3},{3,4},{4,5},{5,6},{6,7},{8,9},{9,10},{10,11},{11... | collective-permute-start | bytes 1105928 | tf_op jit(solution)/shard_map/ppermute | solution.py:368
  19.0 13.0 %collective-permute-start.3 = (bf16[6,60,512]{2,1,0:T(8,128)(2,1)S(1)}, bf16[6,60,512]{2,1,0:T(8,128)(2,1)S(1)}, u32[]{:S(2)}, u32[]{:S(2)}) collective-permute-start(bf16[6,60,512]{2,1,0:T(8,128)(2,1)S(1)} %pad_maximum_fusion.1), channel_id=1, source_target_pairs={{1,0},{2,1},{3,2},{4,3},{5,4},{6,5},{7,6},{9,8},{10,9},{11,10},{12... | collective-permute-start | bytes 1105928 | tf_op jit(solution)/shard_map/ppermute | solution.py:368
  37.8 10.2 %collective-permute-start.4 = (bf16[3,48,512]{2,1,0:T(8,128)(2,1)S(1)}, bf16[3,48,512]{2,1,0:T(8,128)(2,1)S(1)}, u32[]{:S(2)}, u32[]{:S(2)}) collective-permute-start(bf16[3,48,512]{2,1,0:T(8,128)(2,1)S(1)} %get-tuple-element.68), channel_id=1, source_target_pairs={{0,1},{1,2},{2,3},{3,4},{4,5},{5,6},{6,7},{8,9},{9,10},{10,11},{11... | collective-permute-start | bytes 442376 | tf_op jit(solution)/shard_map/ppermute | solution.py:368
  42.2 7.3 %collective-permute-start.5 = (bf16[3,48,512]{2,1,0:T(8,128)(2,1)S(1)}, bf16[3,48,512]{2,1,0:T(8,128)(2,1)S(1)}, u32[]{:S(2)}, u32[]{:S(2)}) collective-permute-start(bf16[3,48,512]{2,1,0:T(8,128)(2,1)S(1)} %get-tuple-element.69), channel_id=1, source_target_pairs={{1,0},{2,1},{3,2},{4,3},{5,4},{6,5},{7,6},{9,8},{10,9},{11,10},{12... | collective-permute-start | bytes 442376 | tf_op jit(solution)/shard_map/ppermute | solution.py:368
  43.5 11.8 %copy-start.13 = (f32[256,49,1]{0,1,2:T(8,128)S(1)}, f32[256,49,1]{0,1,2:T(8,128)}, u32[]{:S(2)}) copy-start(f32[256,49,1]{0,1,2:T(8,128)} %constant.13) | copy-start | bytes 150532
  43.6 19.7 %copy-start.4 = (bf16[2,2048,512]{2,1,0:T(8,128)(2,1)S(1)}, bf16[2,2048,512]{2,1,0:T(8,128)(2,1)}, u32[]{:S(2)}) copy-start(bf16[2,2048,512]{2,1,0:T(8,128)(2,1)} %refs_14_.3) | copy-start | bytes 12582916
  49.8 8.0 %collective-permute-start.7 = (bf16[30,3,512]{2,1,0:T(4,128)(2,1)S(1)}, bf16[30,3,512]{2,1,0:T(4,128)(2,1)S(1)}, u32[]{:S(2)}, u32[]{:S(2)}) collective-permute-start(bf16[30,3,512]{2,1,0:T(4,128)(2,1)S(1)} %get-tuple-element.127), channel_id=1, source_target_pairs={{8,0},{16,8},{24,16},{32,24},{40,32},{48,40},{56,48},{64,56},{72,6... | collective-permute-start | bytes 276488 | tf_op jit(solution)/shard_map/ppermute | solution.py:371
  55.4 7.9 %collective-permute-start.6 = (bf16[30,3,512]{2,1,0:T(4,128)(2,1)S(1)}, bf16[30,3,512]{2,1,0:T(4,128)(2,1)S(1)}, u32[]{:S(2)}, u32[]{:S(2)}) collective-permute-start(bf16[30,3,512]{2,1,0:T(4,128)(2,1)S(1)} %get-tuple-element.128), channel_id=1, source_target_pairs={{0,8},{8,16},{16,24},{24,32},{32,40},{40,48},{48,56},{56,64},{64,7... | collective-permute-start | bytes 276488 | tf_op jit(solution)/shard_map/ppermute | solution.py:371
  79.3 8.8 %collective-permute-start.8 = (bf16[24,6,512]{2,1,0:T(8,128)(2,1)S(1)}, bf16[24,6,512]{2,1,0:T(8,128)(2,1)S(1)}, u32[]{:S(2)}, u32[]{:S(2)}) collective-permute-start(bf16[24,6,512]{2,1,0:T(8,128)(2,1)S(1)} %get-tuple-element.85), channel_id=1, source_target_pairs={{0,8},{8,16},{16,24},{24,32},{32,40},{40,48},{48,56},{56,64},{64,7... | collective-permute-start | bytes 442376 | tf_op jit(solution)/shard_map/ppermute | solution.py:371
  79.4 9.6 %collective-permute-start.9 = (bf16[24,6,512]{2,1,0:T(8,128)(2,1)S(1)}, bf16[24,6,512]{2,1,0:T(8,128)(2,1)S(1)}, u32[]{:S(2)}, u32[]{:S(2)}) collective-permute-start(bf16[24,6,512]{2,1,0:T(8,128)(2,1)S(1)} %get-tuple-element.86), channel_id=1, source_target_pairs={{8,0},{16,8},{24,16},{32,24},{40,32},{48,40},{56,48},{64,56},{72,6... | collective-permute-start | bytes 442376 | tf_op jit(solution)/shard_map/ppermute | solution.py:371
  89.1 12.1 %collective-permute-start.10 = (bf16[6,60,512]{2,1,0:T(8,128)(2,1)S(1)}, bf16[6,60,512]{2,1,0:T(8,128)(2,1)S(1)}, u32[]{:S(2)}, u32[]{:S(2)}) collective-permute-start(bf16[6,60,512]{2,1,0:T(8,128)(2,1)S(1)} %pad_maximum_fusion.2), channel_id=1, source_target_pairs={{0,1},{1,2},{2,3},{3,4},{4,5},{5,6},{6,7},{8,9},{9,10},{10,11},{11... | collective-permute-start | bytes 1105928 | tf_op jit(solution)/shard_map/ppermute | solution.py:368
  92.0 12.7 %collective-permute-start.11 = (bf16[6,60,512]{2,1,0:T(8,128)(2,1)S(1)}, bf16[6,60,512]{2,1,0:T(8,128)(2,1)S(1)}, u32[]{:S(2)}, u32[]{:S(2)}) collective-permute-start(bf16[6,60,512]{2,1,0:T(8,128)(2,1)S(1)} %pad_maximum_fusion.3), channel_id=1, source_target_pairs={{1,0},{2,1},{3,2},{4,3},{5,4},{6,5},{7,6},{9,8},{10,9},{11,10},{12... | collective-permute-start | bytes 1105928 | tf_op jit(solution)/shard_map/ppermute | solution.py:368
  110.1 10.8 %collective-permute-start.12 = (bf16[3,48,512]{2,1,0:T(8,128)(2,1)S(1)}, bf16[3,48,512]{2,1,0:T(8,128)(2,1)S(1)}, u32[]{:S(2)}, u32[]{:S(2)}) collective-permute-start(bf16[3,48,512]{2,1,0:T(8,128)(2,1)S(1)} %get-tuple-element.97), channel_id=1, source_target_pairs={{0,1},{1,2},{2,3},{3,4},{4,5},{5,6},{6,7},{8,9},{9,10},{10,11},{11... | collective-permute-start | bytes 442376 | tf_op jit(solution)/shard_map/ppermute | solution.py:368
  115.2 7.5 %collective-permute-start.13 = (bf16[3,48,512]{2,1,0:T(8,128)(2,1)S(1)}, bf16[3,48,512]{2,1,0:T(8,128)(2,1)S(1)}, u32[]{:S(2)}, u32[]{:S(2)}) collective-permute-start(bf16[3,48,512]{2,1,0:T(8,128)(2,1)S(1)} %get-tuple-element.98), channel_id=1, source_target_pairs={{1,0},{2,1},{3,2},{4,3},{5,4},{6,5},{7,6},{9,8},{10,9},{11,10},{12... | collective-permute-start | bytes 442376 | tf_op jit(solution)/shard_map/ppermute | solution.py:368
  122.9 5.5 %collective-permute-start.15 = (bf16[30,3,512]{2,1,0:T(4,128)(2,1)S(1)}, bf16[30,3,512]{2,1,0:T(4,128)(2,1)S(1)}, u32[]{:S(2)}, u32[]{:S(2)}) collective-permute-start(bf16[30,3,512]{2,1,0:T(4,128)(2,1)S(1)} %get-tuple-element.123), channel_id=1, source_target_pairs={{8,0},{16,8},{24,16},{32,24},{40,32},{48,40},{56,48},{64,56},{72,6... | collective-permute-start | bytes 276488 | tf_op jit(solution)/shard_map/ppermute | solution.py:371
  126.0 7.9 %collective-permute-start.14 = (bf16[30,3,512]{2,1,0:T(4,128)(2,1)S(1)}, bf16[30,3,512]{2,1,0:T(4,128)(2,1)S(1)}, u32[]{:S(2)}, u32[]{:S(2)}) collective-permute-start(bf16[30,3,512]{2,1,0:T(4,128)(2,1)S(1)} %get-tuple-element.124), channel_id=1, source_target_pairs={{0,8},{8,16},{16,24},{24,32},{32,40},{40,48},{48,56},{56,64},{64,7... | collective-permute-start | bytes 276488 | tf_op jit(solution)/shard_map/ppermute | solution.py:371
  (6 other events, 27.6 us)

commit v4 on v3

--- a/solution.py
+++ b/solution.py
@@ -172,15 +172,18 @@
 
         windows = [kv[i * 4 - RADIUS : i * 4 - RADIUS + 16, columns] for i in bands]
     elif kind == "outer":
-        ga, win, kv, n, s, xo, yo, wo, eo, no, so, kvh, wide, halo, mask = refs
+        ga, win, kv, n, s, nc, sc, xo, yo, wo, eo, no, so, kvh, wide, halo, mask = refs
 
         @pl.when(j == 0)
         def _():
             edge = jnp.zeros((12, 2, D), F32)
             wide[:, 0:2] = edge
             wide[:, 62:64] = edge
-            wide[:6, 2:62] = incoming(n)
-            wide[6:, 2:62] = incoming(s)
+            for first, middle, corners in ((0, n, nc), (6, s, sc)):
+                wide[first : first + 6, 8:56] = incoming(middle)
+                sides = incoming(corners)
+                wide[first : first + 6, 2:8] = sides[:, :6]
+                wide[first : first + 6, 56:62] = sides[:, 6:]
             y = wide[...].reshape(12 * 64, D).astype(BF)
             halo[...] = jnp.dot(y, win[:, D:], preferred_element_type=F32).astype(BF).reshape(12, 64, 2 * D)
             kvh[...] = halo[4:8]
@@ -245,7 +248,7 @@
     return call(body, kind, ATTEND_VMEM, 3, args, specs, outs, tuple(whole(o) for o in outs), scratch, cost)
 
 
-def feed_kernel(layer, last, *refs):
+def feed_kernel(layer, last, bands, band_ref, *refs):
     (x_in, x_out, x_mid, y_in, y_out, y_mid, n_ref, s_ref, w_ref, e_ref), refs = refs[:10], refs[10:]
     forward_ref, inverse_ref, kernel_ref, expand_ref, shrink_ref, gain_ref = refs[:6]
     outs, (wide, result, spectra) = refs[6:-3], refs[-3:]
@@ -261,6 +264,14 @@
         for piece in (n_ref, y_out[:4], y_mid[:4], y_in, y_mid[4:], y_out[4:], s_ref):
             wide[first : first + piece.shape[0], 8 : 8 + W] = piece[...].astype(F32)
             first += piece.shape[0]
+
+        @pl.when(band_ref[0] == 0)
+        def _():
+            wide[:REACH] = jnp.zeros((REACH, 64, D), F32)
+
+        @pl.when(band_ref[0] == bands - 1)
+        def _():
+            wide[REACH + H :] = jnp.zeros((REACH, 64, D), F32)
 
     here = pl.ds(pl.multiple_of(step * PAIR * PW, PAIR * PW), PAIR * PW)
     count = PAIR * H // PH
@@ -321,16 +332,17 @@
             oe_ref[r * 6 : r * 6 + 6] = y[:, W - RADIUS :]
 
 
-def feed(last, layer, pieces, matrices, kernels, expand, shrink, gain):
+def feed(last, layer, bands, band, pieces, matrices, kernels, expand, shrink, gain):
     if last:
         outs = (shape(H, W, D),)
     else:
         rows, cols = shape(RADIUS, W, D), shape(H, RADIUS, D)
         outs = (shape(H, W, D, dtype=F32), rows, rows, cols, cols)
-    args = (*pieces, *matrices, kernels, expand, shrink, gain)
-    specs = [whole(a) for a in (*pieces, *matrices)] + [of_layer(a, layer) for a in (kernels, expand, shrink)]
+    args = (band, *pieces, *matrices, kernels, expand, shrink, gain)
+    specs = [pl.BlockSpec(memory_space=pltpu.SMEM)]
+    specs += [whole(a) for a in (*pieces, *matrices)] + [of_layer(a, layer) for a in (kernels, expand, shrink)]
     return call(
-        functools.partial(feed_kernel, layer, last),
+        functools.partial(feed_kernel, layer, last, bands),
         "feed",
         FEED_VMEM,
         W // PW // PAIR,
@@ -359,7 +371,7 @@
     norm_feedforward,
 ):
     nlat, nlon = sizes
-    north = [(i, i + 1) for i in range(nlat - 1)]
+    north = [(i, (i + 1) % nlat) for i in range(nlat)]
     south = [(b, a) for a, b in north]
     east = [(i, (i + 1) % nlon) for i in range(nlon)]
     west = [(b, a) for a, b in east]
@@ -388,12 +400,13 @@
         run = functools.partial(attend, raw=raw, layer=layer, grid_height=nlat * H, band=band, wout=attention_out)
         run = functools.partial(run, gf=gains_f, ga=gains_a, x=x)
         w, e = trade_lon(w, e)
+        n, s = trade_lat(n, s)
         q, kvm = project(layer, x, attention_in, gains_a)
-        n = jnp.concatenate([w[:RADIUS], n, e[:RADIUS]], 1)
-        s = jnp.concatenate([w[H - RADIUS :], s, e[H - RADIUS :]], 1)
-        n, s = trade_lat(n, s)
+        nc = jnp.concatenate([w[:RADIUS], e[:RADIUS]], 1)
+        sc = jnp.concatenate([w[H - RADIUS :], e[H - RADIUS :]], 1)
+        nc, sc = trade_lat(nc, sc)
         x_in, y_in, w_in, e_in, kv = run("inner", q=q, extra=(attention_in, kvm, x, w, e), cost=8)
-        x_out, y_out, w_out, e_out, no, so, kvh = run("outer", q=q, extra=(attention_in, kv, n, s), cost=8)
+        x_out, y_out, w_out, e_out, no, so, kvh = run("outer", q=q, extra=(attention_in, kv, n, s, nc, sc), cost=8)
         n, s = trade_lat(no, so)
         x_mid, y_mid, w_mid, e_mid = run("between", q=q, extra=(kv, kvh), cost=8)
         n, s, w_out, e_out, w_mid, e_mid = lax.optimization_barrier((n, s, w_out, e_out, w_mid, e_mid))
@@ -405,6 +418,8 @@
         x, *edges = feed(
             last,
             layer,
+            nlat,
+            band,
             (x_in, x_out, x_mid, y_in, y_out, y_mid, n, s, w, e),
             matrices,
             kernels,

time: 152 us -> 142 us (0.934)
  waiting for transfers between devices: 30.3 us -> 22 us
    ppermute x8 -> x12, waiting for transfers between devices: 14.4 us -> 0.03 us  [trade_lat(): return (lax.ppermute(s, 'lat', north), lax.ppermute(n, 'lat', south))]
    ppermute x8, waiting for transfers between devices: 15.9 us -> 22 us  [trade_lon(): return (lax.ppermute(e, 'lon', east), lax.ppermute(w, 'lon', west))]
    ppermute x8, starting transfers between devices: 20.3 us -> 16.1 us  [trade_lon(): return (lax.ppermute(e, 'lon', east), lax.ppermute(w, 'lon', west))]
    ppermute x8 -> x12, starting transfers between devices: 20.2 us -> 24.2 us  [trade_lat(): return (lax.ppermute(s, 'lat', north), lax.ppermute(n, 'lat', south))]
  transfers between devices with their start and end apart: 16 -> 20, of which waited for: 12 -> 6; matrix products, arithmetic and copies ran while one was open for 2% -> 2% of each run, Pallas kernels for 18% -> 19%
where the time goes in v4:
time: 142 us; the launch traced here: 141 us
  Pallas kernels  70 us (49%)
  starting transfers between devices  40.4 us (28%)
  waiting for transfers between devices  22 us (15%)
  local copies, waits for them, and re-layouts  6.52 us (5%)
  matrix products  1.86 us (1%)
    pallas_call x10, Pallas kernels, call(): pl.pallas_call(body, grid=(grid,), in_specs=specs, out_specs=out_specs, o...  70 us
    ppermute x12, starting transfers between devices, trade_lat(): return (lax.ppermute(s, 'lat', north), lax.ppermute(n, 'lat', south))  24.2 us
    ppermute x8, waiting for transfers between devices, trade_lon(): return (lax.ppermute(e, 'lon', east), lax.ppermute(w, 'lon', west))  22 us
    ppermute x8, starting transfers between devices, trade_lon(): return (lax.ppermute(e, 'lon', east), lax.ppermute(w, 'lon', west))  16.1 us
    unnamed x49, local copies, waits for them, and re-layouts  4.23 us
  transfers between devices with their start and end apart: 20, of which 6 were waited for; matrix products, arithmetic and copies ran while one was open for 2% of the time, Pallas kernels for 19%

profile of v4, /device:TPU:0, one launch (start us, length us, event | category | flops | bytes accessed | tf_op | source)
XLA Modules:
  0.0 141.3 jit_solution(16320250864966440124)
XLA Ops:
  1.1 6.3 %collective-permute-start.1 = (bf16[24,6,512]{2,1,0:T(8,128)(2,1)S(1)}, bf16[24,6,512]{2,1,0:T(8,128)(2,1)S(1)}, u32[]{:S(2)}, u32[]{:S(2)}) collective-permute-start(bf16[24,6,512]{2,1,0:T(8,128)(2,1)S(1)} %get-tuple-element.113), channel_id=1, source_target_pairs={{8,0},{16,8},{24,16},{32,24},{40,32},{48,40},{56,48},{64,56},{72,6... | collective-permute-start | bytes 442376 | tf_op jit(solution)/shard_map/ppermute | solution.py:383
  8.5 2.9 %collective-permute-start.3 = (bf16[6,48,512]{2,1,0:T(8,128)(2,1)S(1)}, bf16[6,48,512]{2,1,0:T(8,128)(2,1)S(1)}, u32[]{:S(2)}, u32[]{:S(2)}) collective-permute-start(bf16[6,48,512]{2,1,0:T(8,128)(2,1)S(1)} %get-tuple-element.111), channel_id=1, source_target_pairs={{1,0},{2,1},{3,2},{4,3},{5,4},{6,5},{7,6},{0,7},{9,8},{10,9},{11,1... | collective-permute-start | bytes 884744 | tf_op jit(solution)/shard_map/ppermute | solution.py:380
  15.3 3.0 %project.2 = (bf16[24,48,512]{2,1,0:T(8,128)(2,1)S(1)}, bf16[24,32,1024]{2,1,0:T(8,128)(2,1)S(1)}) custom-call(bf16[24,48,512]{2,1,0:T(8,128)(2,1)S(1)} %copy-done.1, bf16[2,512,1536]{2,1,0:T(8,128)(2,1)S(1)} %copy-done.5, f32[2,512]{1,0:T(2,128)S(1)} %copy-done.9), custom_call_target="tpu_custom_call" | custom-call | flops 2400000000 | bytes 1000000 | tf_op jit(solution)/shard_map/project/pallas_call | solution.py:72
  18.6 5.2 %collective-permute-done.refs_10_ = bf16[24,6,512]{2,1,0:T(8,128)(2,1)S(1)} collective-permute-done((bf16[24,6,512]{2,1,0:T(8,128)(2,1)S(1)}, bf16[24,6,512]{2,1,0:T(8,128)(2,1)S(1)}, u32[]{:S(2)}, u32[]{:S(2)}) %collective-permute-start) | collective-permute-done | bytes 147488 | tf_op jit(solution)/shard_map/ppermute | solution.py:383
  24.0 4.2 %collective-permute-start.5 = (bf16[6,12,512]{2,1,0:T(8,128)(2,1)S(1)}, bf16[6,12,512]{2,1,0:T(8,128)(2,1)S(1)}, u32[]{:S(2)}, u32[]{:S(2)}) collective-permute-start(bf16[6,12,512]{2,1,0:T(8,128)(2,1)S(1)} %pad_maximum_fusion.1), channel_id=1, source_target_pairs={{1,0},{2,1},{3,2},{4,3},{5,4},{6,5},{7,6},{0,7},{9,8},{10,9},{11,1... | collective-permute-start | bytes 221192 | tf_op jit(solution)/shard_map/ppermute | solution.py:380
  28.2 5.9 %inner.2 = (f32[8,48,512]{2,1,0:T(8,128)S(1)}, bf16[8,48,512]{2,1,0:T(8,128)(2,1)S(1)}, bf16[8,3,512]{2,1,0:T(4,128)(2,1)S(1)}, bf16[8,3,512]{2,1,0:T(4,128)(2,1)S(1)}, bf16[24,64,1024]{2,1,0:T(8,128)(2,1)S(1)}) custom-call(s32[1]{0:T(128)} %bitcast.band_ref, bf16[24,48,512]{2,1,0:T(8,128)(2,1)S(1)} %get-tuple-element.58.refs_0_.refs_1_, ...), custom_call_target="tpu_custom_call" | custom-call | flops 4800000000 | bytes 1000000 | tf_op jit(solution)/shard_map/inner/pallas_call | solution.py:72
  34.2 6.0 %outer.2 = (f32[8,48,512]{2,1,0:T(8,128)S(1)}, bf16[8,48,512]{2,1,0:T(8,128)(2,1)S(1)}, bf16[8,3,512]{2,1,0:T(4,128)(2,1)S(1)}, bf16[8,3,512]{2,1,0:T(4,128)(2,1...) custom-call(s32[1]{0:T(128)} %bitcast.band_ref, ...), custom_call_target="tpu_custom_call" | custom-call | flops 4800000000 | bytes 1000000 | tf_op jit(solution)/shard_map/outer/pallas_call | solution.py:72
  40.2 4.1 %collective-permute-start.7 = (bf16[3,48,512]{2,1,0:T(8,128)(2,1)S(1)}, bf16[3,48,512]{2,1,0:T(8,128)(2,1)S(1)}, u32[]{:S(2)}, u32[]{:S(2)}) collective-permute-start(bf16[3,48,512]{2,1,0:T(8,128)(2,1)S(1)} %get-tuple-element.69), channel_id=1, source_target_pairs={{1,0},{2,1},{3,2},{4,3},{5,4},{6,5},{7,6},{0,7},{9,8},{10,9},{11,1... | collective-permute-start | bytes 442376 | tf_op jit(solution)/shard_map/ppermute | solution.py:380
  44.4 4.4 %between.2 = (f32[8,48,512]{2,1,0:T(8,128)S(1)}, bf16[8,48,512]{2,1,0:T(8,128)(2,1)S(1)}, bf16[8,3,512]{2,1,0:T(4,128)(2,1)S(1)}, bf16[8,3,512]{2,1,0:T(4,128)(2,1)S(1)}) custom-call(s32[1]{0:T(128)} %bitcast.band_ref, bf16[24,48,512]{2,1,0:T(8,128)(2,1)S(1)} %get-tuple-element.58.refs_0_.refs_1_, ...), custom_call_target="tpu_custom_call" | custom-call | flops 4800000000 | bytes 1000000 | tf_op jit(solution)/shard_map/between/pallas_call | solution.py:72
  51.6 5.7 %collective-permute-done.8.refs_8_ = bf16[30,3,512]{2,1,0:T(4,128)(2,1)S(1)} collective-permute-done((bf16[30,3,512]{2,1,0:T(4,128)(2,1)S(1)}, bf16[30,3,512]{2,1,0:T(4,128)(2,1)S(1)}, u32[]{:S(2)}, u32[]{:S(2)}) %collective-permute-start.8) | collective-permute-done | bytes 92192 | tf_op jit(solution)/shard_map/ppermute | solution.py:383
  57.3 15.8 %feed.2 = (f32[24,48,512]{2,1,0:T(8,128)S(1)}, bf16[6,48,512]{2,1,0:T(8,128)(2,1)S(1)}, bf16[6,48,512]{2,1,0:T(8,128)(2,1)S(1)}, bf16[24,6,512]{2,1,0:T(8,128)(2,1)S(1)}, bf16[24,6,512]{2,1,0:T(8,128)(2,1)S(1)}) custom-call(s32[1]{0:T(128)} %bitcast.band_ref, f32[8,48,512]{2,1,0:T(8,128)S(1)} %get-tuple-element.60.refs_0_, ...), custom_call_target="tpu_custom_call" | custom-call | flops 14400000000 | bytes 1000000 | tf_op jit(solution)/shard_map/feed/pallas_call | solution.py:72
  73.2 5.3 %collective-permute-start.11 = (bf16[24,6,512]{2,1,0:T(8,128)(2,1)S(1)}, bf16[24,6,512]{2,1,0:T(8,128)(2,1)S(1)}, u32[]{:S(2)}, u32[]{:S(2)}) collective-permute-start(bf16[24,6,512]{2,1,0:T(8,128)(2,1)S(1)} %get-tuple-element.86), channel_id=1, source_target_pairs={{8,0},{16,8},{24,16},{32,24},{40,32},{48,40},{56,48},{64,56},{72,6... | collective-permute-start | bytes 442376 | tf_op jit(solution)/shard_map/ppermute | solution.py:383
  78.6 4.1 %collective-permute-start.13 = (bf16[6,48,512]{2,1,0:T(8,128)(2,1)S(1)}, bf16[6,48,512]{2,1,0:T(8,128)(2,1)S(1)}, u32[]{:S(2)}, u32[]{:S(2)}) collective-permute-start(bf16[6,48,512]{2,1,0:T(8,128)(2,1)S(1)} %get-tuple-element.90), channel_id=1, source_target_pairs={{1,0},{2,1},{3,2},{4,3},{5,4},{6,5},{7,6},{0,7},{9,8},{10,9},{11,1... | collective-permute-start | bytes 884744 | tf_op jit(solution)/shard_map/ppermute | solution.py:380
  82.7 3.0 %project.3 = (bf16[24,48,512]{2,1,0:T(8,128)(2,1)S(1)}, bf16[24,32,1024]{2,1,0:T(8,128)(2,1)S(1)}) custom-call(f32[24,48,512]{2,1,0:T(8,128)S(1)} %get-tuple-element.82.x_ref.refs_2_.refs_3_.refs_9_, bf16[2,512,1536]{2,1,0:T(8,128)(2,1)S(1)} %copy-done.6, f32[2,512]{1,0:T(2,128)S(1)} %copy-done.10), custom_call_target="tpu_custom_call" | custom-call | flops 2400000000 | bytes 1000000 | tf_op jit(solution)/shard_map/project/pallas_call | solution.py:72
  85.7 2.7 %collective-permute-done.10.refs_10_ = bf16[24,6,512]{2,1,0:T(8,128)(2,1)S(1)} collective-permute-done((bf16[24,6,512]{2,1,0:T(8,128)(2,1)S(1)}, bf16[24,6,512]{2,1,0:T(8,128)(2,1)S(1)}, u32[]{:S(2)}, u32[]{:S(2)}) %collective-permute-start.10) | collective-permute-done | bytes 147488 | tf_op jit(solution)/shard_map/ppermute | solution.py:383
  90.2 2.9 %collective-permute-start.15 = (bf16[6,12,512]{2,1,0:T(8,128)(2,1)S(1)}, bf16[6,12,512]{2,1,0:T(8,128)(2,1)S(1)}, u32[]{:S(2)}, u32[]{:S(2)}) collective-permute-start(bf16[6,12,512]{2,1,0:T(8,128)(2,1)S(1)} %pad_maximum_fusion.3), channel_id=1, source_target_pairs={{1,0},{2,1},{3,2},{4,3},{5,4},{6,5},{7,6},{0,7},{9,8},{10,9},{11,1... | collective-permute-start | bytes 221192 | tf_op jit(solution)/shard_map/ppermute | solution.py:380
  93.0 5.7 %inner.3 = (f32[8,48,512]{2,1,0:T(8,128)S(1)}, bf16[8,48,512]{2,1,0:T(8,128)(2,1)S(1)}, bf16[8,3,512]{2,1,0:T(4,128)(2,1)S(1)}, bf16[8,3,512]{2,1,0:T(4,128)(2,1)S(1)}, bf16[24,64,1024]{2,1,0:T(8,128)(2,1)S(1)}) custom-call(s32[1]{0:T(128)} %bitcast.band_ref, bf16[24,48,512]{2,1,0:T(8,128)(2,1)S(1)} %get-tuple-element.83.refs_0_.refs_1_, ...), custom_call_target="tpu_custom_call" | custom-call | flops 4800000000 | bytes 1000000 | tf_op jit(solution)/shard_map/inner/pallas_call | solution.py:72
  98.8 5.5 %outer.3 = (f32[8,48,512]{2,1,0:T(8,128)S(1)}, bf16[8,48,512]{2,1,0:T(8,128)(2,1)S(1)}, bf16[8,3,512]{2,1,0:T(4,128)(2,1)S(1)}, bf16[8,3,512]{2,1,0:T(4,128)(2,1...) custom-call(s32[1]{0:T(128)} %bitcast.band_ref, ...), custom_call_target="tpu_custom_call" | custom-call | flops 4800000000 | bytes 1000000 | tf_op jit(solution)/shard_map/outer/pallas_call | solution.py:72
  104.4 4.1 %collective-permute-start.17 = (bf16[3,48,512]{2,1,0:T(8,128)(2,1)S(1)}, bf16[3,48,512]{2,1,0:T(8,128)(2,1)S(1)}, u32[]{:S(2)}, u32[]{:S(2)}) collective-permute-start(bf16[3,48,512]{2,1,0:T(8,128)(2,1)S(1)} %get-tuple-element.98), channel_id=1, source_target_pairs={{1,0},{2,1},{3,2},{4,3},{5,4},{6,5},{7,6},{0,7},{9,8},{10,9},{11,1... | collective-permute-start | bytes 442376 | tf_op jit(solution)/shard_map/ppermute | solution.py:380
  108.5 4.4 %between.3 = (f32[8,48,512]{2,1,0:T(8,128)S(1)}, bf16[8,48,512]{2,1,0:T(8,128)(2,1)S(1)}, bf16[8,3,512]{2,1,0:T(4,128)(2,1)S(1)}, bf16[8,3,512]{2,1,0:T(4,128)(2,1)S(1)}) custom-call(s32[1]{0:T(128)} %bitcast.band_ref, bf16[24,48,512]{2,1,0:T(8,128)(2,1)S(1)} %get-tuple-element.83.refs_0_.refs_1_, ...), custom_call_target="tpu_custom_call" | custom-call | flops 4800000000 | bytes 1000000 | tf_op jit(solution)/shard_map/between/pallas_call | solution.py:72
  113.2 3.9 %collective-permute-start.19 = (bf16[30,3,512]{2,1,0:T(4,128)(2,1)S(1)}, bf16[30,3,512]{2,1,0:T(4,128)(2,1)S(1)}, u32[]{:S(2)}, u32[]{:S(2)}) collective-permute-start(bf16[30,3,512]{2,1,0:T(4,128)(2,1)S(1)} %get-tuple-element.123), channel_id=1, source_target_pairs={{8,0},{16,8},{24,16},{32,24},{40,32},{48,40},{56,48},{64,56},{72,6... | collective-permute-start | bytes 276488 | tf_op jit(solution)/shard_map/ppermute | solution.py:383
  117.1 2.4 %collective-permute-done.19.refs_9_ = bf16[30,3,512]{2,1,0:T(4,128)(2,1)S(1)} collective-permute-done((bf16[30,3,512]{2,1,0:T(4,128)(2,1)S(1)}, bf16[30,3,512]{2,1,0:T(4,128)(2,1)S(1)}, u32[]{:S(2)}, u32[]{:S(2)}) %collective-permute-start.19) | collective-permute-done | bytes 92192 | tf_op jit(solution)/shard_map/ppermute | solution.py:383
  119.5 5.5 %collective-permute-done.18.refs_8_ = bf16[30,3,512]{2,1,0:T(4,128)(2,1)S(1)} collective-permute-done((bf16[30,3,512]{2,1,0:T(4,128)(2,1)S(1)}, bf16[30,3,512]{2,1,0:T(4,128)(2,1)S(1)}, u32[]{:S(2)}, u32[]{:S(2)}) %collective-permute-start.18) | collective-permute-done | bytes 92192 | tf_op jit(solution)/shard_map/ppermute | solution.py:383
  125.0 16.3 %feed.3 = bf16[24,48,512]{2,1,0:T(8,128)(2,1)} custom-call(s32[1]{0:T(128)} %bitcast.band_ref, f32[8,48,512]{2,1,0:T(8,128)S(1)} %get-tuple-element.87.refs_0_, f32[8,48,512]{2,1,0:T(8,128)S(1)} %get-tuple-element.91.refs_1_, f32[8,48,512]{2,1,0:T(8,128)S(1)} %get-tuple-element.93.refs_2_, bf16[8,48,512]{2,1,0:T(8,128)(2,1)S(1)} %get-tuple-element.94.refs_3_, ...), custom_call_target="tpu_custom_call" | custom-call | flops 14400000000 | bytes 1000000 | tf_op jit(solution)/shard_map/feed/pallas_call | solution.py:72
  (88 shorter events, 11.4 us)
Async XLA Ops:
  0.0 49.6 %copy-start = (bf16[2,7,7,2048]{3,0,2,1:T(2,128)(2,1)S(1)}, bf16[2,7,7,2048]{3,0,2,1:T(2,128)(2,1)}, u32[]{:S(2)}) copy-start(bf16[2,7,7,2048]{3,0,2,1:T(2,128)(2,1)} %param.15) | copy-start | bytes 1204228
  1.1 17.5 %collective-permute-start.1 = (bf16[24,6,512]{2,1,0:T(8,128)(2,1)S(1)}, bf16[24,6,512]{2,1,0:T(8,128)(2,1)S(1)}, u32[]{:S(2)}, u32[]{:S(2)}) collective-permute-start(bf16[24,6,512]{2,1,0:T(8,128)(2,1)S(1)} %get-tuple-element.113), channel_id=1, source_target_pairs={{8,0},{16,8},{24,16},{32,24},{40,32},{48,40},{56,48},{64,56},{72,6... | collective-permute-start | bytes 442376 | tf_op jit(solution)/shard_map/ppermute | solution.py:383
  7.4 16.4 %collective-permute-start = (bf16[24,6,512]{2,1,0:T(8,128)(2,1)S(1)}, bf16[24,6,512]{2,1,0:T(8,128)(2,1)S(1)}, u32[]{:S(2)}, u32[]{:S(2)}) collective-permute-start(bf16[24,6,512]{2,1,0:T(8,128)(2,1)S(1)} %get-tuple-element.114), channel_id=1, source_target_pairs={{0,8},{8,16},{16,24},{24,32},{32,40},{40,48},{48,56},{56,64},{64,7... | collective-permute-start | bytes 442376 | tf_op jit(solution)/shard_map/ppermute | solution.py:383
  8.5 25.7 %collective-permute-start.3 = (bf16[6,48,512]{2,1,0:T(8,128)(2,1)S(1)}, bf16[6,48,512]{2,1,0:T(8,128)(2,1)S(1)}, u32[]{:S(2)}, u32[]{:S(2)}) collective-permute-start(bf16[6,48,512]{2,1,0:T(8,128)(2,1)S(1)} %get-tuple-element.111), channel_id=1, source_target_pairs={{1,0},{2,1},{3,2},{4,3},{5,4},{6,5},{7,6},{0,7},{9,8},{10,9},{11,1... | collective-permute-start | bytes 884744 | tf_op jit(solution)/shard_map/ppermute | solution.py:380
  11.4 22.7 %collective-permute-start.2 = (bf16[6,48,512]{2,1,0:T(8,128)(2,1)S(1)}, bf16[6,48,512]{2,1,0:T(8,128)(2,1)S(1)}, u32[]{:S(2)}, u32[]{:S(2)}) collective-permute-start(bf16[6,48,512]{2,1,0:T(8,128)(2,1)S(1)} %get-tuple-element.112), channel_id=1, source_target_pairs={{0,1},{1,2},{2,3},{3,4},{4,5},{5,6},{6,7},{7,0},{8,9},{9,10},{10,1... | collective-permute-start | bytes 884744 | tf_op jit(solution)/shard_map/ppermute | solution.py:380
  15.3 12.9 %copy-start.8 = (f32[2,512]{1,0:T(2,128)S(1)}, f32[2,512]{1,0:T(2,128)}, u32[]{:S(2)}) copy-start(f32[2,512]{1,0:T(2,128)} %refs_5_.11) | copy-start | bytes 12292
  15.3 12.9 %copy-start.10 = (f32[2,512]{1,0:T(2,128)S(1)}, f32[2,512]{1,0:T(2,128)}, u32[]{:S(2)}) copy-start(f32[2,512]{1,0:T(2,128)} %refs_15_.3) | copy-start | bytes 12292
  23.9 10.3 %collective-permute-start.4 = (bf16[6,12,512]{2,1,0:T(8,128)(2,1)S(1)}, bf16[6,12,512]{2,1,0:T(8,128)(2,1)S(1)}, u32[]{:S(2)}, u32[]{:S(2)}) collective-permute-start(bf16[6,12,512]{2,1,0:T(8,128)(2,1)S(1)} %pad_maximum_fusion), channel_id=1, source_target_pairs={{0,1},{1,2},{2,3},{3,4},{4,5},{5,6},{6,7},{7,0},{8,9},{9,10},{10,1... | collective-permute-start | bytes 221192 | tf_op jit(solution)/shard_map/ppermute | solution.py:380
  24.0 10.1 %collective-permute-start.5 = (bf16[6,12,512]{2,1,0:T(8,128)(2,1)S(1)}, bf16[6,12,512]{2,1,0:T(8,128)(2,1)S(1)}, u32[]{:S(2)}, u32[]{:S(2)}) collective-permute-start(bf16[6,12,512]{2,1,0:T(8,128)(2,1)S(1)} %pad_maximum_fusion.1), channel_id=1, source_target_pairs={{1,0},{2,1},{3,2},{4,3},{5,4},{6,5},{7,6},{0,7},{9,8},{10,9},{11,1... | collective-permute-start | bytes 221192 | tf_op jit(solution)/shard_map/ppermute | solution.py:380
  40.1 8.7 %collective-permute-start.6 = (bf16[3,48,512]{2,1,0:T(8,128)(2,1)S(1)}, bf16[3,48,512]{2,1,0:T(8,128)(2,1)S(1)}, u32[]{:S(2)}, u32[]{:S(2)}) collective-permute-start(bf16[3,48,512]{2,1,0:T(8,128)(2,1)S(1)} %get-tuple-element.68), channel_id=1, source_target_pairs={{0,1},{1,2},{2,3},{3,4},{4,5},{5,6},{6,7},{7,0},{8,9},{9,10},{10,1... | collective-permute-start | bytes 442376 | tf_op jit(solution)/shard_map/ppermute | solution.py:380
  40.2 8.6 %collective-permute-start.7 = (bf16[3,48,512]{2,1,0:T(8,128)(2,1)S(1)}, bf16[3,48,512]{2,1,0:T(8,128)(2,1)S(1)}, u32[]{:S(2)}, u32[]{:S(2)}) collective-permute-start(bf16[3,48,512]{2,1,0:T(8,128)(2,1)S(1)} %get-tuple-element.69), channel_id=1, source_target_pairs={{1,0},{2,1},{3,2},{4,3},{5,4},{6,5},{7,6},{0,7},{9,8},{10,9},{11,1... | collective-permute-start | bytes 442376 | tf_op jit(solution)/shard_map/ppermute | solution.py:380
  44.3 13.0 %copy-start.4 = (bf16[2,2048,512]{2,1,0:T(8,128)(2,1)S(1)}, bf16[2,2048,512]{2,1,0:T(8,128)(2,1)}, u32[]{:S(2)}) copy-start(bf16[2,2048,512]{2,1,0:T(8,128)(2,1)} %refs_14_.3) | copy-start | bytes 12582916
  49.0 2.5 %collective-permute-start.9 = (bf16[30,3,512]{2,1,0:T(4,128)(2,1)S(1)}, bf16[30,3,512]{2,1,0:T(4,128)(2,1)S(1)}, u32[]{:S(2)}, u32[]{:S(2)}) collective-permute-start(bf16[30,3,512]{2,1,0:T(4,128)(2,1)S(1)} %get-tuple-element.127), channel_id=1, source_target_pairs={{8,0},{16,8},{24,16},{32,24},{40,32},{48,40},{56,48},{64,56},{72,6... | collective-permute-start | bytes 276488 | tf_op jit(solution)/shard_map/ppermute | solution.py:383
  49.1 8.2 %collective-permute-start.8 = (bf16[30,3,512]{2,1,0:T(4,128)(2,1)S(1)}, bf16[30,3,512]{2,1,0:T(4,128)(2,1)S(1)}, u32[]{:S(2)}, u32[]{:S(2)}) collective-permute-start(bf16[30,3,512]{2,1,0:T(4,128)(2,1)S(1)} %get-tuple-element.128), channel_id=1, source_target_pairs={{0,8},{8,16},{16,24},{24,32},{32,40},{40,48},{48,56},{56,64},{64,7... | collective-permute-start | bytes 276488 | tf_op jit(solution)/shard_map/ppermute | solution.py:383
  73.1 15.3 %collective-permute-start.10 = (bf16[24,6,512]{2,1,0:T(8,128)(2,1)S(1)}, bf16[24,6,512]{2,1,0:T(8,128)(2,1)S(1)}, u32[]{:S(2)}, u32[]{:S(2)}) collective-permute-start(bf16[24,6,512]{2,1,0:T(8,128)(2,1)S(1)} %get-tuple-element.85), channel_id=1, source_target_pairs={{0,8},{8,16},{16,24},{24,32},{32,40},{40,48},{48,56},{56,64},{64,7... | collective-permute-start | bytes 442376 | tf_op jit(solution)/shard_map/ppermute | solution.py:383
  73.2 15.2 %collective-permute-start.11 = (bf16[24,6,512]{2,1,0:T(8,128)(2,1)S(1)}, bf16[24,6,512]{2,1,0:T(8,128)(2,1)S(1)}, u32[]{:S(2)}, u32[]{:S(2)}) collective-permute-start(bf16[24,6,512]{2,1,0:T(8,128)(2,1)S(1)} %get-tuple-element.86), channel_id=1, source_target_pairs={{8,0},{16,8},{24,16},{32,24},{40,32},{48,40},{56,48},{64,56},{72,6... | collective-permute-start | bytes 442376 | tf_op jit(solution)/shard_map/ppermute | solution.py:383
  78.6 20.2 %collective-permute-start.12 = (bf16[6,48,512]{2,1,0:T(8,128)(2,1)S(1)}, bf16[6,48,512]{2,1,0:T(8,128)(2,1)S(1)}, u32[]{:S(2)}, u32[]{:S(2)}) collective-permute-start(bf16[6,48,512]{2,1,0:T(8,128)(2,1)S(1)} %get-tuple-element.89), channel_id=1, source_target_pairs={{0,1},{1,2},{2,3},{3,4},{4,5},{5,6},{6,7},{7,0},{8,9},{9,10},{10,1... | collective-permute-start | bytes 884744 | tf_op jit(solution)/shard_map/ppermute | solution.py:380
  78.6 20.2 %collective-permute-start.13 = (bf16[6,48,512]{2,1,0:T(8,128)(2,1)S(1)}, bf16[6,48,512]{2,1,0:T(8,128)(2,1)S(1)}, u32[]{:S(2)}, u32[]{:S(2)}) collective-permute-start(bf16[6,48,512]{2,1,0:T(8,128)(2,1)S(1)} %get-tuple-element.90), channel_id=1, source_target_pairs={{1,0},{2,1},{3,2},{4,3},{5,4},{6,5},{7,6},{0,7},{9,8},{10,9},{11,1... | collective-permute-start | bytes 884744 | tf_op jit(solution)/shard_map/ppermute | solution.py:380
  88.5 10.3 %collective-permute-start.14 = (bf16[6,12,512]{2,1,0:T(8,128)(2,1)S(1)}, bf16[6,12,512]{2,1,0:T(8,128)(2,1)S(1)}, u32[]{:S(2)}, u32[]{:S(2)}) collective-permute-start(bf16[6,12,512]{2,1,0:T(8,128)(2,1)S(1)} %pad_maximum_fusion.2), channel_id=1, source_target_pairs={{0,1},{1,2},{2,3},{3,4},{4,5},{5,6},{6,7},{7,0},{8,9},{9,10},{10,1... | collective-permute-start | bytes 221192 | tf_op jit(solution)/shard_map/ppermute | solution.py:380
  90.2 8.6 %collective-permute-start.15 = (bf16[6,12,512]{2,1,0:T(8,128)(2,1)S(1)}, bf16[6,12,512]{2,1,0:T(8,128)(2,1)S(1)}, u32[]{:S(2)}, u32[]{:S(2)}) collective-permute-start(bf16[6,12,512]{2,1,0:T(8,128)(2,1)S(1)} %pad_maximum_fusion.3), channel_id=1, source_target_pairs={{1,0},{2,1},{3,2},{4,3},{5,4},{6,5},{7,6},{0,7},{9,8},{10,9},{11,1... | collective-permute-start | bytes 221192 | tf_op jit(solution)/shard_map/ppermute | solution.py:380
  104.3 8.6 %collective-permute-start.16 = (bf16[3,48,512]{2,1,0:T(8,128)(2,1)S(1)}, bf16[3,48,512]{2,1,0:T(8,128)(2,1)S(1)}, u32[]{:S(2)}, u32[]{:S(2)}) collective-permute-start(bf16[3,48,512]{2,1,0:T(8,128)(2,1)S(1)} %get-tuple-element.97), channel_id=1, source_target_pairs={{0,1},{1,2},{2,3},{3,4},{4,5},{5,6},{6,7},{7,0},{8,9},{9,10},{10,1... | collective-permute-start | bytes 442376 | tf_op jit(solution)/shard_map/ppermute | solution.py:380
  104.4 8.6 %collective-permute-start.17 = (bf16[3,48,512]{2,1,0:T(8,128)(2,1)S(1)}, bf16[3,48,512]{2,1,0:T(8,128)(2,1)S(1)}, u32[]{:S(2)}, u32[]{:S(2)}) collective-permute-start(bf16[3,48,512]{2,1,0:T(8,128)(2,1)S(1)} %get-tuple-element.98), channel_id=1, source_target_pairs={{1,0},{2,1},{3,2},{4,3},{5,4},{6,5},{7,6},{0,7},{9,8},{10,9},{11,1... | collective-permute-start | bytes 442376 | tf_op jit(solution)/shard_map/ppermute | solution.py:380
  113.2 6.3 %collective-permute-start.19 = (bf16[30,3,512]{2,1,0:T(4,128)(2,1)S(1)}, bf16[30,3,512]{2,1,0:T(4,128)(2,1)S(1)}, u32[]{:S(2)}, u32[]{:S(2)}) collective-permute-start(bf16[30,3,512]{2,1,0:T(4,128)(2,1)S(1)} %get-tuple-element.123), channel_id=1, source_target_pairs={{8,0},{16,8},{24,16},{32,24},{40,32},{48,40},{56,48},{64,56},{72,6... | collective-permute-start | bytes 276488 | tf_op jit(solution)/shard_map/ppermute | solution.py:383
  117.1 7.9 %collective-permute-start.18 = (bf16[30,3,512]{2,1,0:T(4,128)(2,1)S(1)}, bf16[30,3,512]{2,1,0:T(4,128)(2,1)S(1)}, u32[]{:S(2)}, u32[]{:S(2)}) collective-permute-start(bf16[30,3,512]{2,1,0:T(4,128)(2,1)S(1)} %get-tuple-element.124), channel_id=1, source_target_pairs={{0,8},{8,16},{16,24},{24,32},{32,40},{40,48},{48,56},{56,64},{64,7... | collective-permute-start | bytes 276488 | tf_op jit(solution)/shard_map/ppermute | solution.py:383
  (10 other events, 70.9 us)

commit v5 on v4

--- a/solution.py
+++ b/solution.py
@@ -400,8 +400,9 @@
         run = functools.partial(attend, raw=raw, layer=layer, grid_height=nlat * H, band=band, wout=attention_out)
         run = functools.partial(run, gf=gains_f, ga=gains_a, x=x)
         w, e = trade_lon(w, e)
+        q, kvm = project(layer, x, attention_in, gains_a)
+        n, s, q = lax.optimization_barrier((n, s, q))
         n, s = trade_lat(n, s)
-        q, kvm = project(layer, x, attention_in, gains_a)
         nc = jnp.concatenate([w[:RADIUS], e[:RADIUS]], 1)
         sc = jnp.concatenate([w[H - RADIUS :], e[H - RADIUS :]], 1)
         nc, sc = trade_lat(nc, sc)

time: 142 us -> 153 us (1.077)
  local copies, waits for them, and re-layouts: 6.52 us -> 14.8 us
  starting transfers between devices: 40.4 us -> 45.2 us
  waiting for transfers between devices: 22 us -> 19.6 us
    unnamed x49 -> x61, local copies, waits for them, and re-layouts: 4.23 us -> 11 us
    ppermute x8, starting transfers between devices: 16.1 us -> 19.8 us  [trade_lon(): return (lax.ppermute(e, 'lon', east), lax.ppermute(w, 'lon', west))]
    ppermute x8, waiting for transfers between devices: 22 us -> 19.6 us  [trade_lon(): return (lax.ppermute(e, 'lon', east), lax.ppermute(w, 'lon', west))]
  transfers between devices with their start and end apart: 20 -> 20, of which waited for: 6 -> 5; matrix products, arithmetic and copies ran while one was open for 2% -> 3% of each run, Pallas kernels for 19% -> 17%
where the time goes in v5:
time: 153 us
  Pallas kernels  70.5 us (46%)
  starting transfers between devices  45.2 us (30%)
  waiting for transfers between devices  19.6 us (13%)
  local copies, waits for them, and re-layouts  14.8 us (10%)
  matrix products  1.85 us (1%)
    pallas_call x10, Pallas kernels, call(): pl.pallas_call(body, grid=(grid,), in_specs=specs, out_specs=out_specs, o...  70.5 us
    ppermute x12, starting transfers between devices, trade_lat(): return (lax.ppermute(s, 'lat', north), lax.ppermute(n, 'lat', south))  25.5 us
    ppermute x8, starting transfers between devices, trade_lon(): return (lax.ppermute(e, 'lon', east), lax.ppermute(w, 'lon', west))  19.8 us
    ppermute x8, waiting for transfers between devices, trade_lon(): return (lax.ppermute(e, 'lon', east), lax.ppermute(w, 'lon', west))  19.6 us
    unnamed x61, local copies, waits for them, and re-layouts  11 us
  transfers between devices with their start and end apart: 20, of which 5 were waited for; matrix products, arithmetic and copies ran while one was open for 3% of the time, Pallas kernels for 17%

profile of v5, /device:TPU:0, one launch (start us, length us, event | category | flops | bytes accessed | tf_op | source)
XLA Modules:
  0.0 152.7 jit_solution(15760597918454611093)
XLA Ops:
  1.8 6.2 %collective-permute-start.1 = (bf16[24,6,512]{2,1,0:T(8,128)(2,1)}, bf16[24,6,512]{2,1,0:T(8,128)(2,1)S(1)}, u32[]{:S(2)}, u32[]{:S(2)}) collective-permute-start(bf16[24,6,512]{2,1,0:T(8,128)(2,1)} %get-tuple-element.123), channel_id=1, source_target_pairs={{8,0},{16,8},{24,16},{32,24},{40,32},{48,40},{56,48},{64,56},{72,6... | collective-permute-start | bytes 442376 | tf_op jit(solution)/shard_map/ppermute | solution.py:383
  13.8 3.0 %project.2 = (bf16[24,48,512]{2,1,0:T(8,128)(2,1)S(1)}, bf16[24,32,1024]{2,1,0:T(8,128)(2,1)S(1)}) custom-call(bf16[24,48,512]{2,1,0:T(8,128)(2,1)S(1)} %copy-done.1, bf16[2,512,1536]{2,1,0:T(8,128)(2,1)S(1)} %copy-done.5, f32[2,512]{1,0:T(2,128)S(1)} %copy-done.10), custom_call_target="tpu_custom_call" | custom-call | flops 2400000000 | bytes 1000000 | tf_op jit(solution)/shard_map/project/pallas_call | solution.py:72
  19.6 3.5 %collective-permute-start.3 = (bf16[6,48,512]{2,1,0:T(8,128)(2,1)}, bf16[6,48,512]{2,1,0:T(8,128)(2,1)}, u32[]{:S(2)}, u32[]{:S(2)}) collective-permute-start(bf16[6,48,512]{2,1,0:T(8,128)(2,1)} %get-tuple-element.70), channel_id=1, source_target_pairs={{1,0},{2,1},{3,2},{4,3},{5,4},{6,5},{7,6},{0,7},{9,8},{10,9},{11,1... | collective-permute-start | bytes 884744 | tf_op jit(solution)/shard_map/ppermute | solution.py:380
  23.3 4.2 %collective-permute-start.5 = (bf16[6,12,512]{2,1,0:T(8,128)(2,1)S(1)}, bf16[6,12,512]{2,1,0:T(8,128)(2,1)S(1)}, u32[]{:S(2)}, u32[]{:S(2)}) collective-permute-start(bf16[6,12,512]{2,1,0:T(8,128)(2,1)S(1)} %pad_maximum_fusion.1), channel_id=1, source_target_pairs={{1,0},{2,1},{3,2},{4,3},{5,4},{6,5},{7,6},{0,7},{9,8},{10,9},{11,1... | collective-permute-start | bytes 221192 | tf_op jit(solution)/shard_map/ppermute | solution.py:380
  32.1 5.8 %inner.2 = (f32[8,48,512]{2,1,0:T(8,128)S(1)}, bf16[8,48,512]{2,1,0:T(8,128)(2,1)S(1)}, bf16[8,3,512]{2,1,0:T(4,128)(2,1)S(1)}, bf16[8,3,512]{2,1,0:T(4,128)(2,1)S(1)}, bf16[24,64,1024]{2,1,0:T(8,128)(2,1)S(1)}) custom-call(s32[1]{0:T(128)} %bitcast.band_ref, bf16[24,48,512]{2,1,0:T(8,128)(2,1)S(1)} %copy-done.17, bf16[24,48,512]{2,1,0:T(8,128)(2,1)S(1)} %copy-done.17, ...), custom_call_target="tpu_custom_call" | custom-call | flops 4800000000 | bytes 1000000 | tf_op jit(solution)/shard_map/inner/pallas_call | solution.py:72
  37.9 6.9 %outer.2 = (f32[8,48,512]{2,1,0:T(8,128)S(1)}, bf16[8,48,512]{2,1,0:T(8,128)(2,1)S(1)}, bf16[8,3,512]{2,1,0:T(4,128)(2,1)S(1)}, bf16[8,3,512]{2,1,0:T(4,128)(2,1...) custom-call(s32[1]{0:T(128)} %bitcast.band_ref, ...), custom_call_target="tpu_custom_call" | custom-call | flops 4800000000 | bytes 1000000 | tf_op jit(solution)/shard_map/outer/pallas_call | solution.py:72
  44.9 4.1 %collective-permute-start.7 = (bf16[3,48,512]{2,1,0:T(8,128)(2,1)S(1)}, bf16[3,48,512]{2,1,0:T(8,128)(2,1)S(1)}, u32[]{:S(2)}, u32[]{:S(2)}) collective-permute-start(bf16[3,48,512]{2,1,0:T(8,128)(2,1)S(1)} %get-tuple-element.78), channel_id=1, source_target_pairs={{1,0},{2,1},{3,2},{4,3},{5,4},{6,5},{7,6},{0,7},{9,8},{10,9},{11,1... | collective-permute-start | bytes 442376 | tf_op jit(solution)/shard_map/ppermute | solution.py:380
  49.1 4.4 %between.2 = (f32[8,48,512]{2,1,0:T(8,128)S(1)}, bf16[8,48,512]{2,1,0:T(8,128)(2,1)S(1)}, bf16[8,3,512]{2,1,0:T(4,128)(2,1)S(1)}, bf16[8,3,512]{2,1,0:T(4,128)(2,1)S(1)}) custom-call(s32[1]{0:T(128)} %bitcast.band_ref, bf16[24,48,512]{2,1,0:T(8,128)(2,1)S(1)} %copy-done.18, bf16[24,48,512]{2,1,0:T(8,128)(2,1)S(1)} %copy-done.18, ...), custom_call_target="tpu_custom_call" | custom-call | flops 4800000000 | bytes 1000000 | tf_op jit(solution)/shard_map/between/pallas_call | solution.py:72
  53.7 4.2 %collective-permute-start.9 = (bf16[30,3,512]{2,1,0:T(4,128)(2,1)S(1)}, bf16[30,3,512]{2,1,0:T(4,128)(2,1)S(1)}, u32[]{:S(2)}, u32[]{:S(2)}) collective-permute-start(bf16[30,3,512]{2,1,0:T(4,128)(2,1)S(1)} %get-tuple-element.139), channel_id=1, source_target_pairs={{8,0},{16,8},{24,16},{32,24},{40,32},{48,40},{56,48},{64,56},{72,6... | collective-permute-start | bytes 276488 | tf_op jit(solution)/shard_map/ppermute | solution.py:383
  60.4 5.5 %collective-permute-done.8.refs_8_ = bf16[30,3,512]{2,1,0:T(4,128)(2,1)S(1)} collective-permute-done((bf16[30,3,512]{2,1,0:T(4,128)(2,1)S(1)}, bf16[30,3,512]{2,1,0:T(4,128)(2,1)S(1)}, u32[]{:S(2)}, u32[]{:S(2)}) %collective-permute-start.8) | collective-permute-done | bytes 92192 | tf_op jit(solution)/shard_map/ppermute | solution.py:383
  65.9 15.8 %feed.2 = (f32[24,48,512]{2,1,0:T(8,128)S(1)}, bf16[6,48,512]{2,1,0:T(8,128)(2,1)S(1)}, bf16[6,48,512]{2,1,0:T(8,128)(2,1)S(1)}, bf16[24,6,512]{2,1,0:T(8,128)(2,1)S(1)}, bf16[24,6,512]{2,1,0:T(8,128)(2,1)S(1)}) custom-call(s32[1]{0:T(128)} %bitcast.band_ref, f32[8,48,512]{2,1,0:T(8,128)S(1)} %get-tuple-element.67.refs_0_, ...), custom_call_target="tpu_custom_call" | custom-call | flops 14400000000 | bytes 1000000 | tf_op jit(solution)/shard_map/feed/pallas_call | solution.py:72
  81.8 5.3 %collective-permute-start.11 = (bf16[24,6,512]{2,1,0:T(8,128)(2,1)S(1)}, bf16[24,6,512]{2,1,0:T(8,128)(2,1)S(1)}, u32[]{:S(2)}, u32[]{:S(2)}) collective-permute-start(bf16[24,6,512]{2,1,0:T(8,128)(2,1)S(1)} %get-tuple-element.98), channel_id=1, source_target_pairs={{8,0},{16,8},{24,16},{32,24},{40,32},{48,40},{56,48},{64,56},{72,6... | collective-permute-start | bytes 442376 | tf_op jit(solution)/shard_map/ppermute | solution.py:383
  87.1 3.0 %project.3 = (bf16[24,48,512]{2,1,0:T(8,128)(2,1)S(1)}, bf16[24,32,1024]{2,1,0:T(8,128)(2,1)S(1)}) custom-call(f32[24,48,512]{2,1,0:T(8,128)S(1)} %get-tuple-element.93.x_ref.refs_2_.refs_3_.refs_9_, bf16[2,512,1536]{2,1,0:T(8,128)(2,1)S(1)} %copy-done.7, f32[2,512]{1,0:T(2,128)S(1)} %copy-done.11), custom_call_target="tpu_custom_call" | custom-call | flops 2400000000 | bytes 1000000 | tf_op jit(solution)/shard_map/project/pallas_call | solution.py:72
  90.2 4.1 %collective-permute-start.13 = (bf16[6,48,512]{2,1,0:T(8,128)(2,1)S(1)}, bf16[6,48,512]{2,1,0:T(8,128)(2,1)S(1)}, u32[]{:S(2)}, u32[]{:S(2)}) collective-permute-start(bf16[6,48,512]{2,1,0:T(8,128)(2,1)S(1)} %get-tuple-element.102), channel_id=1, source_target_pairs={{1,0},{2,1},{3,2},{4,3},{5,4},{6,5},{7,6},{0,7},{9,8},{10,9},{11,1... | collective-permute-start | bytes 884744 | tf_op jit(solution)/shard_map/ppermute | solution.py:380
  94.3 5.7 %collective-permute-done.10.refs_10_ = bf16[24,6,512]{2,1,0:T(8,128)(2,1)S(1)} collective-permute-done((bf16[24,6,512]{2,1,0:T(8,128)(2,1)S(1)}, bf16[24,6,512]{2,1,0:T(8,128)(2,1)S(1)}, u32[]{:S(2)}, u32[]{:S(2)}) %collective-permute-start.10) | collective-permute-done | bytes 147488 | tf_op jit(solution)/shard_map/ppermute | solution.py:383
  100.2 4.4 %collective-permute-start.15 = (bf16[6,12,512]{2,1,0:T(8,128)(2,1)S(1)}, bf16[6,12,512]{2,1,0:T(8,128)(2,1)S(1)}, u32[]{:S(2)}, u32[]{:S(2)}) collective-permute-start(bf16[6,12,512]{2,1,0:T(8,128)(2,1)S(1)} %pad_maximum_fusion.3), channel_id=1, source_target_pairs={{1,0},{2,1},{3,2},{4,3},{5,4},{6,5},{7,6},{0,7},{9,8},{10,9},{11,1... | collective-permute-start | bytes 221192 | tf_op jit(solution)/shard_map/ppermute | solution.py:380
  104.6 5.7 %inner.3 = (f32[8,48,512]{2,1,0:T(8,128)S(1)}, bf16[8,48,512]{2,1,0:T(8,128)(2,1)S(1)}, bf16[8,3,512]{2,1,0:T(4,128)(2,1)S(1)}, bf16[8,3,512]{2,1,0:T(4,128)(2,1)S(1)}, bf16[24,64,1024]{2,1,0:T(8,128)(2,1)S(1)}) custom-call(s32[1]{0:T(128)} %bitcast.band_ref, bf16[24,48,512]{2,1,0:T(8,128)(2,1)S(1)} %get-tuple-element.95.refs_0_.refs_1_, ...), custom_call_target="tpu_custom_call" | custom-call | flops 4800000000 | bytes 1000000 | tf_op jit(solution)/shard_map/inner/pallas_call | solution.py:72
  110.3 5.4 %outer.3 = (f32[8,48,512]{2,1,0:T(8,128)S(1)}, bf16[8,48,512]{2,1,0:T(8,128)(2,1)S(1)}, bf16[8,3,512]{2,1,0:T(4,128)(2,1)S(1)}, bf16[8,3,512]{2,1,0:T(4,128)(2,1...) custom-call(s32[1]{0:T(128)} %bitcast.band_ref, ...), custom_call_target="tpu_custom_call" | custom-call | flops 4800000000 | bytes 1000000 | tf_op jit(solution)/shard_map/outer/pallas_call | solution.py:72
  115.8 4.1 %collective-permute-start.17 = (bf16[3,48,512]{2,1,0:T(8,128)(2,1)S(1)}, bf16[3,48,512]{2,1,0:T(8,128)(2,1)S(1)}, u32[]{:S(2)}, u32[]{:S(2)}) collective-permute-start(bf16[3,48,512]{2,1,0:T(8,128)(2,1)S(1)} %get-tuple-element.110), channel_id=1, source_target_pairs={{1,0},{2,1},{3,2},{4,3},{5,4},{6,5},{7,6},{0,7},{9,8},{10,9},{11,1... | collective-permute-start | bytes 442376 | tf_op jit(solution)/shard_map/ppermute | solution.py:380
  119.9 4.4 %between.3 = (f32[8,48,512]{2,1,0:T(8,128)S(1)}, bf16[8,48,512]{2,1,0:T(8,128)(2,1)S(1)}, bf16[8,3,512]{2,1,0:T(4,128)(2,1)S(1)}, bf16[8,3,512]{2,1,0:T(4,128)(2,1)S(1)}) custom-call(s32[1]{0:T(128)} %bitcast.band_ref, bf16[24,48,512]{2,1,0:T(8,128)(2,1)S(1)} %get-tuple-element.95.refs_0_.refs_1_, ...), custom_call_target="tpu_custom_call" | custom-call | flops 4800000000 | bytes 1000000 | tf_op jit(solution)/shard_map/between/pallas_call | solution.py:72
  124.6 3.9 %collective-permute-start.19 = (bf16[30,3,512]{2,1,0:T(4,128)(2,1)S(1)}, bf16[30,3,512]{2,1,0:T(4,128)(2,1)S(1)}, u32[]{:S(2)}, u32[]{:S(2)}) collective-permute-start(bf16[30,3,512]{2,1,0:T(4,128)(2,1)S(1)} %get-tuple-element.135), channel_id=1, source_target_pairs={{8,0},{16,8},{24,16},{32,24},{40,32},{48,40},{56,48},{64,56},{72,6... | collective-permute-start | bytes 276488 | tf_op jit(solution)/shard_map/ppermute | solution.py:383
  128.5 2.4 %collective-permute-done.19.refs_9_ = bf16[30,3,512]{2,1,0:T(4,128)(2,1)S(1)} collective-permute-done((bf16[30,3,512]{2,1,0:T(4,128)(2,1)S(1)}, bf16[30,3,512]{2,1,0:T(4,128)(2,1)S(1)}, u32[]{:S(2)}, u32[]{:S(2)}) %collective-permute-start.19) | collective-permute-done | bytes 92192 | tf_op jit(solution)/shard_map/ppermute | solution.py:383
  131.0 5.5 %collective-permute-done.18.refs_8_ = bf16[30,3,512]{2,1,0:T(4,128)(2,1)S(1)} collective-permute-done((bf16[30,3,512]{2,1,0:T(4,128)(2,1)S(1)}, bf16[30,3,512]{2,1,0:T(4,128)(2,1)S(1)}, u32[]{:S(2)}, u32[]{:S(2)}) %collective-permute-start.18) | collective-permute-done | bytes 92192 | tf_op jit(solution)/shard_map/ppermute | solution.py:383
  136.4 16.3 %feed.3 = bf16[24,48,512]{2,1,0:T(8,128)(2,1)} custom-call(s32[1]{0:T(128)} %bitcast.band_ref, f32[8,48,512]{2,1,0:T(8,128)S(1)} %get-tuple-element.99.refs_0_, f32[8,48,512]{2,1,0:T(8,128)S(1)} %get-tuple-element.103.refs_1_, f32[8,48,512]{2,1,0:T(8,128)S(1)} %get-tuple-element.105.refs_2_, bf16[8,48,512]{2,1,0:T(8,128)(2,1)S(1)} %get-tuple-element.106.refs_3_, ...), custom_call_target="tpu_custom_call" | custom-call | flops 14400000000 | bytes 1000000 | tf_op jit(solution)/shard_map/feed/pallas_call | solution.py:72
  (100 shorter events, 18.5 us)
Async XLA Ops:
  0.0 57.9 %copy-start = (bf16[2,7,7,2048]{3,0,2,1:T(2,128)(2,1)S(1)}, bf16[2,7,7,2048]{3,0,2,1:T(2,128)(2,1)}, u32[]{:S(2)}) copy-start(bf16[2,7,7,2048]{3,0,2,1:T(2,128)(2,1)} %param.15) | copy-start | bytes 1204228
  1.8 21.3 %collective-permute-start.1 = (bf16[24,6,512]{2,1,0:T(8,128)(2,1)}, bf16[24,6,512]{2,1,0:T(8,128)(2,1)S(1)}, u32[]{:S(2)}, u32[]{:S(2)}) collective-permute-start(bf16[24,6,512]{2,1,0:T(8,128)(2,1)} %get-tuple-element.123), channel_id=1, source_target_pairs={{8,0},{16,8},{24,16},{32,24},{40,32},{48,40},{56,48},{64,56},{72,6... | collective-permute-start | bytes 442376 | tf_op jit(solution)/shard_map/ppermute | solution.py:383
  8.0 15.1 %collective-permute-start = (bf16[24,6,512]{2,1,0:T(8,128)(2,1)S(1)}, bf16[24,6,512]{2,1,0:T(8,128)(2,1)S(1)}, u32[]{:S(2)}, u32[]{:S(2)}) collective-permute-start(bf16[24,6,512]{2,1,0:T(8,128)(2,1)S(1)} %get-tuple-element.124), channel_id=1, source_target_pairs={{0,8},{8,16},{16,24},{24,32},{32,40},{40,48},{48,56},{56,64},{64,7... | collective-permute-start | bytes 442376 | tf_op jit(solution)/shard_map/ppermute | solution.py:383
  13.8 13.7 %copy-start.11 = (f32[2,512]{1,0:T(2,128)S(1)}, f32[2,512]{1,0:T(2,128)}, u32[]{:S(2)}) copy-start(f32[2,512]{1,0:T(2,128)} %refs_15_.3) | copy-start | bytes 12292
  19.0 18.9 %collective-permute-start.2 = (bf16[6,48,512]{2,1,0:T(8,128)(2,1)}, bf16[6,48,512]{2,1,0:T(8,128)(2,1)S(1)}, u32[]{:S(2)}, u32[]{:S(2)}) collective-permute-start(bf16[6,48,512]{2,1,0:T(8,128)(2,1)} %get-tuple-element.69), channel_id=1, source_target_pairs={{0,1},{1,2},{2,3},{3,4},{4,5},{5,6},{6,7},{7,0},{8,9},{9,10},{10,1... | collective-permute-start | bytes 884744 | tf_op jit(solution)/shard_map/ppermute | solution.py:380
  19.6 18.3 %collective-permute-start.3 = (bf16[6,48,512]{2,1,0:T(8,128)(2,1)}, bf16[6,48,512]{2,1,0:T(8,128)(2,1)}, u32[]{:S(2)}, u32[]{:S(2)}) collective-permute-start(bf16[6,48,512]{2,1,0:T(8,128)(2,1)} %get-tuple-element.70), channel_id=1, source_target_pairs={{1,0},{2,1},{3,2},{4,3},{5,4},{6,5},{7,6},{0,7},{9,8},{10,9},{11,1... | collective-permute-start | bytes 884744 | tf_op jit(solution)/shard_map/ppermute | solution.py:380
  23.2 14.7 %collective-permute-start.4 = (bf16[6,12,512]{2,1,0:T(8,128)(2,1)S(1)}, bf16[6,12,512]{2,1,0:T(8,128)(2,1)S(1)}, u32[]{:S(2)}, u32[]{:S(2)}) collective-permute-start(bf16[6,12,512]{2,1,0:T(8,128)(2,1)S(1)} %pad_maximum_fusion), channel_id=1, source_target_pairs={{0,1},{1,2},{2,3},{3,4},{4,5},{5,6},{6,7},{7,0},{8,9},{9,10},{10,1... | collective-permute-start | bytes 221192 | tf_op jit(solution)/shard_map/ppermute | solution.py:380
  23.3 14.6 %collective-permute-start.5 = (bf16[6,12,512]{2,1,0:T(8,128)(2,1)S(1)}, bf16[6,12,512]{2,1,0:T(8,128)(2,1)S(1)}, u32[]{:S(2)}, u32[]{:S(2)}) collective-permute-start(bf16[6,12,512]{2,1,0:T(8,128)(2,1)S(1)} %pad_maximum_fusion.1), channel_id=1, source_target_pairs={{1,0},{2,1},{3,2},{4,3},{5,4},{6,5},{7,6},{0,7},{9,8},{10,9},{11,1... | collective-permute-start | bytes 221192 | tf_op jit(solution)/shard_map/ppermute | solution.py:380
  44.9 8.6 %collective-permute-start.6 = (bf16[3,48,512]{2,1,0:T(8,128)(2,1)S(1)}, bf16[3,48,512]{2,1,0:T(8,128)(2,1)S(1)}, u32[]{:S(2)}, u32[]{:S(2)}) collective-permute-start(bf16[3,48,512]{2,1,0:T(8,128)(2,1)S(1)} %get-tuple-element.77), channel_id=1, source_target_pairs={{0,1},{1,2},{2,3},{3,4},{4,5},{5,6},{6,7},{7,0},{8,9},{9,10},{10,1... | collective-permute-start | bytes 442376 | tf_op jit(solution)/shard_map/ppermute | solution.py:380
  44.9 8.5 %collective-permute-start.7 = (bf16[3,48,512]{2,1,0:T(8,128)(2,1)S(1)}, bf16[3,48,512]{2,1,0:T(8,128)(2,1)S(1)}, u32[]{:S(2)}, u32[]{:S(2)}) collective-permute-start(bf16[3,48,512]{2,1,0:T(8,128)(2,1)S(1)} %get-tuple-element.78), channel_id=1, source_target_pairs={{1,0},{2,1},{3,2},{4,3},{5,4},{6,5},{7,6},{0,7},{9,8},{10,9},{11,1... | collective-permute-start | bytes 442376 | tf_op jit(solution)/shard_map/ppermute | solution.py:380
  49.1 16.8 %copy-start.4 = (bf16[2,2048,512]{2,1,0:T(8,128)(2,1)S(1)}, bf16[2,2048,512]{2,1,0:T(8,128)(2,1)}, u32[]{:S(2)}) copy-start(bf16[2,2048,512]{2,1,0:T(8,128)(2,1)} %refs_14_.3) | copy-start | bytes 12582916
  53.7 6.7 %collective-permute-start.9 = (bf16[30,3,512]{2,1,0:T(4,128)(2,1)S(1)}, bf16[30,3,512]{2,1,0:T(4,128)(2,1)S(1)}, u32[]{:S(2)}, u32[]{:S(2)}) collective-permute-start(bf16[30,3,512]{2,1,0:T(4,128)(2,1)S(1)} %get-tuple-element.139), channel_id=1, source_target_pairs={{8,0},{16,8},{24,16},{32,24},{40,32},{48,40},{56,48},{64,56},{72,6... | collective-permute-start | bytes 276488 | tf_op jit(solution)/shard_map/ppermute | solution.py:383
  57.9 7.9 %collective-permute-start.8 = (bf16[30,3,512]{2,1,0:T(4,128)(2,1)S(1)}, bf16[30,3,512]{2,1,0:T(4,128)(2,1)S(1)}, u32[]{:S(2)}, u32[]{:S(2)}) collective-permute-start(bf16[30,3,512]{2,1,0:T(4,128)(2,1)S(1)} %get-tuple-element.140), channel_id=1, source_target_pairs={{0,8},{8,16},{16,24},{24,32},{32,40},{40,48},{48,56},{56,64},{64,7... | collective-permute-start | bytes 276488 | tf_op jit(solution)/shard_map/ppermute | solution.py:383
  65.8 21.3 %copy-start.7 = (bf16[2,512,1536]{2,1,0:T(8,128)(2,1)S(1)}, bf16[2,512,1536]{2,1,0:T(8,128)(2,1)}, u32[]{:S(2)}) copy-start(bf16[2,512,1536]{2,1,0:T(8,128)(2,1)} %refs_7_.7) | copy-start | bytes 9437188
  81.7 18.3 %collective-permute-start.10 = (bf16[24,6,512]{2,1,0:T(8,128)(2,1)S(1)}, bf16[24,6,512]{2,1,0:T(8,128)(2,1)S(1)}, u32[]{:S(2)}, u32[]{:S(2)}) collective-permute-start(bf16[24,6,512]{2,1,0:T(8,128)(2,1)S(1)} %get-tuple-element.97), channel_id=1, source_target_pairs={{0,8},{8,16},{16,24},{24,32},{32,40},{40,48},{48,56},{56,64},{64,7... | collective-permute-start | bytes 442376 | tf_op jit(solution)/shard_map/ppermute | solution.py:383
  81.8 18.2 %collective-permute-start.11 = (bf16[24,6,512]{2,1,0:T(8,128)(2,1)S(1)}, bf16[24,6,512]{2,1,0:T(8,128)(2,1)S(1)}, u32[]{:S(2)}, u32[]{:S(2)}) collective-permute-start(bf16[24,6,512]{2,1,0:T(8,128)(2,1)S(1)} %get-tuple-element.98), channel_id=1, source_target_pairs={{8,0},{16,8},{24,16},{32,24},{40,32},{48,40},{56,48},{64,56},{72,6... | collective-permute-start | bytes 442376 | tf_op jit(solution)/shard_map/ppermute | solution.py:383
  90.1 20.2 %collective-permute-start.12 = (bf16[6,48,512]{2,1,0:T(8,128)(2,1)S(1)}, bf16[6,48,512]{2,1,0:T(8,128)(2,1)S(1)}, u32[]{:S(2)}, u32[]{:S(2)}) collective-permute-start(bf16[6,48,512]{2,1,0:T(8,128)(2,1)S(1)} %get-tuple-element.101), channel_id=1, source_target_pairs={{0,1},{1,2},{2,3},{3,4},{4,5},{5,6},{6,7},{7,0},{8,9},{9,10},{10,1... | collective-permute-start | bytes 884744 | tf_op jit(solution)/shard_map/ppermute | solution.py:380
  90.2 20.1 %collective-permute-start.13 = (bf16[6,48,512]{2,1,0:T(8,128)(2,1)S(1)}, bf16[6,48,512]{2,1,0:T(8,128)(2,1)S(1)}, u32[]{:S(2)}, u32[]{:S(2)}) collective-permute-start(bf16[6,48,512]{2,1,0:T(8,128)(2,1)S(1)} %get-tuple-element.102), channel_id=1, source_target_pairs={{1,0},{2,1},{3,2},{4,3},{5,4},{6,5},{7,6},{0,7},{9,8},{10,9},{11,1... | collective-permute-start | bytes 884744 | tf_op jit(solution)/shard_map/ppermute | solution.py:380
  100.1 10.2 %collective-permute-start.14 = (bf16[6,12,512]{2,1,0:T(8,128)(2,1)S(1)}, bf16[6,12,512]{2,1,0:T(8,128)(2,1)S(1)}, u32[]{:S(2)}, u32[]{:S(2)}) collective-permute-start(bf16[6,12,512]{2,1,0:T(8,128)(2,1)S(1)} %pad_maximum_fusion.2), channel_id=1, source_target_pairs={{0,1},{1,2},{2,3},{3,4},{4,5},{5,6},{6,7},{7,0},{8,9},{9,10},{10,1... | collective-permute-start | bytes 221192 | tf_op jit(solution)/shard_map/ppermute | solution.py:380
  100.2 10.1 %collective-permute-start.15 = (bf16[6,12,512]{2,1,0:T(8,128)(2,1)S(1)}, bf16[6,12,512]{2,1,0:T(8,128)(2,1)S(1)}, u32[]{:S(2)}, u32[]{:S(2)}) collective-permute-start(bf16[6,12,512]{2,1,0:T(8,128)(2,1)S(1)} %pad_maximum_fusion.3), channel_id=1, source_target_pairs={{1,0},{2,1},{3,2},{4,3},{5,4},{6,5},{7,6},{0,7},{9,8},{10,9},{11,1... | collective-permute-start | bytes 221192 | tf_op jit(solution)/shard_map/ppermute | solution.py:380
  115.7 8.6 %collective-permute-start.16 = (bf16[3,48,512]{2,1,0:T(8,128)(2,1)S(1)}, bf16[3,48,512]{2,1,0:T(8,128)(2,1)S(1)}, u32[]{:S(2)}, u32[]{:S(2)}) collective-permute-start(bf16[3,48,512]{2,1,0:T(8,128)(2,1)S(1)} %get-tuple-element.109), channel_id=1, source_target_pairs={{0,1},{1,2},{2,3},{3,4},{4,5},{5,6},{6,7},{7,0},{8,9},{9,10},{10,1... | collective-permute-start | bytes 442376 | tf_op jit(solution)/shard_map/ppermute | solution.py:380
  115.8 8.5 %collective-permute-start.17 = (bf16[3,48,512]{2,1,0:T(8,128)(2,1)S(1)}, bf16[3,48,512]{2,1,0:T(8,128)(2,1)S(1)}, u32[]{:S(2)}, u32[]{:S(2)}) collective-permute-start(bf16[3,48,512]{2,1,0:T(8,128)(2,1)S(1)} %get-tuple-element.110), channel_id=1, source_target_pairs={{1,0},{2,1},{3,2},{4,3},{5,4},{6,5},{7,6},{0,7},{9,8},{10,9},{11,1... | collective-permute-start | bytes 442376 | tf_op jit(solution)/shard_map/ppermute | solution.py:380
  124.6 6.4 %collective-permute-start.19 = (bf16[30,3,512]{2,1,0:T(4,128)(2,1)S(1)}, bf16[30,3,512]{2,1,0:T(4,128)(2,1)S(1)}, u32[]{:S(2)}, u32[]{:S(2)}) collective-permute-start(bf16[30,3,512]{2,1,0:T(4,128)(2,1)S(1)} %get-tuple-element.135), channel_id=1, source_target_pairs={{8,0},{16,8},{24,16},{32,24},{40,32},{48,40},{56,48},{64,56},{72,6... | collective-permute-start | bytes 276488 | tf_op jit(solution)/shard_map/ppermute | solution.py:383
  128.5 7.9 %collective-permute-start.18 = (bf16[30,3,512]{2,1,0:T(4,128)(2,1)S(1)}, bf16[30,3,512]{2,1,0:T(4,128)(2,1)S(1)}, u32[]{:S(2)}, u32[]{:S(2)}) collective-permute-start(bf16[30,3,512]{2,1,0:T(4,128)(2,1)S(1)} %get-tuple-element.136), channel_id=1, source_target_pairs={{0,8},{8,16},{16,24},{24,32},{32,40},{40,48},{48,56},{56,64},{64,7... | collective-permute-start | bytes 276488 | tf_op jit(solution)/shard_map/ppermute | solution.py:383
  (16 other events, 95.5 us)
